TPU v7x, 512 devices: a whole 4x4x16 slice. The times are simulated.
512 devices in a mesh: dp: 16 (over z_hi, x, core), expert: 32 (over y, z_lo).
Axes of the slice: x: 4, y: 4, z: 16 (z_hi: 2, z_lo: 8; z = z_hi * 8 + z_lo), core: 2. Of those that a mesh axis runs over, the one named last changes fastest.
Arguments:
- tokens: bfloat16 [65536, 512], P(('dp', 'expert')), may hold values from -6 to 6
- slot_order: int32 [512, 128], P(('dp', 'expert')), may hold values from 0 to 127, each once within a row
- centroid: bfloat16 [32, 512], P('expert'), may hold values from -0.25 to 0.25
- weight_in: bfloat16 [32, 512, 4096], P('expert', None, 'dp'), may hold values from -0.25 to 0.25
- weight_out: bfloat16 [32, 4096, 512], P('expert', 'dp'), may hold values from -0.09375 to 0.09375
- out_grad: bfloat16 [65536, 512], P(('dp', 'expert')), may hold values from -1.5 to 1.5
Outputs:
- layer_out: bfloat16 [65536, 512], P(('dp', 'expert'))
- grad_tokens: bfloat16 [65536, 512], P(('dp', 'expert'))
- grad_centroid: float32 [32, 512], P('expert')
- grad_in: float32 [32, 512, 4096], P('expert', None, 'dp')
- grad_out: float32 [32, 4096, 512], P('expert', 'dp')
Inputs may be any that keep to these rules, and one draw needn't show every extreme that they name: `slot_order`: in each row (one device, rows in the order of the devices of dp+expert) every number below 128 appears once; entries 4 * e to 4 * e + 3 name the tokens of that device that go to expert e.
All inputs are finite; a program needn't handle non-finite values.
Results may differ from a plain program's by a relative error of at most 0.015.
Values may be sent and summed in bfloat16 or wider, within the bound.
No kernel may reach another device: no remote copies, remote signals or barrier semaphores. Data moves between devices by JAX's collectives and lax.ppermute only.
A program may use at most 64 MiB of HBM per device.

v0:
```python
import jax
import jax.numpy as jnp
from jax import lax
from jax.sharding import PartitionSpec as P


def smooth(values):
    return jax.nn.gelu(values, approximate=True)


def sort_rows(values, order_row, groups):
    picked = values[order_row]
    return picked.reshape(groups, picked.shape[0] // groups, picked.shape[1])


def unsort_rows(values, order_row):
    row_count = order_row.shape[0]
    inverse = (
        jnp.zeros((row_count,), jnp.int32).at[order_row].set(jnp.arange(row_count, dtype=jnp.int32))
    )
    return values.reshape(row_count, -1)[inverse]


def send_home(local_rows, order_row):
    groups = lax.axis_size("expert")
    shaped = local_rows.reshape(groups, local_rows.shape[0] // groups, local_rows.shape[1])
    returned = lax.all_to_all(shaped, "expert", split_axis=0, concat_axis=0, tiled=True)
    return unsort_rows(returned, order_row)


def over_replicas(own_rows, fold_fn, initial):
    return fold_fn(initial, lax.all_gather(own_rows, "dp", axis=0, tiled=True), jnp.int32(0))


def sum_replicas(all_rows, weight):
    return lax.psum_scatter(
        jnp.dot(all_rows, weight, preferred_element_type=jnp.float32).astype(jnp.bfloat16),
        "dp",
        scatter_dimension=0,
        tiled=True,
    ).astype(jnp.float32)


def on_device(tokens, slot_order, centroid, weight_in, weight_out, out_grad):
    groups = lax.axis_size("expert")
    replicas = lax.axis_size("dp")
    own_count = tokens.shape[0]
    features = tokens.shape[1]
    all_count = own_count * replicas
    order_row = slot_order[0]
    first_weight = weight_in[0]
    second_weight = weight_out[0]
    unit_count = first_weight.shape[1]
    arrived = (
        lax.all_to_all(
            sort_rows(tokens, order_row, groups), "expert", split_axis=0, concat_axis=0, tiled=True
        ),
        lax.all_to_all(
            sort_rows(out_grad, order_row, groups),
            "expert",
            split_axis=0,
            concat_axis=0,
            tiled=True,
        ),
    )
    routed = arrived[0].reshape(own_count, features)
    d_routed = arrived[1].reshape(own_count, features)
    gating = jax.nn.sigmoid(jnp.dot(routed, centroid[0], preferred_element_type=jnp.float32))
    empty_pre = jnp.zeros((all_count, unit_count), jnp.float32)

    def forward_fold(totals, shard_rows, offset):
        pre_act = jnp.dot(shard_rows, first_weight, preferred_element_type=jnp.float32)
        return (pre_act, shard_rows)

    pre_all, rows_all = over_replicas(
        routed, forward_fold, (empty_pre, jnp.zeros((all_count, features), jnp.bfloat16))
    )
    hidden_all = smooth(pre_all).astype(jnp.bfloat16)
    expert_out = sum_replicas(hidden_all, second_weight)
    layer_local = (routed.astype(jnp.float32) + gating[:, None] * expert_out).astype(jnp.bfloat16)
    layer_out = send_home(layer_local, order_row)
    d_expert = (gating[:, None] * d_routed.astype(jnp.float32)).astype(jnp.bfloat16)
    d_logit = jnp.sum(d_routed.astype(jnp.float32) * expert_out, axis=1) * gating * (1.0 - gating)
    centroid_term = jnp.dot(d_logit, routed.astype(jnp.float32), precision=lax.Precision.HIGHEST)
    grad_centroid = lax.psum(centroid_term, "dp")
    start_grads = (
        jnp.zeros((features, unit_count), jnp.float32),
        jnp.zeros((unit_count, features), jnp.float32),
        jnp.zeros((all_count, unit_count), jnp.bfloat16),
    )

    def backward_piece(d_piece, rows_piece, pre_piece, hidden_piece):
        back_grad = jnp.dot(d_piece, second_weight.T, preferred_element_type=jnp.float32)
        d_hidden = jax.vjp(smooth, pre_piece)[1](back_grad)[0].astype(jnp.bfloat16)
        first_grad = jnp.dot(rows_piece.T, d_hidden, preferred_element_type=jnp.float32)
        second_grad = jnp.dot(hidden_piece.T, d_piece, preferred_element_type=jnp.float32)
        return (first_grad, second_grad, d_hidden)

    def backward_fold(totals, shard_rows, offset):
        return backward_piece(shard_rows, rows_all, pre_all, hidden_all)

    first_grad, second_grad, d_hidden_all = over_replicas(d_expert, backward_fold, start_grads)
    inner_grad = sum_replicas(d_hidden_all, first_weight.T)
    grad_local = (
        d_routed.astype(jnp.float32)
        + d_logit[:, None] * centroid[0].astype(jnp.float32)
        + inner_grad
    ).astype(jnp.bfloat16)
    grad_tokens = send_home(grad_local, order_row)
    return (layer_out, grad_tokens, grad_centroid[None, :], first_grad[None], second_grad[None])


def solution(mesh):
    placed = (
        P(("dp", "expert"), None),
        P(("dp", "expert"), None),
        P("expert", None),
        P("expert", None, "dp"),
        P("expert", "dp", None),
        P(("dp", "expert"), None),
    )
    return jax.shard_map(
        on_device,
        mesh=mesh,
        in_specs=placed,
        out_specs=(
            P(("dp", "expert"), None),
            P(("dp", "expert"), None),
            P("expert", None),
            P("expert", None, "dp"),
            P("expert", "dp", None),
        ),
        check_vma=False,
    )
```

profile of v0, /device:TPU:6, one launch (start us, length us, event | category | flops | bytes accessed | tf_op | source)
XLA Modules:
  0.0 479.2 jit_solution(4368238487130455802)
XLA Ops:
  7.2 0.0 copy-start
  7.2 0.0 copy-start.8
  7.2 0.0 all-gather.3.cloned.1.call-start
  7.2 0.7 fusion.23
  8.0 1.8 gather_fusion
  9.8 29.7 %all_to_all.20 = bf16[32,4,512]{2,1,0:T(4,128)(2,1)S(1)} all-to-all(bf16[32,4,512]{2,1,0:T(4,128)(2,1)S(1)} %reshape.64), channel_id=1, replica_groups=mesh['dp'=16,'expert'=32] {'expert'}, dimensions={0} | all-to-all | bytes 262144 | tf_op jit(solution)/shard_map/all_to_all | solution.py:55
  39.5 0.7 reshape.65
  40.2 0.0 all-gather.3.cloned.1.call-update
  40.2 0.0 reduce-scatter.3.cloned.1.call-start
  40.3 86.7 %all-gather.3.cloned.1.call-done = bf16[2048,512]{1,0:T(8,128)(2,1)} async-done(((bf16[128,512]{1,0:T(8,128)(2,1)}), bf16[2048,512]{1,0:T(8,128)(2,1)}) %all-gather.3.cloned.1.call-update) | async-done | bytes 2097168 | tf_op jit(solution)/shard_map/all_gather | solution.py:32
  127.0 2.3 fusion.20
  129.3 2.2 convolution_convert_fusion.1
  131.5 0.0 reduce-scatter.3.cloned.1.call-update
  131.5 0.0 all-gather.5.cloned.1.call-start
  131.6 0.8 copy-done.2
  132.4 0.8 gather_fusion.2
  133.3 19.5 %all_to_all.21 = bf16[32,4,512]{2,1,0:T(4,128)(2,1)S(1)} all-to-all(bf16[32,4,512]{2,1,0:T(4,128)(2,1)S(1)} %reshape.68), channel_id=1, replica_groups=mesh['dp'=16,'expert'=32] {'expert'}, dimensions={0} | all-to-all | bytes 262144 | tf_op jit(solution)/shard_map/all_to_all | solution.py:58
  152.9 0.0 copy-start.7
  152.9 0.1 fusion.10
  153.0 91.8 %reduce-scatter.3.cloned.1.call-done = bf16[128,512]{1,0:T(8,128)(2,1)} async-done(((bf16[2048,512]{1,0:T(8,128)(2,1)}), bf16[128,512]{1,0:T(8,128)(2,1)}) %reduce-scatter.3.cloned.1.call-update) | async-done | bytes 131088 | tf_op jit(solution)/shard_map/reduce_scatter | solution.py:36
  244.8 2.2 fusion.13
  247.0 0.0 all-gather.5.cloned.1.call-update
  247.0 0.0 reduce-scatter.5.cloned.1.call-start
  247.1 84.5 %all-gather.5.cloned.1.call-done = bf16[2048,512]{1,0:T(8,128)(2,1)} async-done(((bf16[128,512]{1,0:T(8,128)(2,1)}), bf16[2048,512]{1,0:T(8,128)(2,1)}) %all-gather.5.cloned.1.call-update) | async-done | bytes 2097168 | tf_op jit(solution)/shard_map/all_gather | solution.py:32
  331.6 0.0 copy-done.3
  331.6 3.2 fusion.6
  334.9 3.0 convolution_convert_fusion
  337.9 0.0 reduce-scatter.5.cloned.1.call-update
  337.9 0.5 iota.4
  338.4 1.2 scatter_custom_fusion
  339.7 1.6 reshape.66
  341.3 5.2 %all-to-all-start.1 = ((bf16[32,4,512]{2,1,0:T(4,128)(2,1)}), bf16[32,4,512]{2,1,0:T(4,128)(2,1)}, u32[]{:S(2)}, u32[]{:S(2)}) async-start(bf16[32,4,512]{2,1,0:T(4,128)(2,1)} %reshape.66), calls=%async_computation.2 | async-start | bytes 262144 | tf_op jit(solution)/shard_map/all_to_all | solution.py:27
  346.5 0.7 subtract_multiply_fusion
  347.2 0.5 copy-done.10
  347.7 0.2 fusion.24
  347.9 65.0 %psum.7 = f32[1,512]{1,0:T(1,128)} all-reduce(f32[1,512]{1,0:T(1,128)S(1)} %fusion.24), channel_id=1, replica_groups=mesh['dp'=16,'expert'=32] {'dp'}, use_global_device_ids=true, to_apply=%region_4.0 | all-reduce | flops 512 | bytes 4096 | tf_op jit(solution)/shard_map/psum | solution.py:85
  412.9 0.0 all-to-all-done.1
  412.9 0.9 reshape.67
  413.8 1.5 gather_fusion.1
  415.3 36.1 %reduce-scatter.5.cloned.1.call-done = bf16[128,512]{1,0:T(8,128)(2,1)} async-done(((bf16[2048,512]{1,0:T(8,128)(2,1)}), bf16[128,512]{1,0:T(8,128)(2,1)}) %reduce-scatter.5.cloned.1.call-update) | async-done | bytes 131088 | tf_op jit(solution)/shard_map/reduce_scatter | solution.py:36
  451.5 1.1 add_convert_fusion
  452.6 0.7 reshape.69
  453.3 5.0 %all-to-all-start.3 = ((bf16[32,4,512]{2,1,0:T(4,128)(2,1)}), bf16[32,4,512]{2,1,0:T(4,128)(2,1)S(1)}, u32[]{:S(2)}, u32[]{:S(2)}) async-start(bf16[32,4,512]{2,1,0:T(4,128)(2,1)} %reshape.69), calls=%async_computation.5 | async-start | bytes 262144 | tf_op jit(solution)/shard_map/all_to_all | solution.py:27
  458.3 1.5 convolution_bitcast_fusion.1
  459.8 0.0 copy-done.4
  459.8 3.3 convolution_bitcast_fusion
  463.2 8.0 %all-to-all-done.3 = bf16[32,4,512]{2,1,0:T(4,128)(2,1)S(1)} async-done(((bf16[32,4,512]{2,1,0:T(4,128)(2,1)}), bf16[32,4,512]{2,1,0:T(4,128)(2,1)S(1)}, u32[]{:S(2)}, u32[]{:S(2)}) %all-to-all-start.3) | async-done | bytes 131104 | tf_op jit(solution)/shard_map/all_to_all | solution.py:27
  471.2 1.5 gather_fusion.3
  (24 shorter events, 0.2 us)
Async XLA Ops:
  7.2 122.1 %copy-start = (bf16[1,256,512]{2,1,0:T(8,128)(2,1)S(1)}, bf16[1,256,512]{2,1,0:T(8,128)(2,1)}, u32[]{:S(2)}) copy-start(bf16[1,256,512]{2,1,0:T(8,128)(2,1)} %param.10) | copy-start | bytes 786436
  7.2 119.8 %copy-start.8 = (bf16[1,512,256]{2,1,0:T(8,128)(2,1)S(1)}, bf16[1,512,256]{2,1,0:T(8,128)(2,1)}, u32[]{:S(2)}) copy-start(bf16[1,512,256]{2,1,0:T(8,128)(2,1)} %param.9) | copy-start | bytes 786436
  7.2 119.8 %all-gather.3.cloned.1.call-start = ((), (), s32[]{:S(2)}) async-start(), calls=%async_computation.6 | async-start | bytes 2228224 | tf_op jit(solution)/shard_map/all_gather | solution.py:32
  40.2 204.6 %reduce-scatter.3.cloned.1.call-start = ((), (), s32[]{:S(2)}) async-start(), calls=%async_computation.7 | async-start | bytes 2228224 | tf_op jit(solution)/shard_map/reduce_scatter | solution.py:36
  129.3 202.4 %copy-start.3 = (f32[2048,256]{1,0:T(8,128)}, f32[2048,256]{1,0:T(8,128)S(1)}, u32[]{:S(2)}) copy-start(f32[2048,256]{1,0:T(8,128)S(1)} %fusion.20) | copy-start | bytes 6291460
  131.5 0.9 copy-start.2
  131.5 21.3 %copy-start.5 = (bf16[128,512]{1,0:T(8,128)(2,1)S(1)}, bf16[128,512]{1,0:T(8,128)(2,1)}, u32[]{:S(2)}) copy-start(bf16[128,512]{1,0:T(8,128)(2,1)} %reshape.65) | copy-start | bytes 393220
  131.5 21.4 %copy-start.9 = (bf16[1,512]{1,0:T(2,128)(2,1)S(1)}, bf16[1,512]{1,0:T(2,128)(2,1)}, u32[]{:S(2)}) copy-start(bf16[1,512]{1,0:T(2,128)(2,1)} %param.8) | copy-start | bytes 3076
  131.5 200.1 %all-gather.5.cloned.1.call-start = ((), (), s32[]{:S(2)}) async-start(), calls=%async_computation.8 | async-start | bytes 2228224 | tf_op jit(solution)/shard_map/all_gather | solution.py:32
  152.9 94.2 %copy-start.7 = (f32[128,512]{1,0:T(8,128)}, f32[128,512]{1,0:T(8,128)S(1)}, u32[]{:S(2)}) copy-start(f32[128,512]{1,0:T(8,128)S(1)} %reshape.71) | copy-start | bytes 786436
  247.0 204.5 %reduce-scatter.5.cloned.1.call-start = ((), (), s32[]{:S(2)}) async-start(), calls=%async_computation.9 | async-start | bytes 2228224 | tf_op jit(solution)/shard_map/reduce_scatter | solution.py:36
  337.9 9.8 %copy-start.6 = (bf16[128,512]{1,0:T(8,128)(2,1)S(1)}, bf16[128,512]{1,0:T(8,128)(2,1)}, u32[]{:S(2)}) copy-start(bf16[128,512]{1,0:T(8,128)(2,1)} %reshape.65) | copy-start | bytes 393220
  337.9 120.3 %copy-start.1 = (bf16[2048,512]{1,0:T(8,128)(2,1)S(1)}, bf16[2048,512]{1,0:T(8,128)(2,1)}, u32[]{:S(2)}) copy-start(bf16[2048,512]{1,0:T(8,128)(2,1)} %all-gather.3.cloned.1.call-done) | copy-start | bytes 6291460
  341.3 71.6 %all-to-all-start.1 = ((bf16[32,4,512]{2,1,0:T(4,128)(2,1)}), bf16[32,4,512]{2,1,0:T(4,128)(2,1)}, u32[]{:S(2)}, u32[]{:S(2)}) async-start(bf16[32,4,512]{2,1,0:T(4,128)(2,1)} %reshape.66), calls=%async_computation.2 | async-start | bytes 262144 | tf_op jit(solution)/shard_map/all_to_all | solution.py:27
  347.2 0.5 copy-start.10
  453.3 17.9 %all-to-all-start.3 = ((bf16[32,4,512]{2,1,0:T(4,128)(2,1)}), bf16[32,4,512]{2,1,0:T(4,128)(2,1)S(1)}, u32[]{:S(2)}, u32[]{:S(2)}) async-start(bf16[32,4,512]{2,1,0:T(4,128)(2,1)} %reshape.69), calls=%async_computation.5 | async-start | bytes 262144 | tf_op jit(solution)/shard_map/all_to_all | solution.py:27
  458.2 1.6 copy-start.4
Sparse Core Ops, SparseCore 0:
  40.3 86.5 all-gather.2
  131.8 112.9 reduce-scatter.2
  248.7 82.9 all-gather.4
  338.0 113.4 reduce-scatter.4
where the time goes:
time: 480 us; the launch traced here: 479 us
  waiting for transfers between devices  307 us (64%)
  blocking collectives  114 us (24%)
  matrix products  15.9 us (3%)
  between operations  14 us (3%)
  local copies, waits for them, and re-layouts  12.9 us (3%)
  starting transfers between devices  10.3 us (2%)
    all_gather x2, waiting for transfers between devices, over_replicas(): lax.all_gather(own_rows, 'dp', axis=0, tiled=True)  171 us
    reduce_scatter x2, waiting for transfers between devices, sum_replicas(): lax.psum_scatter(jnp.dot(all_rows, weight, preferred_element_type=jnp.flo...  128 us
    psum x1, blocking collectives, on_device(): grad_centroid = lax.psum(centroid_term, 'dp')  65 us
    all_to_all x1, blocking collectives, on_device(): lax.all_to_all(sort_rows(tokens, order_row, groups), 'expert', split_axis...  29.7 us
    all_to_all x1, blocking collectives, on_device(): lax.all_to_all(sort_rows(out_grad, order_row, groups), 'expert', split_ax...  19.5 us
    all_to_all x2, starting transfers between devices, send_home(): lax.all_to_all(shaped, 'expert', split_axis=0, concat_axis=0, tiled=True)  10.1 us
  transfers between devices with their start and end apart: 6, of which 5 were waited for; matrix products, arithmetic and copies ran while one was open for 3% of the time, Pallas kernels for 0%

commit v1 on v0

v1 whole, which is shorter than its diff:
```python
import math

import jax
import jax.numpy as jnp
from jax import lax
from jax.experimental import pallas as pl
from jax.experimental.pallas import tpu as pltpu
from jax.sharding import Mesh
from jax.sharding import PartitionSpec as P

BF = jnp.bfloat16
F32 = jnp.float32
ZH, X, CORE, Y, ZL = 2, 4, 2, 4, 8
EXPERTS = Y * ZL
BLK = 4
D = 512
TOK = EXPERTS * BLK
ROWS = ZH * TOK
MIXED = 2 * ROWS
UNITS = 256
HALF = D // 2
PACKED = D + 2 * UNITS
NOTE = 16
VMEM_LIMIT = 16 * 1024 * 1024


def dot(a, b, ca=1, cb=0):
    return lax.dot_general(a, b, (((ca,), (cb,)), ((), ())), preferred_element_type=F32)


def iota(shape, axis):
    return lax.broadcasted_iota(jnp.int32, shape, axis)


def mixed_picks(rows, on_rows_first):
    shape = (rows, 2 * rows) if on_rows_first else (2 * rows, rows)
    plain = iota(shape, 0 if on_rows_first else 1)
    mixed = iota(shape, 1 if on_rows_first else 0)
    place = (plain // BLK) * (2 * BLK) + plain % BLK
    return (mixed == place).astype(BF), (mixed == place + BLK).astype(BF)


def pack_kernel(order_ref, tok_ref, grad_ref, out_ref):
    token_pick, grad_pick = mixed_picks(TOK, True)
    order = jnp.broadcast_to(order_ref[...].astype(F32), (8, TOK)).astype(BF)
    source = iota((TOK, 2 * TOK), 0).astype(F32)
    token_source = dot(order, token_pick)[0:1]
    grad_source = dot(order, grad_pick)[0:1]
    kind = (iota((TOK, 2 * TOK), 1) // BLK) % 2
    pick_token = ((source == token_source) & (kind == 0)).astype(BF)
    pick_grad = ((source == grad_source) & (kind == 1)).astype(BF)
    mixed = (dot(pick_token, tok_ref[...], 0, 0) + dot(pick_grad, grad_ref[...], 0, 0)).astype(BF)
    for half in range(ZH):
        out_ref[half * 2 * TOK : (half + 1) * 2 * TOK, :] = mixed


def expert_kernel(
    rows_ref, centroid_ref, s0, s1, s2, s3,
    mixed_ref, centroid_grad_ref, routed_ref, d_expert_ref, hidden_ref, d_hidden_ref,
):
    token_pick, grad_pick = mixed_picks(ROWS, True)
    received = rows_ref[...]
    routed = dot(token_pick, received)
    d_routed = dot(grad_pick, received)
    centroid = centroid_ref[...].astype(F32)
    gating = jax.nn.sigmoid(jnp.sum(routed * centroid, axis=1, keepdims=True))
    routed_half = routed.astype(BF)
    d_expert = (gating * d_routed).astype(BF)
    routed_ref[...] = routed_half
    d_expert_ref[...] = d_expert
    out_part = jnp.zeros((ROWS, D), F32)
    inner_part = jnp.zeros((ROWS, D), F32)
    scale = math.sqrt(2.0 / math.pi)
    d_expert_a, d_expert_b = d_expert[:, :HALF], d_expert[:, HALF:]
    for k, shard in enumerate((s0, s1, s2, s3)):
        w = shard[:D, :]
        v_a, v_b = shard[D : D + UNITS, :], shard[D + UNITS :, :]
        pre = dot(routed_half, w)
        square = pre * pre
        bend = jnp.tanh(scale * pre * (1.0 + 0.044715 * square))
        half_up = 0.5 * (1.0 + bend)
        hidden = (pre * half_up).astype(BF)
        slope = half_up + 0.5 * pre * (1.0 - bend * bend) * (
            scale * (1.0 + 3.0 * 0.044715 * square)
        )
        back = dot(d_expert_a, v_a, 1, 1) + dot(d_expert_b, v_b, 1, 1)
        d_hidden = (back * slope).astype(BF)
        out_part += jnp.concatenate([dot(hidden, v_a), dot(hidden, v_b)], axis=1)
        inner_part += dot(d_hidden, w, 1, 1)
        hidden_ref[:, k * UNITS : (k + 1) * UNITS] = hidden
        d_hidden_ref[:, k * UNITS : (k + 1) * UNITS] = d_hidden
    d_logit = jnp.sum(d_routed * out_part, axis=1, keepdims=True) * gating * (1.0 - gating)
    centroid_grad_ref[...] = jnp.sum(d_logit * routed, axis=0, keepdims=True)
    layer_part = (gating * out_part).astype(BF)
    grad_part = (inner_part + d_logit * centroid).astype(BF)
    token_place, grad_place = mixed_picks(ROWS, False)
    mixed_ref[...] = (dot(token_place, layer_part) + dot(grad_place, grad_part)).astype(BF)


def weight_grad_kernel(
    centroid_a, routed_a, d_expert_a, hidden_a, d_hidden_a,
    centroid_b, routed_b, d_expert_b, hidden_b, d_hidden_b,
    own_in, own_out, own_centroid, *sent,
):
    centroid_grad = centroid_a[...] + centroid_b[...]
    own_centroid[...] = centroid_grad
    high = centroid_grad.astype(BF).astype(F32)
    row = iota((NOTE, D), 0)
    note = jnp.where(row == 0, high, jnp.where(row == 1, centroid_grad - high, 0.0)).astype(BF)
    for k in range(X):
        units = slice(k * UNITS, (k + 1) * UNITS)
        first = dot(routed_a[...], d_hidden_a[:, units], 0, 0) + dot(
            routed_b[...], d_hidden_b[:, units], 0, 0
        )
        second = dot(hidden_a[:, units], d_expert_a[...], 0, 0) + dot(
            hidden_b[:, units], d_expert_b[...], 0, 0
        )
        if k == 0:
            own_in[...] = first
            own_out[...] = second
        else:
            packed = sent[k - 1]
            packed[:D, :] = first.astype(BF)
            packed[D : D + UNITS, :] = second[:, :HALF].astype(BF)
            packed[D + UNITS : PACKED, :] = second[:, HALF:].astype(BF)
            packed[PACKED : PACKED + NOTE, :] = note[:, :HALF]
            packed[PACKED + NOTE :, :] = note[:, HALF:]


def unpack_kernel(order_ref, home_ref, tok_ref, grad_ref, layer_ref, grad_out_ref):
    order = jnp.broadcast_to(order_ref[...].astype(F32), (8, TOK)).astype(BF)
    token = iota((TOK, 2 * TOK), 0).astype(F32)
    token_pick, grad_pick = mixed_picks(TOK, True)
    kind = (iota((TOK, 2 * TOK), 1) // BLK) % 2
    pick_token = ((token == dot(order, token_pick)[0:1]) & (kind == 0)).astype(BF)
    pick_grad = ((token == dot(order, grad_pick)[0:1]) & (kind == 1)).astype(BF)
    layer = tok_ref[...].astype(F32)
    grad = grad_ref[...].astype(F32)
    for half in range(ZH):
        rows = home_ref[half * 2 * TOK : (half + 1) * 2 * TOK, :]
        layer += dot(pick_token, rows)
        grad += dot(pick_grad, rows)
    layer_ref[...] = layer.astype(BF)
    grad_out_ref[...] = grad.astype(BF)


def call(kernel, shapes, *operands):
    return pl.pallas_call(
        kernel,
        out_shape=[jax.ShapeDtypeStruct(shape, dtype) for shape, dtype in shapes],
        compiler_params=pltpu.CompilerParams(vmem_limit_bytes=VMEM_LIMIT),
    )(*operands)


def shift(value, axis, size, by):
    return lax.ppermute(value, axis, [(i, (i + by) % size) for i in range(size)])


def on_device(tokens, slot_order, centroid, weight_in, weight_out, out_grad):
    second = weight_out[0]
    shard = jnp.concatenate([weight_in[0], second[:, :HALF], second[:, HALF:]], axis=0)
    shards = [shard] + [shift(shard, "x", X, -k) for k in range(1, X)]
    (packed,) = call(pack_kernel, [((MIXED, D), BF)], slot_order, tokens, out_grad)
    own_rows = lax.all_to_all(
        packed.reshape(ZH * EXPERTS, 2 * BLK, D), ("zh", "y", "zl"), 0, 0, tiled=True
    ).reshape(MIXED, D)
    other_rows = shift(own_rows, "core", CORE, 1)
    part_shapes = [
        ((MIXED, D), BF), ((1, D), F32), ((ROWS, D), BF), ((ROWS, D), BF),
        ((ROWS, X * UNITS), BF), ((ROWS, X * UNITS), BF),
    ]
    own = call(expert_kernel, part_shapes, own_rows, centroid, *shards)
    other = call(expert_kernel, part_shapes, other_rows, centroid, *shards)
    from_other = shift(other[0], "core", CORE, 1)
    grads = call(
        weight_grad_kernel,
        [((D, UNITS), F32), ((UNITS, D), F32), ((1, D), F32)]
        + [((PACKED + 2 * NOTE, UNITS), BF)] * (X - 1),
        *own[1:], *other[1:],
    )
    first_grad, second_grad, centroid_grad = grads[:3]
    for k in range(1, X):
        arrived = shift(grads[2 + k], "x", X, k).astype(F32)
        first_grad += arrived[:D]
        second_grad += jnp.concatenate([arrived[D : D + UNITS], arrived[D + UNITS : PACKED]], axis=1)
        note = jnp.concatenate([arrived[PACKED : PACKED + 2], arrived[PACKED + NOTE : PACKED + NOTE + 2]], axis=1)
        centroid_grad += note[0:1] + note[1:2]
    turns = [(1, 0), (0, 1), (1, 1)]
    grad_centroid = centroid_grad + sum(
        lax.ppermute(
            centroid_grad,
            ("zh", "core"),
            [(2 * a + b, 2 * (a ^ i) + (b ^ j)) for a in range(ZH) for b in range(CORE)],
        )
        for i, j in turns
    )
    returned = (own[0].astype(F32) + from_other.astype(F32)).astype(BF)
    home = lax.all_to_all(
        returned.reshape(ZH * EXPERTS, 2 * BLK, D), ("zh", "y", "zl"), 0, 0, tiled=True
    ).reshape(MIXED, D)
    layer_out, grad_tokens = call(
        unpack_kernel, [((TOK, D), BF), ((TOK, D), BF)], slot_order, home, tokens, out_grad
    )
    return (layer_out, grad_tokens, grad_centroid, first_grad[None], second_grad[None])


def solution(mesh):
    fine = Mesh(mesh.devices.reshape(ZH, X, CORE, Y, ZL), ("zh", "x", "core", "y", "zl"))
    dp, expert = ("zh", "x", "core"), ("y", "zl")
    both = dp + expert
    placed = (
        P(both, None),
        P(both, None),
        P(expert, None),
        P(expert, None, dp),
        P(expert, dp, None),
        P(both, None),
    )
    return jax.shard_map(
        on_device,
        mesh=fine,
        in_specs=placed,
        out_specs=(
            P(both, None),
            P(both, None),
            P(expert, None),
            P(expert, None, dp),
            P(expert, dp, None),
        ),
        check_vma=False,
    )
```

time: 480 us -> 129 us (0.27)
  waiting for transfers between devices: 307 us -> 36.1 us
  blocking collectives: 114 us -> 0 us
  starting transfers between devices: 10.3 us -> 66.6 us
  matrix products: 15.9 us -> 0 us
  between operations: 14 us -> 0.9 us
  Pallas kernels: 0 us -> 9.08 us
  local copies, waits for them, and re-layouts: 12.9 us -> 7.57 us
    all_gather x2 -> x0, waiting for transfers between devices: 171 us -> none  [over_replicas(): lax.all_gather(own_rows, 'dp', axis=0, tiled=True)]
    reduce_scatter x2 -> x0, waiting for transfers between devices: 128 us -> none  [sum_replicas(): lax.psum_scatter(jnp.dot(all_rows, weight, preferred_element_type=jnp.flo...]
    psum x1 -> x0, blocking collectives: 65 us -> none  [on_device(): grad_centroid = lax.psum(centroid_term, 'dp')]
    all_to_all x2 -> x0, blocking collectives: 49.2 us -> none  [the longest x1 29.7 us: on_device(): lax.all_to_all(sort_rows(tokens, order_row, groups), 'expert', split_axis...]
    ppermute x0 -> x11, starting transfers between devices: none -> 37.8 us  [the longest x8 21.2 us: shift(): lax.ppermute(value, axis, [(i, (i + by) % size) for i in range(size)])]
    all_to_all x2, starting transfers between devices: 10.1 us -> 28.8 us  [the longest x1 18.9 us: on_device(): lax.all_to_all(packed.reshape(ZH * EXPERTS, 2 * BLK, D), ('zh', 'y', 'zl'...]
    dot_general x8 -> x0, matrix products: 15.9 us -> none  [the longest x2 5.24 us: sum_replicas(): jnp.dot(all_rows, weight, preferred_element_type=jnp.float32)]
    all_to_all x2, waiting for transfers between devices: 8 us -> 23.5 us  [the longest x1 23.5 us: on_device(): lax.all_to_all(packed.reshape(ZH * EXPERTS, 2 * BLK, D), ('zh', 'y', 'zl'...]
  transfers between devices with their start and end apart: 6 -> 13, of which waited for: 5 -> 4; matrix products, arithmetic and copies ran while one was open for 3% -> 9% of each run, Pallas kernels for 0% -> 3%
where the time goes in v1:
time: 129 us; the launch traced here: 127 us
  starting transfers between devices  66.6 us (52%)
  waiting for transfers between devices  36.1 us (28%)
  Pallas kernels  9.08 us (7%)
  local copies, waits for them, and re-layouts  7.57 us (6%)
  other arithmetic  6.79 us (5%)
    all_to_all x1, waiting for transfers between devices, on_device(): lax.all_to_all(packed.reshape(ZH * EXPERTS, 2 * BLK, D), ('zh', 'y', 'zl'...  23.5 us
    ppermute x8, starting transfers between devices, shift(): lax.ppermute(value, axis, [(i, (i + by) % size) for i in range(size)])  21.2 us
    all_to_all x1, starting transfers between devices, on_device(): lax.all_to_all(packed.reshape(ZH * EXPERTS, 2 * BLK, D), ('zh', 'y', 'zl'...  18.9 us
    ppermute x3, starting transfers between devices, on_device(): lax.ppermute(centroid_grad, ('zh', 'core'), [(2 * a + b, 2 * (a ^ i) + (b...  16.6 us
    ppermute x8, waiting for transfers between devices, shift(): lax.ppermute(value, axis, [(i, (i + by) % size) for i in range(size)])  12.7 us
    all_to_all x1, starting transfers between devices, on_device(): lax.all_to_all(returned.reshape(ZH * EXPERTS, 2 * BLK, D), ('zh', 'y', 'z...  9.94 us
    pallas_call x5, Pallas kernels, call(): pl.pallas_call(kernel, out_shape=[jax.ShapeDtypeStruct(shape, dtype) for...  9.08 us
    convert_element_type x3, other arithmetic, on_device(): arrived = shift(grads[2 + k], 'x', X, k).astype(F32)  3.37 us
  transfers between devices with their start and end apart: 13, of which 4 were waited for; matrix products, arithmetic and copies ran while one was open for 9% of the time, Pallas kernels for 3%

profile of v1, /device:TPU:6, one launch (start us, length us, event | category | flops | bytes accessed | tf_op | source)
XLA Modules:
  0.0 127.1 jit_solution(10169252121050813901)
XLA Ops:
  0.6 0.0 copy-start
  0.6 0.9 copy-done
  1.5 0.9 copy-done.2
  2.4 0.7 copy-done.5
  3.1 1.2 shard_map.101
  4.4 18.9 %all-to-all-start = ((bf16[64,8,512]{2,1,0:T(8,128)(2,1)}), bf16[64,8,512]{2,1,0:T(8,128)(2,1)S(1)}, u32[]{:S(2)}, u32[]{:S(2)}) async-start(bf16[64,8,512]{2,1,0:T(8,128)(2,1)} %bitcast), calls=%async_computation | async-start | bytes 1048576 | tf_op jit(solution)/shard_map/all_to_all | solution.py:164
  23.3 2.4 %collective-permute-start.2 = (bf16[1024,256]{1,0:T(8,128)(2,1)S(1)}, bf16[1024,256]{1,0:T(8,128)(2,1)S(1)}, u32[]{:S(2)}, u32[]{:S(2)}) collective-permute-start(bf16[1024,256]{1,0:T(8,128)(2,1)S(1)} %pad_maximum_fusion.s0), channel_id=1, source_target_pairs={{0,64},{64,128},{128,192},{192,0},{1,65},{65,129},{129,193},{193,1... | collective-permute-start | bytes 1572872 | tf_op jit(solution)/shard_map/ppermute | solution.py:156
  25.7 4.3 %collective-permute-start.1 = (bf16[1024,256]{1,0:T(8,128)(2,1)S(1)}, bf16[1024,256]{1,0:T(8,128)(2,1)S(1)}, u32[]{:S(2)}, u32[]{:S(2)}) collective-permute-start(bf16[1024,256]{1,0:T(8,128)(2,1)S(1)} %pad_maximum_fusion.s0), channel_id=1, source_target_pairs={{0,128},{64,192},{128,0},{192,64},{1,129},{65,193},{129,1},{193,65... | collective-permute-start | bytes 1572872 | tf_op jit(solution)/shard_map/ppermute | solution.py:156
  30.0 1.9 %collective-permute-start = (bf16[1024,256]{1,0:T(8,128)(2,1)S(1)}, bf16[1024,256]{1,0:T(8,128)(2,1)S(1)}, u32[]{:S(2)}, u32[]{:S(2)}) collective-permute-start(bf16[1024,256]{1,0:T(8,128)(2,1)S(1)} %pad_maximum_fusion.s0), channel_id=1, source_target_pairs={{0,192},{64,0},{128,64},{192,128},{1,193},{65,1},{129,65},{193,129... | collective-permute-start | bytes 1572872 | tf_op jit(solution)/shard_map/ppermute | solution.py:156
  32.0 23.5 %all-to-all-done = bf16[64,8,512]{2,1,0:T(8,128)(2,1)S(1)} async-done(((bf16[64,8,512]{2,1,0:T(8,128)(2,1)}), bf16[64,8,512]{2,1,0:T(8,128)(2,1)S(1)}, u32[]{:S(2)}, u32[]{:S(2)}) %all-to-all-start) | async-done | bytes 524320 | tf_op jit(solution)/shard_map/all_to_all | solution.py:164
  55.4 1.9 %collective-permute-start.3 = (bf16[512,512]{1,0:T(8,128)(2,1)S(1)}, bf16[512,512]{1,0:T(8,128)(2,1)S(1)}, u32[]{:S(2)}, u32[]{:S(2)}) collective-permute-start(bf16[512,512]{1,0:T(8,128)(2,1)S(1)} %bitcast.12), channel_id=1, source_target_pairs={{0,32},{32,0},{1,33},{33,1},{2,34},{34,2},{3,35},{35,3},{4,36},{36... | collective-permute-start | bytes 1572872 | tf_op jit(solution)/shard_map/ppermute | solution.py:156
  57.3 0.0 collective-permute-done.2.s3
  57.4 0.0 collective-permute-done.1.s2
  57.4 0.0 collective-permute-done.s1
  57.4 1.8 %collective-permute-done.3.rows_ref = bf16[512,512]{1,0:T(8,128)(2,1)S(1)} collective-permute-done((bf16[512,512]{1,0:T(8,128)(2,1)S(1)}, bf16[512,512]{1,0:T(8,128)(2,1)S(1)}, u32[]{:S(2)}, u32[]{:S(2)}) %collective-permute-start.3) | collective-permute-done | bytes 524320 | tf_op jit(solution)/shard_map/ppermute | solution.py:156
  59.2 2.7 %shard_map.103 = (bf16[512,512]{1,0:T(8,128)(2,1)S(1)}, f32[1,512]{1,0:T(1,128)S(1)}, bf16[256,512]{1,0:T(8,128)(2,1)S(1)}, bf16[256,512]{1,0:T(8,128)(2,1)S(1)}...) custom-call(bf16[512,512]{1,0:T(8,128)(2,1)S(1)} %collective-permute-done.3.rows_ref, ...), custom_call_target="tpu_custom_call" | custom-call | tf_op jit(solution)/shard_map/pallas_call | solution.py:148
  61.9 2.0 %collective-permute-start.4 = (bf16[512,512]{1,0:T(8,128)(2,1)S(1)}, bf16[512,512]{1,0:T(8,128)(2,1)S(1)}, u32[]{:S(2)}, u32[]{:S(2)}) collective-permute-start(bf16[512,512]{1,0:T(8,128)(2,1)S(1)} %get-tuple-element.26), channel_id=1, source_target_pairs={{0,32},{32,0},{1,33},{33,1},{2,34},{34,2},{3,35},{35,3},{4,36},{36... | collective-permute-start | bytes 1572872 | tf_op jit(solution)/shard_map/ppermute | solution.py:156
  64.0 2.7 %shard_map.102 = (bf16[512,512]{1,0:T(8,128)(2,1)S(1)}, f32[1,512]{1,0:T(1,128)S(1)}, bf16[256,512]{1,0:T(8,128)(2,1)S(1)}, bf16[256,512]{1,0:T(8,128)(2,1)S(1)}...) custom-call(bf16[512,512]{1,0:T(8,128)(2,1)S(1)} %bitcast.13, bf16[1,512]{1,0:T(2,128)(2,1)S(1)} %copy-done.4, ...), custom_call_target="tpu_custom_call" | custom-call | tf_op jit(solution)/shard_map/pallas_call | solution.py:148
  66.6 1.4 %shard_map.105 = (f32[512,256]{1,0:T(8,128)S(1)}, f32[256,512]{1,0:T(8,128)S(1)}, f32[1,512]{1,0:T(1,128)S(1)}, bf16[1056,256]{1,0:T(8,128)(2,1)S(1)}, bf16[1056...) custom-call(f32[1,512]{1,0:T(1,128)S(1)} %get-tuple-element.29.centroid_a, ...), custom_call_target="tpu_custom_call" | custom-call | tf_op jit(solution)/shard_map/pallas_call | solution.py:148
  68.0 2.4 %collective-permute-start.5 = (bf16[1056,256]{1,0:T(8,128)(2,1)S(1)}, bf16[1056,256]{1,0:T(8,128)(2,1)}, u32[]{:S(2)}, u32[]{:S(2)}) collective-permute-start(bf16[1056,256]{1,0:T(8,128)(2,1)S(1)} %get-tuple-element.40), channel_id=1, source_target_pairs={{0,64},{64,128},{128,192},{192,0},{1,65},{65,129},{129,193},{193,1... | collective-permute-start | bytes 1622024 | tf_op jit(solution)/shard_map/ppermute | solution.py:156
  70.4 4.3 %collective-permute-start.6 = (bf16[1056,256]{1,0:T(8,128)(2,1)S(1)}, bf16[1056,256]{1,0:T(8,128)(2,1)}, u32[]{:S(2)}, u32[]{:S(2)}) collective-permute-start(bf16[1056,256]{1,0:T(8,128)(2,1)S(1)} %get-tuple-element.41), channel_id=1, source_target_pairs={{0,128},{64,192},{128,0},{192,64},{1,129},{65,193},{129,1},{193,65... | collective-permute-start | bytes 1622024 | tf_op jit(solution)/shard_map/ppermute | solution.py:156
  74.8 1.9 %collective-permute-start.7 = (bf16[1056,256]{1,0:T(8,128)(2,1)S(1)}, bf16[1056,256]{1,0:T(8,128)(2,1)}, u32[]{:S(2)}, u32[]{:S(2)}) collective-permute-start(bf16[1056,256]{1,0:T(8,128)(2,1)S(1)} %get-tuple-element.42), channel_id=1, source_target_pairs={{0,192},{64,0},{128,64},{192,128},{1,193},{65,1},{129,65},{193,129... | collective-permute-start | bytes 1622024 | tf_op jit(solution)/shard_map/ppermute | solution.py:156
  76.7 0.0 collective-permute-done.4
  76.7 0.9 fusion
  77.6 9.9 %all-to-all-start.1 = ((bf16[64,8,512]{2,1,0:T(8,128)(2,1)}), bf16[64,8,512]{2,1,0:T(8,128)(2,1)S(1)}, u32[]{:S(2)}, u32[]{:S(2)}) async-start(bf16[64,8,512]{2,1,0:T(8,128)(2,1)} %fusion), calls=%async_computation.1 | async-start | bytes 1048576 | tf_op jit(solution)/shard_map/all_to_all | solution.py:198
  87.6 0.0 collective-permute-done.5
  87.6 0.7 fusion.16
  88.3 0.8 collective-permute-done.6
  89.1 0.7 fusion.15
  89.8 10.0 %collective-permute-done.7 = bf16[1056,256]{1,0:T(8,128)(2,1)} collective-permute-done((bf16[1056,256]{1,0:T(8,128)(2,1)S(1)}, bf16[1056,256]{1,0:T(8,128)(2,1)}, u32[]{:S(2)}, u32[]{:S(2)}) %collective-permute-start.7) | collective-permute-done | bytes 540704 | tf_op jit(solution)/shard_map/ppermute | solution.py:156
  99.8 0.7 fusion.14
  100.5 6.0 %collective-permute-start.10 = (f32[1,512]{1,0:T(1,128)S(1)}, f32[1,512]{1,0:T(1,128)S(1)}, u32[]{:S(2)}, u32[]{:S(2)}) collective-permute-start(f32[1,512]{1,0:T(1,128)S(1)} %add_add_fusion.1), channel_id=1, source_target_pairs={{0,288},{32,256},{256,32},{288,0},{1,289},{33,257},{257,33},{289,1... | collective-permute-start | bytes 6152 | tf_op jit(solution)/shard_map/ppermute | solution.py:190
  106.5 2.4 %collective-permute-start.9 = (f32[1,512]{1,0:T(1,128)S(1)}, f32[1,512]{1,0:T(1,128)S(1)}, u32[]{:S(2)}, u32[]{:S(2)}) collective-permute-start(f32[1,512]{1,0:T(1,128)S(1)} %add_add_fusion.1), channel_id=1, source_target_pairs={{0,32},{32,0},{256,288},{288,256},{1,33},{33,1},{257,289},{289,257... | collective-permute-start | bytes 6152 | tf_op jit(solution)/shard_map/ppermute | solution.py:190
  108.9 8.2 %collective-permute-start.8 = (f32[1,512]{1,0:T(1,128)S(1)}, f32[1,512]{1,0:T(1,128)S(1)}, u32[]{:S(2)}, u32[]{:S(2)}) collective-permute-start(f32[1,512]{1,0:T(1,128)S(1)} %add_add_fusion.1), channel_id=1, source_target_pairs={{0,256},{32,288},{256,0},{288,32},{1,257},{33,289},{257,1},{289,33... | collective-permute-start | bytes 6152 | tf_op jit(solution)/shard_map/ppermute | solution.py:190
  117.1 1.1 convert_element_type.21
  118.2 1.1 convert_element_type.22
  119.4 1.1 convert_element_type.23
  120.5 1.0 fusion.13
  121.5 1.0 fusion.12
  122.5 1.0 fusion.11
  123.5 0.9 fusion.1
  124.5 0.9 fusion.4
  125.4 0.0 collective-permute-done.10
  125.4 0.0 collective-permute-done.9
  125.4 0.0 collective-permute-done.8
  125.4 0.6 add_add_fusion
  126.0 0.0 all-to-all-done.1
  126.0 1.1 shard_map.104
  (17 shorter events, 0.1 us)
Async XLA Ops:
  0.6 0.9 copy-start
  1.5 0.9 copy-start.2
  2.4 0.7 copy-start.5
  3.1 20.1 %copy-start.7 = (bf16[1,256,512]{2,1,0:T(8,128)(2,1)S(1)}, bf16[1,256,512]{2,1,0:T(8,128)(2,1)}, u32[]{:S(2)}) copy-start(bf16[1,256,512]{2,1,0:T(8,128)(2,1)} %param.10) | copy-start | bytes 786436
  3.1 20.2 %copy-start.8 = (bf16[1,512,256]{2,1,0:T(8,128)(2,1)S(1)}, bf16[1,512,256]{2,1,0:T(8,128)(2,1)}, u32[]{:S(2)}) copy-start(bf16[1,512,256]{2,1,0:T(8,128)(2,1)} %param.9) | copy-start | bytes 786436
  4.4 54.9 %copy-start.4 = (bf16[1,512]{1,0:T(2,128)(2,1)S(1)}, bf16[1,512]{1,0:T(2,128)(2,1)}, u32[]{:S(2)}) copy-start(bf16[1,512]{1,0:T(2,128)(2,1)} %centroid_ref.3) | copy-start | bytes 3076
  4.4 51.1 %all-to-all-start = ((bf16[64,8,512]{2,1,0:T(8,128)(2,1)}), bf16[64,8,512]{2,1,0:T(8,128)(2,1)S(1)}, u32[]{:S(2)}, u32[]{:S(2)}) async-start(bf16[64,8,512]{2,1,0:T(8,128)(2,1)} %bitcast), calls=%async_computation | async-start | bytes 1048576 | tf_op jit(solution)/shard_map/all_to_all | solution.py:164
  23.3 34.0 %collective-permute-start.2 = (bf16[1024,256]{1,0:T(8,128)(2,1)S(1)}, bf16[1024,256]{1,0:T(8,128)(2,1)S(1)}, u32[]{:S(2)}, u32[]{:S(2)}) collective-permute-start(bf16[1024,256]{1,0:T(8,128)(2,1)S(1)} %pad_maximum_fusion.s0), channel_id=1, source_target_pairs={{0,64},{64,128},{128,192},{192,0},{1,65},{65,129},{129,193},{193,1... | collective-permute-start | bytes 1572872 | tf_op jit(solution)/shard_map/ppermute | solution.py:156
  25.7 31.6 %collective-permute-start.1 = (bf16[1024,256]{1,0:T(8,128)(2,1)S(1)}, bf16[1024,256]{1,0:T(8,128)(2,1)S(1)}, u32[]{:S(2)}, u32[]{:S(2)}) collective-permute-start(bf16[1024,256]{1,0:T(8,128)(2,1)S(1)} %pad_maximum_fusion.s0), channel_id=1, source_target_pairs={{0,128},{64,192},{128,0},{192,64},{1,129},{65,193},{129,1},{193,65... | collective-permute-start | bytes 1572872 | tf_op jit(solution)/shard_map/ppermute | solution.py:156
  30.0 27.3 %collective-permute-start = (bf16[1024,256]{1,0:T(8,128)(2,1)S(1)}, bf16[1024,256]{1,0:T(8,128)(2,1)S(1)}, u32[]{:S(2)}, u32[]{:S(2)}) collective-permute-start(bf16[1024,256]{1,0:T(8,128)(2,1)S(1)} %pad_maximum_fusion.s0), channel_id=1, source_target_pairs={{0,192},{64,0},{128,64},{192,128},{1,193},{65,1},{129,65},{193,129... | collective-permute-start | bytes 1572872 | tf_op jit(solution)/shard_map/ppermute | solution.py:156
  55.4 3.8 %collective-permute-start.3 = (bf16[512,512]{1,0:T(8,128)(2,1)S(1)}, bf16[512,512]{1,0:T(8,128)(2,1)S(1)}, u32[]{:S(2)}, u32[]{:S(2)}) collective-permute-start(bf16[512,512]{1,0:T(8,128)(2,1)S(1)} %bitcast.12), channel_id=1, source_target_pairs={{0,32},{32,0},{1,33},{33,1},{2,34},{34,2},{3,35},{35,3},{4,36},{36... | collective-permute-start | bytes 1572872 | tf_op jit(solution)/shard_map/ppermute | solution.py:156
  61.9 14.8 %collective-permute-start.4 = (bf16[512,512]{1,0:T(8,128)(2,1)S(1)}, bf16[512,512]{1,0:T(8,128)(2,1)S(1)}, u32[]{:S(2)}, u32[]{:S(2)}) collective-permute-start(bf16[512,512]{1,0:T(8,128)(2,1)S(1)} %get-tuple-element.26), channel_id=1, source_target_pairs={{0,32},{32,0},{1,33},{33,1},{2,34},{34,2},{3,35},{35,3},{4,36},{36... | collective-permute-start | bytes 1572872 | tf_op jit(solution)/shard_map/ppermute | solution.py:156
  68.0 19.6 %collective-permute-start.5 = (bf16[1056,256]{1,0:T(8,128)(2,1)S(1)}, bf16[1056,256]{1,0:T(8,128)(2,1)}, u32[]{:S(2)}, u32[]{:S(2)}) collective-permute-start(bf16[1056,256]{1,0:T(8,128)(2,1)S(1)} %get-tuple-element.40), channel_id=1, source_target_pairs={{0,64},{64,128},{128,192},{192,0},{1,65},{65,129},{129,193},{193,1... | collective-permute-start | bytes 1622024 | tf_op jit(solution)/shard_map/ppermute | solution.py:156
  70.4 18.7 %collective-permute-start.6 = (bf16[1056,256]{1,0:T(8,128)(2,1)S(1)}, bf16[1056,256]{1,0:T(8,128)(2,1)}, u32[]{:S(2)}, u32[]{:S(2)}) collective-permute-start(bf16[1056,256]{1,0:T(8,128)(2,1)S(1)} %get-tuple-element.41), channel_id=1, source_target_pairs={{0,128},{64,192},{128,0},{192,64},{1,129},{65,193},{129,1},{193,65... | collective-permute-start | bytes 1622024 | tf_op jit(solution)/shard_map/ppermute | solution.py:156
  74.8 25.0 %collective-permute-start.7 = (bf16[1056,256]{1,0:T(8,128)(2,1)S(1)}, bf16[1056,256]{1,0:T(8,128)(2,1)}, u32[]{:S(2)}, u32[]{:S(2)}) collective-permute-start(bf16[1056,256]{1,0:T(8,128)(2,1)S(1)} %get-tuple-element.42), channel_id=1, source_target_pairs={{0,192},{64,0},{128,64},{192,128},{1,193},{65,1},{129,65},{193,129... | collective-permute-start | bytes 1622024 | tf_op jit(solution)/shard_map/ppermute | solution.py:156
  77.6 48.4 %all-to-all-start.1 = ((bf16[64,8,512]{2,1,0:T(8,128)(2,1)}), bf16[64,8,512]{2,1,0:T(8,128)(2,1)S(1)}, u32[]{:S(2)}, u32[]{:S(2)}) async-start(bf16[64,8,512]{2,1,0:T(8,128)(2,1)} %fusion), calls=%async_computation.1 | async-start | bytes 1048576 | tf_op jit(solution)/shard_map/all_to_all | solution.py:198
  100.5 24.9 %collective-permute-start.10 = (f32[1,512]{1,0:T(1,128)S(1)}, f32[1,512]{1,0:T(1,128)S(1)}, u32[]{:S(2)}, u32[]{:S(2)}) collective-permute-start(f32[1,512]{1,0:T(1,128)S(1)} %add_add_fusion.1), channel_id=1, source_target_pairs={{0,288},{32,256},{256,32},{288,0},{1,289},{33,257},{257,33},{289,1... | collective-permute-start | bytes 6152 | tf_op jit(solution)/shard_map/ppermute | solution.py:190
  106.5 18.9 %collective-permute-start.9 = (f32[1,512]{1,0:T(1,128)S(1)}, f32[1,512]{1,0:T(1,128)S(1)}, u32[]{:S(2)}, u32[]{:S(2)}) collective-permute-start(f32[1,512]{1,0:T(1,128)S(1)} %add_add_fusion.1), channel_id=1, source_target_pairs={{0,32},{32,0},{256,288},{288,256},{1,33},{33,1},{257,289},{289,257... | collective-permute-start | bytes 6152 | tf_op jit(solution)/shard_map/ppermute | solution.py:190
  108.9 16.5 %collective-permute-start.8 = (f32[1,512]{1,0:T(1,128)S(1)}, f32[1,512]{1,0:T(1,128)S(1)}, u32[]{:S(2)}, u32[]{:S(2)}) collective-permute-start(f32[1,512]{1,0:T(1,128)S(1)} %add_add_fusion.1), channel_id=1, source_target_pairs={{0,256},{32,288},{256,0},{288,32},{1,257},{33,289},{257,1},{289,33... | collective-permute-start | bytes 6152 | tf_op jit(solution)/shard_map/ppermute | solution.py:190
  124.5 1.5 %copy-start.1 = (bf16[128,512]{1,0:T(8,128)(2,1)S(1)}, bf16[128,512]{1,0:T(8,128)(2,1)}, u32[]{:S(2)}) copy-start(bf16[128,512]{1,0:T(8,128)(2,1)} %tok_ref.3) | copy-start | bytes 393220
  124.5 1.5 %copy-start.3 = (bf16[128,512]{1,0:T(8,128)(2,1)S(1)}, bf16[128,512]{1,0:T(8,128)(2,1)}, u32[]{:S(2)}) copy-start(bf16[128,512]{1,0:T(8,128)(2,1)} %grad_ref.3) | copy-start | bytes 393220
  124.5 1.5 %copy-start.6 = (s32[1,128]{1,0:T(1,128)S(1)}, s32[1,128]{1,0:T(1,128)}, u32[]{:S(2)}) copy-start(s32[1,128]{1,0:T(1,128)} %order_ref.3) | copy-start | bytes 1540

commit v2 on v1

v2 whole, which is shorter than its diff:
```python
import math

import jax
import jax.numpy as jnp
from jax import lax
from jax.experimental import pallas as pl
from jax.experimental.pallas import tpu as pltpu
from jax.sharding import Mesh
from jax.sharding import PartitionSpec as P

BF = jnp.bfloat16
F32 = jnp.float32
ZH, X, CORE, Y, ZL = 2, 4, 2, 4, 8
EXPERTS = Y * ZL
BLK = 4
D = 512
TOK = EXPERTS * BLK
ROWS = ZH * TOK
MIXED = 2 * ROWS
UNITS = 256
HALF = D // 2
PACKED = D + 2 * UNITS
SHARDS = X * CORE
VMEM_LIMIT = 16 * 1024 * 1024


def dot(a, b, ca=1, cb=0):
    return lax.dot_general(a, b, (((ca,), (cb,)), ((), ())), preferred_element_type=F32)


def iota(shape, axis):
    return lax.broadcasted_iota(jnp.int32, shape, axis)


def mixed_picks(rows, on_rows_first):
    shape = (rows, 2 * rows) if on_rows_first else (2 * rows, rows)
    plain = iota(shape, 0 if on_rows_first else 1)
    mixed = iota(shape, 1 if on_rows_first else 0)
    place = (plain // BLK) * (2 * BLK) + plain % BLK
    return (mixed == place).astype(BF), (mixed == place + BLK).astype(BF)


def pack_kernel(
    order_ref, tok_ref, grad_ref, first_ref, second_ref,
    out_ref, shard_ref, order_vmem, tok_vmem, grad_vmem, sems,
):
    copies = [
        pltpu.make_async_copy(source, target, sems.at[i])
        for i, (source, target) in enumerate(
            (
                (order_ref, order_vmem),
                (tok_ref, tok_vmem),
                (grad_ref, grad_vmem),
                (first_ref.at[0], shard_ref.at[:D, :]),
                (second_ref.at[0, :, :HALF], shard_ref.at[D : D + UNITS, :]),
                (second_ref.at[0, :, HALF:], shard_ref.at[D + UNITS :, :]),
            )
        )
    ]
    for copy in copies:
        copy.start()
    token_pick, grad_pick = mixed_picks(TOK, True)
    copies[0].wait()
    order = jnp.broadcast_to(order_vmem[...].astype(F32), (8, TOK)).astype(BF)
    source = iota((TOK, 2 * TOK), 0).astype(F32)
    token_source = dot(order, token_pick)[0:1]
    grad_source = dot(order, grad_pick)[0:1]
    kind = (iota((TOK, 2 * TOK), 1) // BLK) % 2
    pick_token = ((source == token_source) & (kind == 0)).astype(BF)
    pick_grad = ((source == grad_source) & (kind == 1)).astype(BF)
    copies[1].wait()
    mixed = dot(pick_token, tok_vmem[...], 0, 0)
    copies[2].wait()
    mixed = (mixed + dot(pick_grad, grad_vmem[...], 0, 0)).astype(BF)
    for half in range(ZH):
        out_ref[half * 2 * TOK : (half + 1) * 2 * TOK, :] = mixed
    for copy in copies[3:]:
        copy.wait()


def expert_kernel(
    rows_ref, centroid_ref, shards_ref,
    mixed_ref, centroid_grad_ref, routed_ref, d_expert_ref, hidden_ref, d_hidden_ref,
    shards_vmem, sems,
):
    copies = [
        pltpu.make_async_copy(
            shards_ref.at[k * PACKED : (k + 1) * PACKED, :], shards_vmem.at[k], sems.at[k]
        )
        for k in range(SHARDS)
    ]
    for copy in copies:
        copy.start()
    token_pick, grad_pick = mixed_picks(ROWS, True)
    received = rows_ref[...]
    routed = dot(token_pick, received)
    d_routed = dot(grad_pick, received)
    centroid = centroid_ref[...].astype(F32)
    gating = jax.nn.sigmoid(jnp.sum(routed * centroid, axis=1, keepdims=True))
    routed_half = routed.astype(BF)
    d_expert = (gating * d_routed).astype(BF)
    routed_ref[...] = routed_half
    d_expert_ref[...] = d_expert
    d_expert_a, d_expert_b = d_expert[:, :HALF], d_expert[:, HALF:]
    out_part = jnp.zeros((ROWS, D), F32)
    inner_part = jnp.zeros((ROWS, D), F32)
    scale = math.sqrt(2.0 / math.pi)
    for k in range(SHARDS):
        copies[k].wait()
        w = shards_vmem[k, :D, :]
        v_a, v_b = shards_vmem[k, D : D + UNITS, :], shards_vmem[k, D + UNITS :, :]
        pre = dot(routed_half, w)
        square = pre * pre
        bend = jnp.tanh(scale * pre * (1.0 + 0.044715 * square))
        half_up = 0.5 * (1.0 + bend)
        hidden = (pre * half_up).astype(BF)
        slope = half_up + 0.5 * pre * (1.0 - bend * bend) * (
            scale * (1.0 + 3.0 * 0.044715 * square)
        )
        back = dot(d_expert_a, v_a, 1, 1) + dot(d_expert_b, v_b, 1, 1)
        d_hidden = (back * slope).astype(BF)
        out_part += jnp.concatenate([dot(hidden, v_a), dot(hidden, v_b)], axis=1)
        inner_part += dot(d_hidden, w, 1, 1)
        hidden_ref[:, k * UNITS : (k + 1) * UNITS] = hidden
        d_hidden_ref[:, k * UNITS : (k + 1) * UNITS] = d_hidden
    d_logit = jnp.sum(d_routed * out_part, axis=1, keepdims=True) * gating * (1.0 - gating)
    centroid_grad_ref[...] = jnp.sum(d_logit * routed, axis=0, keepdims=True)
    layer_part = (gating * out_part).astype(BF)
    grad_part = (inner_part + d_logit * centroid).astype(BF)
    token_place, grad_place = mixed_picks(ROWS, False)
    mixed_ref[...] = (dot(token_place, layer_part) + dot(grad_place, grad_part)).astype(BF)


def weight_grad_kernel(
    routed_ref, d_expert_ref, hidden_ref, d_hidden_ref, packed_ref, packed_vmem, sems
):
    copies = []
    for k in range(SHARDS):
        units = slice(k * UNITS, (k + 1) * UNITS)
        first = dot(routed_ref[...], d_hidden_ref[:, units], 0, 0)
        second = dot(hidden_ref[:, units], d_expert_ref[...], 0, 0)
        packed_vmem[k, :D, :] = first.astype(BF)
        packed_vmem[k, D : D + UNITS, :] = second[:, :HALF].astype(BF)
        packed_vmem[k, D + UNITS :, :] = second[:, HALF:].astype(BF)
        copies.append(
            pltpu.make_async_copy(
                packed_vmem.at[k], packed_ref.at[k * PACKED : (k + 1) * PACKED, :], sems.at[k]
            )
        )
        copies[k].start()
    for copy in copies:
        copy.wait()


def spread_kernel(packed_ref, first_ref, second_ref):
    first_ref[0] = packed_ref[:D, :].astype(F32)
    second_ref[0, :, :HALF] = packed_ref[D : D + UNITS, :].astype(F32)
    second_ref[0, :, HALF:] = packed_ref[D + UNITS :, :].astype(F32)


def unpack_kernel(order_ref, home_ref, tok_ref, grad_ref, layer_ref, grad_out_ref):
    order = jnp.broadcast_to(order_ref[...].astype(F32), (8, TOK)).astype(BF)
    token = iota((TOK, 2 * TOK), 0).astype(F32)
    token_pick, grad_pick = mixed_picks(TOK, True)
    kind = (iota((TOK, 2 * TOK), 1) // BLK) % 2
    pick_token = ((token == dot(order, token_pick)[0:1]) & (kind == 0)).astype(BF)
    pick_grad = ((token == dot(order, grad_pick)[0:1]) & (kind == 1)).astype(BF)
    layer = tok_ref[...].astype(F32)
    grad = grad_ref[...].astype(F32)
    for half in range(ZH):
        rows = home_ref[half * 2 * TOK : (half + 1) * 2 * TOK, :]
        layer += dot(pick_token, rows)
        grad += dot(pick_grad, rows)
    layer_ref[...] = layer.astype(BF)
    grad_out_ref[...] = grad.astype(BF)


def in_hbm(value):
    return pltpu.with_memory_space_constraint(value, pltpu.HBM)


def hbm_out(shape, dtype):
    return pltpu.HBM(shape, dtype)


def call(kernel, outs, *operands, **options):
    return pl.pallas_call(
        kernel,
        out_shape=[
            out if hasattr(out, "memory_space") else jax.ShapeDtypeStruct(*out) for out in outs
        ],
        compiler_params=pltpu.CompilerParams(vmem_limit_bytes=VMEM_LIMIT),
        **options,
    )(*operands)


def on_device(tokens, slot_order, centroid, weight_in, weight_out, out_grad):
    vmem, hbm = pl.BlockSpec(memory_space=pltpu.VMEM), pl.BlockSpec(memory_space=pltpu.HBM)
    packed, shard = call(
        pack_kernel,
        [((MIXED, D), BF), hbm_out((PACKED, UNITS), BF)],
        *(in_hbm(each) for each in (slot_order, tokens, out_grad, weight_in, weight_out)),
        in_specs=[hbm] * 5,
        out_specs=[vmem, hbm],
        scratch_shapes=[
            pltpu.VMEM((1, TOK), jnp.int32),
            pltpu.VMEM((TOK, D), BF),
            pltpu.VMEM((TOK, D), BF),
            pltpu.SemaphoreType.DMA((6,)),
        ],
    )
    shards = lax.all_gather(shard, ("x", "core"), axis=0, tiled=True)
    rows = lax.all_to_all(
        packed.reshape(ZH * EXPERTS, 2 * BLK, D), ("zh", "y", "zl"), 0, 0, tiled=True
    ).reshape(MIXED, D)
    mixed, centroid_term, *kept = call(
        expert_kernel,
        [
            ((MIXED, D), BF), ((1, D), F32), ((ROWS, D), BF), ((ROWS, D), BF),
            ((ROWS, SHARDS * UNITS), BF), ((ROWS, SHARDS * UNITS), BF),
        ],
        rows, centroid, in_hbm(shards),
        in_specs=[vmem, vmem, hbm],
        out_specs=[vmem] * 6,
        scratch_shapes=[
            pltpu.VMEM((SHARDS, PACKED, UNITS), BF), pltpu.SemaphoreType.DMA((SHARDS,)),
        ],
    )
    home = lax.all_to_all(
        mixed.reshape(ZH * EXPERTS, 2 * BLK, D), ("zh", "y", "zl"), 0, 0, tiled=True
    ).reshape(MIXED, D)
    (packed_grads,) = call(
        weight_grad_kernel,
        [hbm_out((SHARDS * PACKED, UNITS), BF)],
        *kept,
        in_specs=[vmem] * 4,
        out_specs=[hbm],
        scratch_shapes=[
            pltpu.VMEM((SHARDS, PACKED, UNITS), BF), pltpu.SemaphoreType.DMA((SHARDS,)),
        ],
    )
    grads = lax.psum_scatter(packed_grads, ("x", "core"), scatter_dimension=0, tiled=True)
    first_grad, second_grad = call(
        spread_kernel, [((1, D, UNITS), F32), ((1, UNITS, D), F32)], grads
    )
    centroid_terms = lax.all_gather(centroid_term, ("zh", "x", "core"), axis=0, tiled=True)
    grad_centroid = jnp.sum(centroid_terms, axis=0, keepdims=True)
    layer_out, grad_tokens = call(
        unpack_kernel, [((TOK, D), BF), ((TOK, D), BF)], slot_order, home, tokens, out_grad
    )
    return (layer_out, grad_tokens, grad_centroid, first_grad, second_grad)


def solution(mesh):
    fine = Mesh(mesh.devices.reshape(ZH, X, CORE, Y, ZL), ("zh", "x", "core", "y", "zl"))
    dp, expert = ("zh", "x", "core"), ("y", "zl")
    both = dp + expert
    placed = (
        P(both, None),
        P(both, None),
        P(expert, None),
        P(expert, None, dp),
        P(expert, dp, None),
        P(both, None),
    )
    return jax.shard_map(
        on_device,
        mesh=fine,
        in_specs=placed,
        out_specs=(
            P(both, None),
            P(both, None),
            P(expert, None),
            P(expert, None, dp),
            P(expert, dp, None),
        ),
        check_vma=False,
    )
```

time: 129 us -> 159 us (1.23)
  blocking collectives: 0 us -> 104 us
  starting transfers between devices: 66.6 us -> 7.57 us
  waiting for transfers between devices: 36.1 us -> 0.04 us
  Pallas kernels: 9.08 us -> 28.1 us
  between operations: 0.9 us -> 14.1 us
  other arithmetic: 6.79 us -> 0.62 us
  local copies, waits for them, and re-layouts: 7.57 us -> 1.74 us
    all_gather x0 -> x1, blocking collectives: none -> 53 us  [on_device(): lax.all_gather(centroid_term, ('zh', 'x', 'core'), axis=0, tiled=True)]
    all_to_all x0 -> x1, blocking collectives: none -> 50.7 us  [on_device(): lax.all_to_all(packed.reshape(ZH * EXPERTS, 2 * BLK, D), ('zh', 'y', 'zl'...]
    ppermute x11 -> x0, starting transfers between devices: 37.8 us -> none  [the longest x8 21.2 us: shift(): lax.ppermute(value, axis, [(i, (i + by) % size) for i in range(size)])]
    all_to_all x2 -> x1, waiting for transfers between devices: 23.5 us -> 0.01 us  [on_device(): lax.all_to_all(mixed.reshape(ZH * EXPERTS, 2 * BLK, D), ('zh', 'y', 'zl')...]
    all_to_all x2 -> x1, starting transfers between devices: 28.8 us -> 7.49 us  [on_device(): lax.all_to_all(mixed.reshape(ZH * EXPERTS, 2 * BLK, D), ('zh', 'y', 'zl')...]
    pallas_call x5, Pallas kernels: 9.08 us -> 28.1 us  [call(): pl.pallas_call(kernel, out_shape=[out if hasattr(out, 'memory_space') els...]
    ppermute x11 -> x0, waiting for transfers between devices: 12.7 us -> none  [the longest x8 12.7 us: shift(): lax.ppermute(value, axis, [(i, (i + by) % size) for i in range(size)])]
    slice x7 -> x0, local copies, waits for them, and re-layouts: 5.09 us -> none  [the longest x3 3.02 us: on_device(): arrived[D:D + UNITS]]
  transfers between devices with their start and end apart: 13 -> 3, of which waited for: 4 -> 0; matrix products, arithmetic and copies ran while one was open for 9% -> 0% of each run, Pallas kernels for 3% -> 1%
where the time goes in v2:
time: 159 us; the launch traced here: 156 us
  blocking collectives  104 us (65%)
  Pallas kernels  28.1 us (18%)
  between operations  14.1 us (9%)
  starting transfers between devices  7.57 us (5%)
  local copies, waits for them, and re-layouts  1.74 us (1%)
    all_gather x1, blocking collectives, on_device(): lax.all_gather(centroid_term, ('zh', 'x', 'core'), axis=0, tiled=True)  53 us
    all_to_all x1, blocking collectives, on_device(): lax.all_to_all(packed.reshape(ZH * EXPERTS, 2 * BLK, D), ('zh', 'y', 'zl'...  50.7 us
    pallas_call x5, Pallas kernels, call(): pl.pallas_call(kernel, out_shape=[out if hasattr(out, 'memory_space') els...  28.1 us
    all_to_all x1, starting transfers between devices, on_device(): lax.all_to_all(mixed.reshape(ZH * EXPERTS, 2 * BLK, D), ('zh', 'y', 'zl')...  7.49 us
  transfers between devices with their start and end apart: 3, of which 0 were waited for; matrix products, arithmetic and copies ran while one was open for 0% of the time, Pallas kernels for 1%

profile of v2, /device:TPU:6, one launch (start us, length us, event | category | flops | bytes accessed | tf_op | source)
XLA Modules:
  0.0 155.9 jit_solution(7246825475833676156)
XLA Ops:
  7.2 0.0 all-gather.3.cloned.1.call-start
  7.2 17.0 %shard_map.101 = (bf16[512,512]{1,0:T(8,128)(2,1)S(1)}, bf16[1024,256]{1,0:T(8,128)(2,1)}) custom-call(s32[1,128]{1,0:T(1,128)} %order_ref.3, bf16[128,512]{1,0:T(8,128)(2,1)} %tok_ref.3, bf16[128,512]{1,0:T(8,128)(2,1)} %grad_ref.3, bf16[1,512,256]{2,1,0:T(8,128)(2,1)} %first_ref.1, bf16[1,256,512]{2,1,0:T(8,128)(2,1)} %second_ref.1), custom_call_target="tpu_custom_call" | custom-call | tf_op jit(solution)/shard_map/pallas_call | solution.py:187
  24.3 0.0 all-gather.3.cloned.1.call-update
  24.3 0.0 reduce-scatter.2.cloned.1.call-start
  24.3 50.7 %all_to_all.10 = bf16[64,8,512]{2,1,0:T(8,128)(2,1)S(1)} all-to-all(bf16[64,8,512]{2,1,0:T(8,128)(2,1)S(1)} %bitcast.8), channel_id=1, replica_groups=mesh['zh'=2,'x'=4,'core'=2,'y'=4,'zl'=8] {'zh','y','zl'}, dimensions={0} | all-to-all | bytes 1048576 | tf_op jit(solution)/shard_map/all_to_all | solution.py:213
  75.1 0.0 all-gather.3.cloned.1.call-done.shards_ref
  75.1 0.0 copy-start.3
  75.1 0.7 copy-done.3
  75.8 6.6 %shard_map.102 = (bf16[512,512]{1,0:T(8,128)(2,1)}, f32[1,512]{1,0:T(1,128)S(1)}, bf16[256,512]{1,0:T(8,128)(2,1)S(1)}, bf16[256,512]{1,0:T(8,128)(2,1)S(1)}, bf...) custom-call(bf16[512,512]{1,0:T(8,128)(2,1)S(1)} %bitcast.6, bf16[1,512]{1,0:T(2,128)(2,1)S(1)} %copy-done.3, ...), custom_call_target="tpu_custom_call" | custom-call | tf_op jit(solution)/shard_map/pallas_call | solution.py:187
  82.4 2.4 %shard_map.104 = bf16[8192,256]{1,0:T(8,128)(2,1)} custom-call(bf16[256,512]{1,0:T(8,128)(2,1)S(1)} %get-tuple-element.23.routed_ref, bf16[256,512]{1,0:T(8,128)(2,1)S(1)} %get-tuple-element.24.d_expert_ref, bf16[256,2048]{1,0:T(8,128)(2,1)S(1)} %get-tuple-element.25.hidden_ref, bf16[256,2048]{1,0:T(8,128)(2,1)S(1)} %get-tuple-element.26.d_hidden_ref), custom_call_target="tpu_custom_call" | custom-call | tf_op jit(solution)/shard_map/pallas_call | solution.py:187
  84.7 0.0 copy-start.1
  84.7 0.0 copy-start.2
  84.8 0.0 copy-start.4
  84.8 0.0 reduce-scatter.2.cloned.1.call-update
  84.8 7.5 %all-to-all-start.1 = ((bf16[64,8,512]{2,1,0:T(8,128)(2,1)}), bf16[64,8,512]{2,1,0:T(8,128)(2,1)S(1)}, u32[]{:S(2)}, u32[]{:S(2)}) async-start(bf16[64,8,512]{2,1,0:T(8,128)(2,1)} %bitcast.2), calls=%async_computation.1 | async-start | bytes 1048576 | tf_op jit(solution)/shard_map/all_to_all | solution.py:229
  92.3 53.0 %all-gather = f32[16,1,512]{2,1,0:T(1,128)S(1)} all-gather(f32[1,1,512]{2,1,0:T(1,128)S(1)} %bitcast.9), channel_id=1, replica_groups=mesh['zh'=2,'x'=4,'core'=2,'y'=4,'zl'=8] {'zh','x','core'}, dimensions={0}, use_global_device_ids=true | all-gather | bytes 34816 | tf_op jit(solution)/shard_map/all_gather | solution.py:246
  145.3 0.6 reduce_sum.9
  145.9 0.0 all-to-all-done.1
  145.9 0.0 copy-done.1
  145.9 0.0 copy-done.2
  145.9 0.0 copy-done.4
  145.9 1.1 shard_map.103
  147.0 0.0 reduce-scatter.2.cloned.1.call-done.packed_ref
  147.0 0.0 copy-start
  147.0 1.0 copy-done
  148.0 1.0 shard_map.105
Async XLA Ops:
  7.2 67.9 %all-gather.3.cloned.1.call-start = ((), (), s32[]{:S(2)}) async-start(), calls=%async_computation.3 | async-start | bytes 4718592 | tf_op jit(solution)/shard_map/all_gather | solution.py:212
  24.3 122.7 %reduce-scatter.2.cloned.1.call-start = ((), (), s32[]{:S(2)}) async-start(), calls=%async_computation.4 | async-start | bytes 4718592 | tf_op jit(solution)/shard_map/reduce_scatter | solution.py:242
  75.1 0.7 copy-start.3
  84.7 61.1 %copy-start.1 = (bf16[128,512]{1,0:T(8,128)(2,1)S(1)}, bf16[128,512]{1,0:T(8,128)(2,1)}, u32[]{:S(2)}) copy-start(bf16[128,512]{1,0:T(8,128)(2,1)} %tok_ref.3) | copy-start | bytes 393220
  84.7 61.1 %copy-start.2 = (bf16[128,512]{1,0:T(8,128)(2,1)S(1)}, bf16[128,512]{1,0:T(8,128)(2,1)}, u32[]{:S(2)}) copy-start(bf16[128,512]{1,0:T(8,128)(2,1)} %grad_ref.3) | copy-start | bytes 393220
  84.8 61.1 %copy-start.4 = (s32[1,128]{1,0:T(1,128)S(1)}, s32[1,128]{1,0:T(1,128)}, u32[]{:S(2)}) copy-start(s32[1,128]{1,0:T(1,128)} %order_ref.3) | copy-start | bytes 1540
  84.8 61.1 %all-to-all-start.1 = ((bf16[64,8,512]{2,1,0:T(8,128)(2,1)}), bf16[64,8,512]{2,1,0:T(8,128)(2,1)S(1)}, u32[]{:S(2)}, u32[]{:S(2)}) async-start(bf16[64,8,512]{2,1,0:T(8,128)(2,1)} %bitcast.2), calls=%async_computation.1 | async-start | bytes 1048576 | tf_op jit(solution)/shard_map/all_to_all | solution.py:229
  147.0 1.0 copy-start
Sparse Core Ops, SparseCore 0:
  24.4 42.3 all-gather.2
  84.9 36.0 reduce-scatter.1

commit v3 on v1

--- a/solution.py
+++ b/solution.py
@@ -40,22 +40,36 @@
     return (mixed == place).astype(BF), (mixed == place + BLK).astype(BF)
 
 
-def pack_kernel(order_ref, tok_ref, grad_ref, out_ref):
+def pack_kernel(
+    order_ref, tok_ref, grad_ref, out_ref, order_vmem, tok_vmem, grad_vmem, sems
+):
+    copies = [
+        pltpu.make_async_copy(source, target, sems.at[i])
+        for i, (source, target) in enumerate(
+            ((order_ref, order_vmem), (tok_ref, tok_vmem), (grad_ref, grad_vmem))
+        )
+    ]
+    for copy in copies:
+        copy.start()
     token_pick, grad_pick = mixed_picks(TOK, True)
-    order = jnp.broadcast_to(order_ref[...].astype(F32), (8, TOK)).astype(BF)
     source = iota((TOK, 2 * TOK), 0).astype(F32)
+    kind = (iota((TOK, 2 * TOK), 1) // BLK) % 2
+    copies[0].wait()
+    order = jnp.broadcast_to(order_vmem[...].astype(F32), (8, TOK)).astype(BF)
     token_source = dot(order, token_pick)[0:1]
     grad_source = dot(order, grad_pick)[0:1]
-    kind = (iota((TOK, 2 * TOK), 1) // BLK) % 2
     pick_token = ((source == token_source) & (kind == 0)).astype(BF)
     pick_grad = ((source == grad_source) & (kind == 1)).astype(BF)
-    mixed = (dot(pick_token, tok_ref[...], 0, 0) + dot(pick_grad, grad_ref[...], 0, 0)).astype(BF)
+    copies[1].wait()
+    mixed = dot(pick_token, tok_vmem[...], 0, 0)
+    copies[2].wait()
+    mixed = (mixed + dot(pick_grad, grad_vmem[...], 0, 0)).astype(BF)
     for half in range(ZH):
         out_ref[half * 2 * TOK : (half + 1) * 2 * TOK, :] = mixed
 
 
 def expert_kernel(
-    rows_ref, centroid_ref, s0, s1, s2, s3,
+    rows_ref, centroid_ref, before_ref, s0, s1, s2, s3,
     mixed_ref, centroid_grad_ref, routed_ref, d_expert_ref, hidden_ref, d_hidden_ref,
 ):
     token_pick, grad_pick = mixed_picks(ROWS, True)
@@ -90,23 +104,28 @@
         hidden_ref[:, k * UNITS : (k + 1) * UNITS] = hidden
         d_hidden_ref[:, k * UNITS : (k + 1) * UNITS] = d_hidden
     d_logit = jnp.sum(d_routed * out_part, axis=1, keepdims=True) * gating * (1.0 - gating)
-    centroid_grad_ref[...] = jnp.sum(d_logit * routed, axis=0, keepdims=True)
+    centroid_grad = before_ref[...] + jnp.sum(d_logit * routed, axis=0, keepdims=True)
+    centroid_grad_ref[...] = centroid_grad
     layer_part = (gating * out_part).astype(BF)
     grad_part = (inner_part + d_logit * centroid).astype(BF)
     token_place, grad_place = mixed_picks(ROWS, False)
-    mixed_ref[...] = (dot(token_place, layer_part) + dot(grad_place, grad_part)).astype(BF)
-
-
-def weight_grad_kernel(
-    centroid_a, routed_a, d_expert_a, hidden_a, d_hidden_a,
-    centroid_b, routed_b, d_expert_b, hidden_b, d_hidden_b,
-    own_in, own_out, own_centroid, *sent,
-):
-    centroid_grad = centroid_a[...] + centroid_b[...]
-    own_centroid[...] = centroid_grad
+    mixed_ref[:MIXED, :] = (dot(token_place, layer_part) + dot(grad_place, grad_part)).astype(BF)
     high = centroid_grad.astype(BF).astype(F32)
     row = iota((NOTE, D), 0)
-    note = jnp.where(row == 0, high, jnp.where(row == 1, centroid_grad - high, 0.0)).astype(BF)
+    note = jnp.where(row == 0, high, jnp.where(row == 1, centroid_grad - high, 0.0))
+    mixed_ref[MIXED:, :] = note.astype(BF)
+
+
+def join_kernel(own_ref, other_ref, own_centroid_ref, out_ref, centroid_grad_ref):
+    out_ref[...] = (own_ref[:MIXED, :].astype(F32) + other_ref[:MIXED, :].astype(F32)).astype(BF)
+    note = other_ref[MIXED:, :].astype(F32)
+    centroid_grad_ref[...] = own_centroid_ref[...] + note[0:1] + note[1:2]
+
+
+def weight_grad_kernel(
+    routed_a, d_expert_a, hidden_a, d_hidden_a, routed_b, d_expert_b, hidden_b, d_hidden_b,
+    after_ref, own_in, own_out, *sent,
+):
     for k in range(X):
         units = slice(k * UNITS, (k + 1) * UNITS)
         first = dot(routed_a[...], d_hidden_a[:, units], 0, 0) + dot(
@@ -122,9 +141,16 @@
             packed = sent[k - 1]
             packed[:D, :] = first.astype(BF)
             packed[D : D + UNITS, :] = second[:, :HALF].astype(BF)
-            packed[D + UNITS : PACKED, :] = second[:, HALF:].astype(BF)
-            packed[PACKED : PACKED + NOTE, :] = note[:, :HALF]
-            packed[PACKED + NOTE :, :] = note[:, HALF:]
+            packed[D + UNITS :, :] = second[:, HALF:].astype(BF)
+
+
+def total_kernel(own_in, own_out, p1, p2, p3, first_ref, second_ref):
+    def total(rows):
+        return p1[rows, :].astype(F32) + p2[rows, :].astype(F32) + p3[rows, :].astype(F32)
+
+    first_ref[0] = own_in[...] + total(slice(0, D))
+    second_ref[0, :, :HALF] = own_out[:, :HALF] + total(slice(D, D + UNITS))
+    second_ref[0, :, HALF:] = own_out[:, HALF:] + total(slice(D + UNITS, PACKED))
 
 
 def unpack_kernel(order_ref, home_ref, tok_ref, grad_ref, layer_ref, grad_out_ref):
@@ -144,11 +170,16 @@
     grad_out_ref[...] = grad.astype(BF)
 
 
-def call(kernel, shapes, *operands):
+def in_hbm(value):
+    return pltpu.with_memory_space_constraint(value, pltpu.HBM)
+
+
+def call(kernel, outs, *operands, **options):
     return pl.pallas_call(
         kernel,
-        out_shape=[jax.ShapeDtypeStruct(shape, dtype) for shape, dtype in shapes],
+        out_shape=[jax.ShapeDtypeStruct(*out) for out in outs],
         compiler_params=pltpu.CompilerParams(vmem_limit_bytes=VMEM_LIMIT),
+        **options,
     )(*operands)
 
 
@@ -157,51 +188,57 @@
 
 
 def on_device(tokens, slot_order, centroid, weight_in, weight_out, out_grad):
+    vmem, hbm = pl.BlockSpec(memory_space=pltpu.VMEM), pl.BlockSpec(memory_space=pltpu.HBM)
     second = weight_out[0]
     shard = jnp.concatenate([weight_in[0], second[:, :HALF], second[:, HALF:]], axis=0)
     shards = [shard] + [shift(shard, "x", X, -k) for k in range(1, X)]
-    (packed,) = call(pack_kernel, [((MIXED, D), BF)], slot_order, tokens, out_grad)
+    (packed,) = call(
+        pack_kernel,
+        [((MIXED, D), BF)],
+        *(in_hbm(each) for each in (slot_order, tokens, out_grad)),
+        in_specs=[hbm] * 3,
+        out_specs=[vmem],
+        scratch_shapes=[
+            pltpu.VMEM((1, TOK), jnp.int32),
+            pltpu.VMEM((TOK, D), BF),
+            pltpu.VMEM((TOK, D), BF),
+            pltpu.SemaphoreType.DMA((3,)),
+        ],
+    )
     own_rows = lax.all_to_all(
         packed.reshape(ZH * EXPERTS, 2 * BLK, D), ("zh", "y", "zl"), 0, 0, tiled=True
     ).reshape(MIXED, D)
     other_rows = shift(own_rows, "core", CORE, 1)
     part_shapes = [
-        ((MIXED, D), BF), ((1, D), F32), ((ROWS, D), BF), ((ROWS, D), BF),
+        ((MIXED + NOTE, D), BF), ((1, D), F32), ((ROWS, D), BF), ((ROWS, D), BF),
         ((ROWS, X * UNITS), BF), ((ROWS, X * UNITS), BF),
     ]
-    own = call(expert_kernel, part_shapes, own_rows, centroid, *shards)
-    other = call(expert_kernel, part_shapes, other_rows, centroid, *shards)
+    nothing = jnp.zeros((1, D), F32)
+    own = call(expert_kernel, part_shapes, own_rows, centroid, nothing, *shards)
+    other = call(expert_kernel, part_shapes, other_rows, centroid, own[1], *shards)
     from_other = shift(other[0], "core", CORE, 1)
-    grads = call(
-        weight_grad_kernel,
-        [((D, UNITS), F32), ((UNITS, D), F32), ((1, D), F32)]
-        + [((PACKED + 2 * NOTE, UNITS), BF)] * (X - 1),
-        *own[1:], *other[1:],
-    )
-    first_grad, second_grad, centroid_grad = grads[:3]
-    for k in range(1, X):
-        arrived = shift(grads[2 + k], "x", X, k).astype(F32)
-        first_grad += arrived[:D]
-        second_grad += jnp.concatenate([arrived[D : D + UNITS], arrived[D + UNITS : PACKED]], axis=1)
-        note = jnp.concatenate([arrived[PACKED : PACKED + 2], arrived[PACKED + NOTE : PACKED + NOTE + 2]], axis=1)
-        centroid_grad += note[0:1] + note[1:2]
-    turns = [(1, 0), (0, 1), (1, 1)]
-    grad_centroid = centroid_grad + sum(
-        lax.ppermute(
-            centroid_grad,
-            ("zh", "core"),
-            [(2 * a + b, 2 * (a ^ i) + (b ^ j)) for a in range(ZH) for b in range(CORE)],
-        )
-        for i, j in turns
-    )
-    returned = (own[0].astype(F32) + from_other.astype(F32)).astype(BF)
+    returned, centroid_grad = call(
+        join_kernel, [((MIXED, D), BF), ((1, D), F32)], own[0], from_other, other[1]
+    )
     home = lax.all_to_all(
         returned.reshape(ZH * EXPERTS, 2 * BLK, D), ("zh", "y", "zl"), 0, 0, tiled=True
     ).reshape(MIXED, D)
+    grads = call(
+        weight_grad_kernel,
+        [((D, UNITS), F32), ((UNITS, D), F32)] + [((PACKED, UNITS), BF)] * (X - 1),
+        *own[2:], *other[2:], returned,
+        in_specs=[vmem] * 8 + [pl.BlockSpec(memory_space=pl.ANY)],
+    )
+    arrived = [shift(grads[1 + k], "x", X, k) for k in range(1, X)]
+    first_grad, second_grad = call(
+        total_kernel, [((1, D, UNITS), F32), ((1, UNITS, D), F32)], *grads[:2], *arrived
+    )
+    centroid_grad += shift(centroid_grad, "zh", ZH, 1)
+    grad_centroid = centroid_grad + sum(shift(centroid_grad, "x", X, k) for k in range(1, X))
     layer_out, grad_tokens = call(
         unpack_kernel, [((TOK, D), BF), ((TOK, D), BF)], slot_order, home, tokens, out_grad
     )
-    return (layer_out, grad_tokens, grad_centroid, first_grad[None], second_grad[None])
+    return (layer_out, grad_tokens, grad_centroid, first_grad, second_grad)
 
 
 def solution(mesh):

time: 129 us -> 132 us (1.023)
  the two profiles are of different devices: /device:TPU:6 before, /device:TPU:8 now
where the time goes in v3:
time: 132 us; the launch traced here: 131 us
  starting transfers between devices  80.3 us (61%)
  waiting for transfers between devices  32.4 us (25%)
  Pallas kernels  11.9 us (9%)
  local copies, waits for them, and re-layouts  5.02 us (4%)
    ppermute x12, starting transfers between devices, shift(): lax.ppermute(value, axis, [(i, (i + by) % size) for i in range(size)])  49.5 us
    all_to_all x1, waiting for transfers between devices, on_device(): lax.all_to_all(packed.reshape(ZH * EXPERTS, 2 * BLK, D), ('zh', 'y', 'zl'...  19.9 us
    all_to_all x1, starting transfers between devices, on_device(): lax.all_to_all(packed.reshape(ZH * EXPERTS, 2 * BLK, D), ('zh', 'y', 'zl'...  18.9 us
    ppermute x12, waiting for transfers between devices, shift(): lax.ppermute(value, axis, [(i, (i + by) % size) for i in range(size)])  12.5 us
    pallas_call x7, Pallas kernels, call(): pl.pallas_call(kernel, out_shape=[jax.ShapeDtypeStruct(*out) for out in o...  11.9 us
    all_to_all x1, starting transfers between devices, on_device(): lax.all_to_all(returned.reshape(ZH * EXPERTS, 2 * BLK, D), ('zh', 'y', 'z...  11.9 us
    unnamed x32, local copies, waits for them, and re-layouts  5 us
  transfers between devices with their start and end apart: 14, of which 5 were waited for; matrix products, arithmetic and copies ran while one was open for 0% of the time, Pallas kernels for 4%

profile of v3, /device:TPU:8, one launch (start us, length us, event | category | flops | bytes accessed | tf_op | source)
XLA Modules:
  0.0 131.2 jit_solution(4830946190555117576)
XLA Ops:
  0.6 2.1 %shard_map.101 = bf16[512,512]{1,0:T(8,128)(2,1)} custom-call(s32[1,128]{1,0:T(1,128)} %order_ref.3, bf16[128,512]{1,0:T(8,128)(2,1)} %tok_ref.3, bf16[128,512]{1,0:T(8,128)(2,1)} %grad_ref.3), custom_call_target="tpu_custom_call" | custom-call | tf_op jit(solution)/shard_map/pallas_call | solution.py:178
  2.8 0.0 copy-start.14
  2.8 18.9 %all-to-all-start = ((bf16[64,8,512]{2,1,0:T(8,128)(2,1)}), bf16[64,8,512]{2,1,0:T(8,128)(2,1)S(1)}, u32[]{:S(2)}, u32[]{:S(2)}) async-start(bf16[64,8,512]{2,1,0:T(8,128)(2,1)} %bitcast), calls=%async_computation | async-start | bytes 1048576 | tf_op jit(solution)/shard_map/all_to_all | solution.py:208
  21.7 0.0 copy-start.15
  21.7 0.9 copy-done.15
  22.7 0.0 copy-start.12
  22.7 3.4 %collective-permute-start.2 = (bf16[1024,256]{1,0:T(8,128)(2,1)S(1)}, bf16[1024,256]{1,0:T(8,128)(2,1)S(1)}, u32[]{:S(2)}, u32[]{:S(2)}) collective-permute-start(bf16[1024,256]{1,0:T(8,128)(2,1)S(1)} %pad_maximum_fusion.s0), channel_id=1, source_target_pairs={{0,64},{64,128},{128,192},{192,0},{1,65},{65,129},{129,193},{193,1... | collective-permute-start | bytes 1572872 | tf_op jit(solution)/shard_map/ppermute | solution.py:187
  26.1 4.6 %collective-permute-start.1 = (bf16[1024,256]{1,0:T(8,128)(2,1)S(1)}, bf16[1024,256]{1,0:T(8,128)(2,1)S(1)}, u32[]{:S(2)}, u32[]{:S(2)}) collective-permute-start(bf16[1024,256]{1,0:T(8,128)(2,1)S(1)} %pad_maximum_fusion.s0), channel_id=1, source_target_pairs={{0,128},{64,192},{128,0},{192,64},{1,129},{65,193},{129,1},{193,65... | collective-permute-start | bytes 1572872 | tf_op jit(solution)/shard_map/ppermute | solution.py:187
  30.7 3.3 %collective-permute-start = (bf16[1024,256]{1,0:T(8,128)(2,1)S(1)}, bf16[1024,256]{1,0:T(8,128)(2,1)S(1)}, u32[]{:S(2)}, u32[]{:S(2)}) collective-permute-start(bf16[1024,256]{1,0:T(8,128)(2,1)S(1)} %pad_maximum_fusion.s0), channel_id=1, source_target_pairs={{0,192},{64,0},{128,64},{192,128},{1,193},{65,1},{129,65},{193,129... | collective-permute-start | bytes 1572872 | tf_op jit(solution)/shard_map/ppermute | solution.py:187
  34.1 19.9 %all-to-all-done = bf16[64,8,512]{2,1,0:T(8,128)(2,1)S(1)} async-done(((bf16[64,8,512]{2,1,0:T(8,128)(2,1)}), bf16[64,8,512]{2,1,0:T(8,128)(2,1)S(1)}, u32[]{:S(2)}, u32[]{:S(2)}) %all-to-all-start) | async-done | bytes 524320 | tf_op jit(solution)/shard_map/all_to_all | solution.py:208
  54.0 1.9 %collective-permute-start.3 = (bf16[512,512]{1,0:T(8,128)(2,1)S(1)}, bf16[512,512]{1,0:T(8,128)(2,1)S(1)}, u32[]{:S(2)}, u32[]{:S(2)}) collective-permute-start(bf16[512,512]{1,0:T(8,128)(2,1)S(1)} %bitcast.6), channel_id=1, source_target_pairs={{0,32},{32,0},{1,33},{33,1},{2,34},{34,2},{3,35},{35,3},{4,36},{36... | collective-permute-start | bytes 1572872 | tf_op jit(solution)/shard_map/ppermute | solution.py:187
  55.9 0.0 collective-permute-done.2.s3
  55.9 0.0 collective-permute-done.1.s2
  55.9 0.0 collective-permute-done.s1
  56.0 2.7 %shard_map.102 = (bf16[528,512]{1,0:T(8,128)(2,1)S(1)}, f32[1,512]{1,0:T(1,128)S(1)}, bf16[256,512]{1,0:T(8,128)(2,1)S(1)}, bf16[256,512]{1,0:T(8,128)(2,1)S(1)}...) custom-call(bf16[512,512]{1,0:T(8,128)(2,1)S(1)} %bitcast.7, bf16[1,512]{1,0:T(2,128)(2,1)S(1)} %copy-done.12, ...), custom_call_target="tpu_custom_call" | custom-call | tf_op jit(solution)/shard_map/pallas_call | solution.py:178
  58.7 0.0 copy-start
  58.7 0.8 copy-done
  59.5 0.7 copy-done.6
  60.2 2.7 %shard_map.103 = (bf16[528,512]{1,0:T(8,128)(2,1)S(1)}, f32[1,512]{1,0:T(1,128)S(1)}, bf16[256,512]{1,0:T(8,128)(2,1)S(1)}, bf16[256,512]{1,0:T(8,128)(2,1)S(1)}...) custom-call(bf16[512,512]{1,0:T(8,128)(2,1)S(1)} %collective-permute-done.3.rows_ref, ...), custom_call_target="tpu_custom_call" | custom-call | tf_op jit(solution)/shard_map/pallas_call | solution.py:178
  62.9 0.0 copy-start.2
  62.9 2.4 %collective-permute-start.4 = (bf16[528,512]{1,0:T(8,128)(2,1)S(1)}, bf16[528,512]{1,0:T(8,128)(2,1)S(1)}, u32[]{:S(2)}, u32[]{:S(2)}) collective-permute-start(bf16[528,512]{1,0:T(8,128)(2,1)S(1)} %get-tuple-element.30), channel_id=1, source_target_pairs={{0,32},{32,0},{1,33},{33,1},{2,34},{34,2},{3,35},{35,3},{4,36},{36... | collective-permute-start | bytes 1622024 | tf_op jit(solution)/shard_map/ppermute | solution.py:187
  65.3 1.5 %collective-permute-done.4.other_ref = bf16[528,512]{1,0:T(8,128)(2,1)S(1)} collective-permute-done((bf16[528,512]{1,0:T(8,128)(2,1)S(1)}, bf16[528,512]{1,0:T(8,128)(2,1)S(1)}, u32[]{:S(2)}, u32[]{:S(2)}) %collective-permute-start.4) | collective-permute-done | bytes 540704 | tf_op jit(solution)/shard_map/ppermute | solution.py:187
  66.8 0.9 shard_map.104
  67.8 0.0 copy-start.3
  67.8 11.9 %all-to-all-start.1 = ((bf16[64,8,512]{2,1,0:T(8,128)(2,1)}), bf16[64,8,512]{2,1,0:T(8,128)(2,1)S(1)}, u32[]{:S(2)}, u32[]{:S(2)}) async-start(bf16[64,8,512]{2,1,0:T(8,128)(2,1)} %bitcast.4), calls=%async_computation.1 | async-start | bytes 1048576 | tf_op jit(solution)/shard_map/all_to_all | solution.py:223
  79.7 0.9 copy-done.9
  80.7 0.9 copy-done.11
  81.6 1.3 shard_map.106
  82.9 4.3 %collective-permute-start.9 = (bf16[1024,256]{1,0:T(8,128)(2,1)S(1)}, bf16[1024,256]{1,0:T(8,128)(2,1)S(1)}, u32[]{:S(2)}, u32[]{:S(2)}) collective-permute-start(bf16[1024,256]{1,0:T(8,128)(2,1)S(1)} %get-tuple-element.46), channel_id=1, source_target_pairs={{0,64},{64,128},{128,192},{192,0},{1,65},{65,129},{129,193},{193,1... | collective-permute-start | bytes 1572872 | tf_op jit(solution)/shard_map/ppermute | solution.py:187
  87.2 3.6 %collective-permute-start.10 = (bf16[1024,256]{1,0:T(8,128)(2,1)S(1)}, bf16[1024,256]{1,0:T(8,128)(2,1)S(1)}, u32[]{:S(2)}, u32[]{:S(2)}) collective-permute-start(bf16[1024,256]{1,0:T(8,128)(2,1)S(1)} %get-tuple-element.47), channel_id=1, source_target_pairs={{0,128},{64,192},{128,0},{192,64},{1,129},{65,193},{129,1},{193,65... | collective-permute-start | bytes 1572872 | tf_op jit(solution)/shard_map/ppermute | solution.py:187
  90.8 3.5 %collective-permute-start.11 = (bf16[1024,256]{1,0:T(8,128)(2,1)S(1)}, bf16[1024,256]{1,0:T(8,128)(2,1)S(1)}, u32[]{:S(2)}, u32[]{:S(2)}) collective-permute-start(bf16[1024,256]{1,0:T(8,128)(2,1)S(1)} %get-tuple-element.48), channel_id=1, source_target_pairs={{0,192},{64,0},{128,64},{192,128},{1,193},{65,1},{129,65},{193,129... | collective-permute-start | bytes 1572872 | tf_op jit(solution)/shard_map/ppermute | solution.py:187
  94.3 12.2 %collective-permute-start.5 = (f32[1,512]{1,0:T(1,128)S(1)}, f32[1,512]{1,0:T(1,128)S(1)}, u32[]{:S(2)}, u32[]{:S(2)}) collective-permute-start(f32[1,512]{1,0:T(1,128)S(1)} %get-tuple-element.35), channel_id=1, source_target_pairs={{0,256},{256,0},{1,257},{257,1},{2,258},{258,2},{3,259},{259,3},{4... | collective-permute-start | bytes 6152 | tf_op jit(solution)/shard_map/ppermute | solution.py:187
  106.6 6.2 %collective-permute-done.5 = f32[1,512]{1,0:T(1,128)S(1)} collective-permute-done((f32[1,512]{1,0:T(1,128)S(1)}, f32[1,512]{1,0:T(1,128)S(1)}, u32[]{:S(2)}, u32[]{:S(2)}) %collective-permute-start.5) | collective-permute-done | bytes 2080 | tf_op jit(solution)/shard_map/ppermute | solution.py:187
  112.7 4.6 %collective-permute-start.8 = (f32[1,512]{1,0:T(1,128)S(1)}, f32[1,512]{1,0:T(1,128)S(1)}, u32[]{:S(2)}, u32[]{:S(2)}) collective-permute-start(f32[1,512]{1,0:T(1,128)S(1)} %add.12), channel_id=1, source_target_pairs={{0,192},{64,0},{128,64},{192,128},{1,193},{65,1},{129,65},{193,129... | collective-permute-start | bytes 6152 | tf_op jit(solution)/shard_map/ppermute | solution.py:187
  117.3 3.7 %collective-permute-start.7 = (f32[1,512]{1,0:T(1,128)S(1)}, f32[1,512]{1,0:T(1,128)S(1)}, u32[]{:S(2)}, u32[]{:S(2)}) collective-permute-start(f32[1,512]{1,0:T(1,128)S(1)} %add.12), channel_id=1, source_target_pairs={{0,128},{64,192},{128,0},{192,64},{1,129},{65,193},{129,1},{193,65... | collective-permute-start | bytes 6152 | tf_op jit(solution)/shard_map/ppermute | solution.py:187
  121.0 0.0 collective-permute-done.8
  121.0 1.9 %collective-permute-start.6 = (f32[1,512]{1,0:T(1,128)S(1)}, f32[1,512]{1,0:T(1,128)S(1)}, u32[]{:S(2)}, u32[]{:S(2)}) collective-permute-start(f32[1,512]{1,0:T(1,128)S(1)} %add.12), channel_id=1, source_target_pairs={{0,64},{64,128},{128,192},{192,0},{1,65},{65,129},{129,193},{193,1... | collective-permute-start | bytes 6152 | tf_op jit(solution)/shard_map/ppermute | solution.py:187
  123.0 1.3 %collective-permute-done.7 = f32[1,512]{1,0:T(1,128)S(1)} collective-permute-done((f32[1,512]{1,0:T(1,128)S(1)}, f32[1,512]{1,0:T(1,128)S(1)}, u32[]{:S(2)}, u32[]{:S(2)}) %collective-permute-start.7) | collective-permute-done | bytes 2080 | tf_op jit(solution)/shard_map/ppermute | solution.py:187
  124.3 3.4 %collective-permute-done.6 = f32[1,512]{1,0:T(1,128)S(1)} collective-permute-done((f32[1,512]{1,0:T(1,128)S(1)}, f32[1,512]{1,0:T(1,128)S(1)}, u32[]{:S(2)}, u32[]{:S(2)}) %collective-permute-start.6) | collective-permute-done | bytes 2080 | tf_op jit(solution)/shard_map/ppermute | solution.py:187
  127.7 0.6 add_add_fusion
  128.3 0.0 collective-permute-done.9.p1
  128.3 0.0 collective-permute-done.10.p2
  128.3 0.0 copy-start.4
  128.3 0.0 copy-start.5
  128.3 1.1 shard_map.107
  129.4 0.0 all-to-all-done.1
  129.5 0.6 copy-done.13
  130.1 1.1 shard_map.105
  (24 shorter events, 0.1 us)
Async XLA Ops:
  2.8 18.9 %copy-start.14 = (bf16[1,256,512]{2,1,0:T(8,128)(2,1)S(1)}, bf16[1,256,512]{2,1,0:T(8,128)(2,1)}, u32[]{:S(2)}) copy-start(bf16[1,256,512]{2,1,0:T(8,128)(2,1)} %param.10) | copy-start | bytes 786436
  2.8 51.2 %all-to-all-start = ((bf16[64,8,512]{2,1,0:T(8,128)(2,1)}), bf16[64,8,512]{2,1,0:T(8,128)(2,1)S(1)}, u32[]{:S(2)}, u32[]{:S(2)}) async-start(bf16[64,8,512]{2,1,0:T(8,128)(2,1)} %bitcast), calls=%async_computation | async-start | bytes 1048576 | tf_op jit(solution)/shard_map/all_to_all | solution.py:208
  21.7 1.0 copy-start.15
  22.7 33.3 %copy-start.12 = (bf16[1,512]{1,0:T(2,128)(2,1)S(1)}, bf16[1,512]{1,0:T(2,128)(2,1)}, u32[]{:S(2)}) copy-start(bf16[1,512]{1,0:T(2,128)(2,1)} %centroid_ref.3) | copy-start | bytes 3076
  22.7 33.3 %collective-permute-start.2 = (bf16[1024,256]{1,0:T(8,128)(2,1)S(1)}, bf16[1024,256]{1,0:T(8,128)(2,1)S(1)}, u32[]{:S(2)}, u32[]{:S(2)}) collective-permute-start(bf16[1024,256]{1,0:T(8,128)(2,1)S(1)} %pad_maximum_fusion.s0), channel_id=1, source_target_pairs={{0,64},{64,128},{128,192},{192,0},{1,65},{65,129},{129,193},{193,1... | collective-permute-start | bytes 1572872 | tf_op jit(solution)/shard_map/ppermute | solution.py:187
  26.1 29.9 %collective-permute-start.1 = (bf16[1024,256]{1,0:T(8,128)(2,1)S(1)}, bf16[1024,256]{1,0:T(8,128)(2,1)S(1)}, u32[]{:S(2)}, u32[]{:S(2)}) collective-permute-start(bf16[1024,256]{1,0:T(8,128)(2,1)S(1)} %pad_maximum_fusion.s0), channel_id=1, source_target_pairs={{0,128},{64,192},{128,0},{192,64},{1,129},{65,193},{129,1},{193,65... | collective-permute-start | bytes 1572872 | tf_op jit(solution)/shard_map/ppermute | solution.py:187
  30.7 25.2 %collective-permute-start = (bf16[1024,256]{1,0:T(8,128)(2,1)S(1)}, bf16[1024,256]{1,0:T(8,128)(2,1)S(1)}, u32[]{:S(2)}, u32[]{:S(2)}) collective-permute-start(bf16[1024,256]{1,0:T(8,128)(2,1)S(1)} %pad_maximum_fusion.s0), channel_id=1, source_target_pairs={{0,192},{64,0},{128,64},{192,128},{1,193},{65,1},{129,65},{193,129... | collective-permute-start | bytes 1572872 | tf_op jit(solution)/shard_map/ppermute | solution.py:187
  54.0 6.2 %collective-permute-start.3 = (bf16[512,512]{1,0:T(8,128)(2,1)S(1)}, bf16[512,512]{1,0:T(8,128)(2,1)S(1)}, u32[]{:S(2)}, u32[]{:S(2)}) collective-permute-start(bf16[512,512]{1,0:T(8,128)(2,1)S(1)} %bitcast.6), channel_id=1, source_target_pairs={{0,32},{32,0},{1,33},{33,1},{2,34},{34,2},{3,35},{35,3},{4,36},{36... | collective-permute-start | bytes 1572872 | tf_op jit(solution)/shard_map/ppermute | solution.py:187
  58.7 0.8 copy-start
  59.5 0.7 copy-start.6
  62.9 4.9 %copy-start.2 = (bf16[256,1024]{1,0:T(8,128)(2,1)}, bf16[256,1024]{1,0:T(8,128)(2,1)S(1)}, u32[]{:S(2)}) copy-start(bf16[256,1024]{1,0:T(8,128)(2,1)S(1)} %get-tuple-element.43.d_hidden_b) | copy-start | bytes 1572868
  62.9 4.9 %copy-start.8 = (bf16[256,512]{1,0:T(8,128)(2,1)}, bf16[256,512]{1,0:T(8,128)(2,1)S(1)}, u32[]{:S(2)}) copy-start(bf16[256,512]{1,0:T(8,128)(2,1)S(1)} %get-tuple-element.40.routed_b) | copy-start | bytes 786436
  62.9 4.9 %copy-start.10 = (bf16[256,512]{1,0:T(8,128)(2,1)}, bf16[256,512]{1,0:T(8,128)(2,1)S(1)}, u32[]{:S(2)}) copy-start(bf16[256,512]{1,0:T(8,128)(2,1)S(1)} %get-tuple-element.41.d_expert_b) | copy-start | bytes 786436
  62.9 3.9 %collective-permute-start.4 = (bf16[528,512]{1,0:T(8,128)(2,1)S(1)}, bf16[528,512]{1,0:T(8,128)(2,1)S(1)}, u32[]{:S(2)}, u32[]{:S(2)}) collective-permute-start(bf16[528,512]{1,0:T(8,128)(2,1)S(1)} %get-tuple-element.30), channel_id=1, source_target_pairs={{0,32},{32,0},{1,33},{33,1},{2,34},{34,2},{3,35},{35,3},{4,36},{36... | collective-permute-start | bytes 1622024 | tf_op jit(solution)/shard_map/ppermute | solution.py:187
  66.8 12.9 %copy-start.7 = (bf16[256,512]{1,0:T(8,128)(2,1)S(1)}, bf16[256,512]{1,0:T(8,128)(2,1)}, u32[]{:S(2)}) copy-start(bf16[256,512]{1,0:T(8,128)(2,1)} %copy-done.6) | copy-start | bytes 786436
  67.8 11.9 %copy-start.1 = (bf16[256,1024]{1,0:T(8,128)(2,1)S(1)}, bf16[256,1024]{1,0:T(8,128)(2,1)}, u32[]{:S(2)}) copy-start(bf16[256,1024]{1,0:T(8,128)(2,1)} %copy-done) | copy-start | bytes 1572868
  67.8 11.9 %copy-start.3 = (bf16[256,1024]{1,0:T(8,128)(2,1)S(1)}, bf16[256,1024]{1,0:T(8,128)(2,1)}, u32[]{:S(2)}) copy-start(bf16[256,1024]{1,0:T(8,128)(2,1)} %copy-done.2) | copy-start | bytes 1572868
  67.8 61.7 %all-to-all-start.1 = ((bf16[64,8,512]{2,1,0:T(8,128)(2,1)}), bf16[64,8,512]{2,1,0:T(8,128)(2,1)S(1)}, u32[]{:S(2)}, u32[]{:S(2)}) async-start(bf16[64,8,512]{2,1,0:T(8,128)(2,1)} %bitcast.4), calls=%async_computation.1 | async-start | bytes 1048576 | tf_op jit(solution)/shard_map/all_to_all | solution.py:223
  79.7 1.0 copy-start.9
  80.7 0.9 copy-start.11
  82.9 45.4 %collective-permute-start.9 = (bf16[1024,256]{1,0:T(8,128)(2,1)S(1)}, bf16[1024,256]{1,0:T(8,128)(2,1)S(1)}, u32[]{:S(2)}, u32[]{:S(2)}) collective-permute-start(bf16[1024,256]{1,0:T(8,128)(2,1)S(1)} %get-tuple-element.46), channel_id=1, source_target_pairs={{0,64},{64,128},{128,192},{192,0},{1,65},{65,129},{129,193},{193,1... | collective-permute-start | bytes 1572872 | tf_op jit(solution)/shard_map/ppermute | solution.py:187
  87.2 41.1 %collective-permute-start.10 = (bf16[1024,256]{1,0:T(8,128)(2,1)S(1)}, bf16[1024,256]{1,0:T(8,128)(2,1)S(1)}, u32[]{:S(2)}, u32[]{:S(2)}) collective-permute-start(bf16[1024,256]{1,0:T(8,128)(2,1)S(1)} %get-tuple-element.47), channel_id=1, source_target_pairs={{0,128},{64,192},{128,0},{192,64},{1,129},{65,193},{129,1},{193,65... | collective-permute-start | bytes 1572872 | tf_op jit(solution)/shard_map/ppermute | solution.py:187
  90.8 37.5 %collective-permute-start.11 = (bf16[1024,256]{1,0:T(8,128)(2,1)S(1)}, bf16[1024,256]{1,0:T(8,128)(2,1)S(1)}, u32[]{:S(2)}, u32[]{:S(2)}) collective-permute-start(bf16[1024,256]{1,0:T(8,128)(2,1)S(1)} %get-tuple-element.48), channel_id=1, source_target_pairs={{0,192},{64,0},{128,64},{192,128},{1,193},{65,1},{129,65},{193,129... | collective-permute-start | bytes 1572872 | tf_op jit(solution)/shard_map/ppermute | solution.py:187
  94.3 18.4 %collective-permute-start.5 = (f32[1,512]{1,0:T(1,128)S(1)}, f32[1,512]{1,0:T(1,128)S(1)}, u32[]{:S(2)}, u32[]{:S(2)}) collective-permute-start(f32[1,512]{1,0:T(1,128)S(1)} %get-tuple-element.35), channel_id=1, source_target_pairs={{0,256},{256,0},{1,257},{257,1},{2,258},{258,2},{3,259},{259,3},{4... | collective-permute-start | bytes 6152 | tf_op jit(solution)/shard_map/ppermute | solution.py:187
  112.7 8.3 %collective-permute-start.8 = (f32[1,512]{1,0:T(1,128)S(1)}, f32[1,512]{1,0:T(1,128)S(1)}, u32[]{:S(2)}, u32[]{:S(2)}) collective-permute-start(f32[1,512]{1,0:T(1,128)S(1)} %add.12), channel_id=1, source_target_pairs={{0,192},{64,0},{128,64},{192,128},{1,193},{65,1},{129,65},{193,129... | collective-permute-start | bytes 6152 | tf_op jit(solution)/shard_map/ppermute | solution.py:187
  117.3 7.0 %collective-permute-start.7 = (f32[1,512]{1,0:T(1,128)S(1)}, f32[1,512]{1,0:T(1,128)S(1)}, u32[]{:S(2)}, u32[]{:S(2)}) collective-permute-start(f32[1,512]{1,0:T(1,128)S(1)} %add.12), channel_id=1, source_target_pairs={{0,128},{64,192},{128,0},{192,64},{1,129},{65,193},{129,1},{193,65... | collective-permute-start | bytes 6152 | tf_op jit(solution)/shard_map/ppermute | solution.py:187
  121.0 6.7 %collective-permute-start.6 = (f32[1,512]{1,0:T(1,128)S(1)}, f32[1,512]{1,0:T(1,128)S(1)}, u32[]{:S(2)}, u32[]{:S(2)}) collective-permute-start(f32[1,512]{1,0:T(1,128)S(1)} %add.12), channel_id=1, source_target_pairs={{0,64},{64,128},{128,192},{192,0},{1,65},{65,129},{129,193},{193,1... | collective-permute-start | bytes 6152 | tf_op jit(solution)/shard_map/ppermute | solution.py:187
  128.3 1.1 copy-start.4
  128.3 1.1 copy-start.5
  129.4 0.7 copy-start.13

commit v4 on v3

--- a/solution.py
+++ b/solution.py
@@ -20,6 +20,7 @@
 UNITS = 256
 HALF = D // 2
 PACKED = D + 2 * UNITS
+HID, DHID, ROUTED, DEXP, KEPT = 0, X * UNITS, 2 * X * UNITS, 2 * X * UNITS + D, 2 * X * UNITS + 2 * D
 NOTE = 16
 VMEM_LIMIT = 16 * 1024 * 1024
 
@@ -70,8 +71,17 @@
 
 def expert_kernel(
     rows_ref, centroid_ref, before_ref, s0, s1, s2, s3,
-    mixed_ref, centroid_grad_ref, routed_ref, d_expert_ref, hidden_ref, d_hidden_ref,
+    mixed_ref, centroid_grad_ref, kept_ref, kept, sems,
 ):
+    def keep(value, at, slot):
+        columns = slice(at, at + value.shape[1])
+        kept[:, columns] = value
+        copies.append(
+            pltpu.make_async_copy(kept.at[:, columns], kept_ref.at[:, columns], sems.at[slot])
+        )
+        copies[-1].start()
+
+    copies = []
     token_pick, grad_pick = mixed_picks(ROWS, True)
     received = rows_ref[...]
     routed = dot(token_pick, received)
@@ -80,8 +90,8 @@
     gating = jax.nn.sigmoid(jnp.sum(routed * centroid, axis=1, keepdims=True))
     routed_half = routed.astype(BF)
     d_expert = (gating * d_routed).astype(BF)
-    routed_ref[...] = routed_half
-    d_expert_ref[...] = d_expert
+    keep(routed_half, ROUTED, 0)
+    keep(d_expert, DEXP, 1)
     out_part = jnp.zeros((ROWS, D), F32)
     inner_part = jnp.zeros((ROWS, D), F32)
     scale = math.sqrt(2.0 / math.pi)
@@ -101,56 +111,76 @@
         d_hidden = (back * slope).astype(BF)
         out_part += jnp.concatenate([dot(hidden, v_a), dot(hidden, v_b)], axis=1)
         inner_part += dot(d_hidden, w, 1, 1)
-        hidden_ref[:, k * UNITS : (k + 1) * UNITS] = hidden
-        d_hidden_ref[:, k * UNITS : (k + 1) * UNITS] = d_hidden
+        keep(hidden, HID + k * UNITS, 2 + 2 * k)
+        keep(d_hidden, DHID + k * UNITS, 3 + 2 * k)
     d_logit = jnp.sum(d_routed * out_part, axis=1, keepdims=True) * gating * (1.0 - gating)
     centroid_grad = before_ref[...] + jnp.sum(d_logit * routed, axis=0, keepdims=True)
     centroid_grad_ref[...] = centroid_grad
     layer_part = (gating * out_part).astype(BF)
     grad_part = (inner_part + d_logit * centroid).astype(BF)
     token_place, grad_place = mixed_picks(ROWS, False)
-    mixed_ref[:MIXED, :] = (dot(token_place, layer_part) + dot(grad_place, grad_part)).astype(BF)
+    mixed_ref[...] = (dot(token_place, layer_part) + dot(grad_place, grad_part)).astype(BF)
+    for copy in copies:
+        copy.wait()
+
+
+def join_kernel(own_ref, other_ref, here_ref, there_ref, out_ref, centroid_grad_ref):
+    out_ref[...] = (own_ref[...].astype(F32) + other_ref[...].astype(F32)).astype(BF)
+    centroid_grad_ref[...] = here_ref[...] + there_ref[...]
+
+
+def weight_grad_kernel(
+    kept_a_ref, kept_b_ref, here_ref, there_ref,
+    own_in, own_out, own_centroid, p1, p2, p3, kept_a, kept_b, sems,
+):
+    copies = [
+        pltpu.make_async_copy(kept_a_ref, kept_a, sems.at[0]),
+        pltpu.make_async_copy(kept_b_ref, kept_b, sems.at[1]),
+    ]
+    for copy in copies:
+        copy.start()
+    centroid_grad = here_ref[...] + there_ref[...]
+    own_centroid[...] = centroid_grad
     high = centroid_grad.astype(BF).astype(F32)
     row = iota((NOTE, D), 0)
-    note = jnp.where(row == 0, high, jnp.where(row == 1, centroid_grad - high, 0.0))
-    mixed_ref[MIXED:, :] = note.astype(BF)
-
-
-def join_kernel(own_ref, other_ref, own_centroid_ref, out_ref, centroid_grad_ref):
-    out_ref[...] = (own_ref[:MIXED, :].astype(F32) + other_ref[:MIXED, :].astype(F32)).astype(BF)
-    note = other_ref[MIXED:, :].astype(F32)
-    centroid_grad_ref[...] = own_centroid_ref[...] + note[0:1] + note[1:2]
-
-
-def weight_grad_kernel(
-    routed_a, d_expert_a, hidden_a, d_hidden_a, routed_b, d_expert_b, hidden_b, d_hidden_b,
-    after_ref, own_in, own_out, *sent,
-):
-    for k in range(X):
-        units = slice(k * UNITS, (k + 1) * UNITS)
-        first = dot(routed_a[...], d_hidden_a[:, units], 0, 0) + dot(
-            routed_b[...], d_hidden_b[:, units], 0, 0
-        )
-        second = dot(hidden_a[:, units], d_expert_a[...], 0, 0) + dot(
-            hidden_b[:, units], d_expert_b[...], 0, 0
-        )
-        if k == 0:
+    note = jnp.where(row == 0, high, jnp.where(row == 1, centroid_grad - high, 0.0)).astype(BF)
+    for copy in copies:
+        copy.wait()
+    for k, packed in enumerate((None, p1, p2, p3)):
+        units = slice(HID + k * UNITS, HID + (k + 1) * UNITS)
+        d_units = slice(DHID + k * UNITS, DHID + (k + 1) * UNITS)
+        first = dot(kept_a[:, ROUTED:DEXP], kept_a[:, d_units], 0, 0) + dot(
+            kept_b[:, ROUTED:DEXP], kept_b[:, d_units], 0, 0
+        )
+        second = dot(kept_a[:, units], kept_a[:, DEXP:KEPT], 0, 0) + dot(
+            kept_b[:, units], kept_b[:, DEXP:KEPT], 0, 0
+        )
+        if packed is None:
             own_in[...] = first
             own_out[...] = second
         else:
-            packed = sent[k - 1]
             packed[:D, :] = first.astype(BF)
             packed[D : D + UNITS, :] = second[:, :HALF].astype(BF)
-            packed[D + UNITS :, :] = second[:, HALF:].astype(BF)
-
-
-def total_kernel(own_in, own_out, p1, p2, p3, first_ref, second_ref):
+            packed[D + UNITS : PACKED, :] = second[:, HALF:].astype(BF)
+            packed[PACKED : PACKED + NOTE, :] = note[:, :HALF]
+            packed[PACKED + NOTE :, :] = note[:, HALF:]
+
+
+def total_kernel(
+    own_in, own_out, own_centroid, p1, p2, p3, first_ref, second_ref, centroid_grad_ref
+):
     def total(rows):
         return p1[rows, :].astype(F32) + p2[rows, :].astype(F32) + p3[rows, :].astype(F32)
+
+    def note(at):
+        rows = total(slice(at, at + NOTE))
+        return rows[0:1] + rows[1:2]
 
     first_ref[0] = own_in[...] + total(slice(0, D))
     second_ref[0, :, :HALF] = own_out[:, :HALF] + total(slice(D, D + UNITS))
     second_ref[0, :, HALF:] = own_out[:, HALF:] + total(slice(D + UNITS, PACKED))
+    centroid_grad_ref[:, :HALF] = own_centroid[:, :HALF] + note(PACKED)
+    centroid_grad_ref[:, HALF:] = own_centroid[:, HALF:] + note(PACKED + NOTE)
 
 
 def unpack_kernel(order_ref, home_ref, tok_ref, grad_ref, layer_ref, grad_out_ref):
@@ -177,7 +207,9 @@
 def call(kernel, outs, *operands, **options):
     return pl.pallas_call(
         kernel,
-        out_shape=[jax.ShapeDtypeStruct(*out) for out in outs],
+        out_shape=[
+            out if hasattr(out, "memory_space") else jax.ShapeDtypeStruct(*out) for out in outs
+        ],
         compiler_params=pltpu.CompilerParams(vmem_limit_bytes=VMEM_LIMIT),
         **options,
     )(*operands)
@@ -209,32 +241,41 @@
         packed.reshape(ZH * EXPERTS, 2 * BLK, D), ("zh", "y", "zl"), 0, 0, tiled=True
     ).reshape(MIXED, D)
     other_rows = shift(own_rows, "core", CORE, 1)
-    part_shapes = [
-        ((MIXED + NOTE, D), BF), ((1, D), F32), ((ROWS, D), BF), ((ROWS, D), BF),
-        ((ROWS, X * UNITS), BF), ((ROWS, X * UNITS), BF),
-    ]
+    options = dict(
+        in_specs=[vmem] * (3 + X),
+        out_specs=[vmem, vmem, hbm],
+        scratch_shapes=[pltpu.VMEM((ROWS, KEPT), BF), pltpu.SemaphoreType.DMA((2 + 2 * X,))],
+    )
+    outs = [((MIXED, D), BF), ((1, D), F32), pltpu.HBM((ROWS, KEPT), BF)]
     nothing = jnp.zeros((1, D), F32)
-    own = call(expert_kernel, part_shapes, own_rows, centroid, nothing, *shards)
-    other = call(expert_kernel, part_shapes, other_rows, centroid, own[1], *shards)
+    own = call(expert_kernel, outs, own_rows, centroid, nothing, *shards, **options)
+    other = call(expert_kernel, outs, other_rows, centroid, own[1], *shards, **options)
     from_other = shift(other[0], "core", CORE, 1)
-    returned, centroid_grad = call(
-        join_kernel, [((MIXED, D), BF), ((1, D), F32)], own[0], from_other, other[1]
+    returned, centroid_term = call(
+        join_kernel,
+        [((MIXED, D), BF), ((1, D), F32)],
+        own[0], from_other, other[1], shift(other[1], "zh", ZH, 1),
     )
     home = lax.all_to_all(
         returned.reshape(ZH * EXPERTS, 2 * BLK, D), ("zh", "y", "zl"), 0, 0, tiled=True
     ).reshape(MIXED, D)
     grads = call(
         weight_grad_kernel,
-        [((D, UNITS), F32), ((UNITS, D), F32)] + [((PACKED, UNITS), BF)] * (X - 1),
-        *own[2:], *other[2:], returned,
-        in_specs=[vmem] * 8 + [pl.BlockSpec(memory_space=pl.ANY)],
-    )
-    arrived = [shift(grads[1 + k], "x", X, k) for k in range(1, X)]
-    first_grad, second_grad = call(
-        total_kernel, [((1, D, UNITS), F32), ((1, UNITS, D), F32)], *grads[:2], *arrived
-    )
-    centroid_grad += shift(centroid_grad, "zh", ZH, 1)
-    grad_centroid = centroid_grad + sum(shift(centroid_grad, "x", X, k) for k in range(1, X))
+        [((D, UNITS), F32), ((UNITS, D), F32), ((1, D), F32)]
+        + [((PACKED + 2 * NOTE, UNITS), BF)] * (X - 1),
+        in_hbm(own[2]), in_hbm(other[2]), centroid_term, shift(centroid_term, "core", CORE, 1),
+        in_specs=[hbm, hbm, vmem, vmem],
+        scratch_shapes=[
+            pltpu.VMEM((ROWS, KEPT), BF), pltpu.VMEM((ROWS, KEPT), BF),
+            pltpu.SemaphoreType.DMA((2,)),
+        ],
+    )
+    arrived = [shift(grads[2 + k], "x", X, k) for k in range(1, X)]
+    first_grad, second_grad, grad_centroid = call(
+        total_kernel,
+        [((1, D, UNITS), F32), ((1, UNITS, D), F32), ((1, D), F32)],
+        *grads[:3], *arrived,
+    )
     layer_out, grad_tokens = call(
         unpack_kernel, [((TOK, D), BF), ((TOK, D), BF)], slot_order, home, tokens, out_grad
     )

time: 132 us -> 132 us (level)
  the two profiles are of different devices: /device:TPU:8 before, /device:TPU:6 now
where the time goes in v4:
time: 132 us; the launch traced here: 130 us
  starting transfers between devices  61.4 us (47%)
  waiting for transfers between devices  53.1 us (40%)
  Pallas kernels  14.3 us (11%)
    ppermute x10, starting transfers between devices, shift(): lax.ppermute(value, axis, [(i, (i + by) % size) for i in range(size)])  32.2 us
    ppermute x10, waiting for transfers between devices, shift(): lax.ppermute(value, axis, [(i, (i + by) % size) for i in range(size)])  29.7 us
    all_to_all x1, waiting for transfers between devices, on_device(): lax.all_to_all(packed.reshape(ZH * EXPERTS, 2 * BLK, D), ('zh', 'y', 'zl'...  23.4 us
    all_to_all x1, starting transfers between devices, on_device(): lax.all_to_all(packed.reshape(ZH * EXPERTS, 2 * BLK, D), ('zh', 'y', 'zl'...  18.7 us
    pallas_call x7, Pallas kernels, call(): pl.pallas_call(kernel, out_shape=[out if hasattr(out, 'memory_space') els...  14.3 us
    all_to_all x1, starting transfers between devices, on_device(): lax.all_to_all(returned.reshape(ZH * EXPERTS, 2 * BLK, D), ('zh', 'y', 'z...  10.5 us
  transfers between devices with their start and end apart: 12, of which 6 were waited for; matrix products, arithmetic and copies ran while one was open for 0% of the time, Pallas kernels for 6%

profile of v4, /device:TPU:6, one launch (start us, length us, event | category | flops | bytes accessed | tf_op | source)
XLA Modules:
  0.0 129.9 jit_solution(2374667013676955210)
XLA Ops:
  0.6 0.0 copy-start.4
  0.6 0.0 copy-start.5
  0.7 0.0 copy-start.2
  0.7 2.2 %shard_map.101 = bf16[512,512]{1,0:T(8,128)(2,1)} custom-call(s32[1,128]{1,0:T(1,128)} %order_ref.3, bf16[128,512]{1,0:T(8,128)(2,1)} %tok_ref.3, bf16[128,512]{1,0:T(8,128)(2,1)} %grad_ref.3), custom_call_target="tpu_custom_call" | custom-call | tf_op jit(solution)/shard_map/pallas_call | solution.py:208
  2.8 18.7 %all-to-all-start = ((bf16[64,8,512]{2,1,0:T(8,128)(2,1)}), bf16[64,8,512]{2,1,0:T(8,128)(2,1)S(1)}, u32[]{:S(2)}, u32[]{:S(2)}) async-start(bf16[64,8,512]{2,1,0:T(8,128)(2,1)} %bitcast), calls=%async_computation | async-start | bytes 1048576 | tf_op jit(solution)/shard_map/all_to_all | solution.py:240
  21.6 0.0 copy-done.4
  21.6 0.0 copy-done.5
  21.7 2.4 %collective-permute-start.2 = (bf16[1024,256]{1,0:T(8,128)(2,1)S(1)}, bf16[1024,256]{1,0:T(8,128)(2,1)S(1)}, u32[]{:S(2)}, u32[]{:S(2)}) collective-permute-start(bf16[1024,256]{1,0:T(8,128)(2,1)S(1)} %pad_maximum_fusion.s0), channel_id=1, source_target_pairs={{0,64},{64,128},{128,192},{192,0},{1,65},{65,129},{129,193},{193,1... | collective-permute-start | bytes 1572872 | tf_op jit(solution)/shard_map/ppermute | solution.py:219
  24.1 4.3 %collective-permute-start.1 = (bf16[1024,256]{1,0:T(8,128)(2,1)S(1)}, bf16[1024,256]{1,0:T(8,128)(2,1)S(1)}, u32[]{:S(2)}, u32[]{:S(2)}) collective-permute-start(bf16[1024,256]{1,0:T(8,128)(2,1)S(1)} %pad_maximum_fusion.s0), channel_id=1, source_target_pairs={{0,128},{64,192},{128,0},{192,64},{1,129},{65,193},{129,1},{193,65... | collective-permute-start | bytes 1572872 | tf_op jit(solution)/shard_map/ppermute | solution.py:219
  28.4 1.9 %collective-permute-start = (bf16[1024,256]{1,0:T(8,128)(2,1)S(1)}, bf16[1024,256]{1,0:T(8,128)(2,1)S(1)}, u32[]{:S(2)}, u32[]{:S(2)}) collective-permute-start(bf16[1024,256]{1,0:T(8,128)(2,1)S(1)} %pad_maximum_fusion.s0), channel_id=1, source_target_pairs={{0,192},{64,0},{128,64},{192,128},{1,193},{65,1},{129,65},{193,129... | collective-permute-start | bytes 1572872 | tf_op jit(solution)/shard_map/ppermute | solution.py:219
  30.3 23.4 %all-to-all-done = bf16[64,8,512]{2,1,0:T(8,128)(2,1)S(1)} async-done(((bf16[64,8,512]{2,1,0:T(8,128)(2,1)}), bf16[64,8,512]{2,1,0:T(8,128)(2,1)S(1)}, u32[]{:S(2)}, u32[]{:S(2)}) %all-to-all-start) | async-done | bytes 524320 | tf_op jit(solution)/shard_map/all_to_all | solution.py:240
  53.8 1.9 %collective-permute-start.3 = (bf16[512,512]{1,0:T(8,128)(2,1)S(1)}, bf16[512,512]{1,0:T(8,128)(2,1)S(1)}, u32[]{:S(2)}, u32[]{:S(2)}) collective-permute-start(bf16[512,512]{1,0:T(8,128)(2,1)S(1)} %bitcast.6), channel_id=1, source_target_pairs={{0,32},{32,0},{1,33},{33,1},{2,34},{34,2},{3,35},{35,3},{4,36},{36... | collective-permute-start | bytes 1572872 | tf_op jit(solution)/shard_map/ppermute | solution.py:219
  55.7 0.0 collective-permute-done.2.s3
  55.7 0.0 collective-permute-done.1.s2
  55.7 0.0 collective-permute-done.s1
  55.8 0.0 copy-done.2
  55.8 2.9 %shard_map.102 = (bf16[512,512]{1,0:T(8,128)(2,1)S(1)}, f32[1,512]{1,0:T(1,128)S(1)}, bf16[256,3072]{1,0:T(8,128)(2,1)}) custom-call(bf16[512,512]{1,0:T(8,128)(2,1)S(1)} %bitcast.7, bf16[1,512]{1,0:T(2,128)(2,1)S(1)} %copy-done.2, f32[1,512]{1,0:T(1,128)S(1)} %broadcast_in_dim.3.before_ref, bf16[1024,256]{1,0:T(8,128)(2,1)S(1)} %pad_maximum_fusion.s0, ...), custom_call_target="tpu_custom_call" | custom-call | tf_op jit(solution)/shard_map/pallas_call | solution.py:208
  58.7 0.0 collective-permute-done.3.rows_ref
  58.7 2.9 %shard_map.103 = (bf16[512,512]{1,0:T(8,128)(2,1)S(1)}, f32[1,512]{1,0:T(1,128)S(1)}, bf16[256,3072]{1,0:T(8,128)(2,1)}) custom-call(bf16[512,512]{1,0:T(8,128)(2,1)S(1)} %collective-permute-done.3.rows_ref, bf16[1,512]{1,0:T(2,128)(2,1)S(1)} %copy-done.2, f32[1,512]{1,0:T(1,128)S(1)} %get-tuple-element.25.before_ref, ...), custom_call_target="tpu_custom_call" | custom-call | tf_op jit(solution)/shard_map/pallas_call | solution.py:208
  61.6 2.4 %collective-permute-start.4 = (bf16[512,512]{1,0:T(8,128)(2,1)S(1)}, bf16[512,512]{1,0:T(8,128)(2,1)S(1)}, u32[]{:S(2)}, u32[]{:S(2)}) collective-permute-start(bf16[512,512]{1,0:T(8,128)(2,1)S(1)} %get-tuple-element.26), channel_id=1, source_target_pairs={{0,32},{32,0},{1,33},{33,1},{2,34},{34,2},{3,35},{35,3},{4,36},{36... | collective-permute-start | bytes 1572872 | tf_op jit(solution)/shard_map/ppermute | solution.py:219
  64.0 7.6 %collective-permute-start.5 = (f32[1,512]{1,0:T(1,128)S(1)}, f32[1,512]{1,0:T(1,128)S(1)}, u32[]{:S(2)}, u32[]{:S(2)}) collective-permute-start(f32[1,512]{1,0:T(1,128)S(1)} %get-tuple-element.27.here_ref), channel_id=1, source_target_pairs={{0,256},{256,0},{1,257},{257,1},{2,258},{258,2},{3,259},{259,3},{4... | collective-permute-start | bytes 6152 | tf_op jit(solution)/shard_map/ppermute | solution.py:219
  71.6 6.6 %collective-permute-done.5.there_ref = f32[1,512]{1,0:T(1,128)S(1)} collective-permute-done((f32[1,512]{1,0:T(1,128)S(1)}, f32[1,512]{1,0:T(1,128)S(1)}, u32[]{:S(2)}, u32[]{:S(2)}) %collective-permute-start.5) | collective-permute-done | bytes 2080 | tf_op jit(solution)/shard_map/ppermute | solution.py:219
  78.2 0.0 collective-permute-done.4.other_ref
  78.2 0.9 shard_map.104
  79.1 10.5 %all-to-all-start.1 = ((bf16[64,8,512]{2,1,0:T(8,128)(2,1)}), bf16[64,8,512]{2,1,0:T(8,128)(2,1)S(1)}, u32[]{:S(2)}, u32[]{:S(2)}) async-start(bf16[64,8,512]{2,1,0:T(8,128)(2,1)} %bitcast.4), calls=%async_computation.1 | async-start | bytes 1048576 | tf_op jit(solution)/shard_map/all_to_all | solution.py:259
  89.6 1.9 %collective-permute-start.6 = (f32[1,512]{1,0:T(1,128)S(1)}, f32[1,512]{1,0:T(1,128)S(1)}, u32[]{:S(2)}, u32[]{:S(2)}) collective-permute-start(f32[1,512]{1,0:T(1,128)S(1)} %get-tuple-element.33.here_ref), channel_id=1, source_target_pairs={{0,32},{32,0},{1,33},{33,1},{2,34},{34,2},{3,35},{35,3},{4,36},{36... | collective-permute-start | bytes 6152 | tf_op jit(solution)/shard_map/ppermute | solution.py:219
  91.5 1.1 collective-permute-done.6.there_ref
  92.6 3.2 %shard_map.106 = (f32[512,256]{1,0:T(8,128)S(1)}, f32[256,512]{1,0:T(8,128)S(1)}, f32[1,512]{1,0:T(1,128)S(1)}, bf16[1056,256]{1,0:T(8,128)(2,1)S(1)}, bf16[1056...) custom-call(bf16[256,3072]{1,0:T(8,128)(2,1)} %get-tuple-element.31.kept_a_ref, ...), custom_call_target="tpu_custom_call" | custom-call | tf_op jit(solution)/shard_map/pallas_call | solution.py:208
  95.9 0.0 copy-start
  95.9 0.0 copy-start.1
  95.9 0.0 copy-start.3
  95.9 2.6 %collective-permute-start.7 = (bf16[1056,256]{1,0:T(8,128)(2,1)S(1)}, bf16[1056,256]{1,0:T(8,128)(2,1)S(1)}, u32[]{:S(2)}, u32[]{:S(2)}) collective-permute-start(bf16[1056,256]{1,0:T(8,128)(2,1)S(1)} %get-tuple-element.37), channel_id=1, source_target_pairs={{0,64},{64,128},{128,192},{192,0},{1,65},{65,129},{129,193},{193,1... | collective-permute-start | bytes 1622024 | tf_op jit(solution)/shard_map/ppermute | solution.py:219
  98.6 4.3 %collective-permute-start.8 = (bf16[1056,256]{1,0:T(8,128)(2,1)S(1)}, bf16[1056,256]{1,0:T(8,128)(2,1)S(1)}, u32[]{:S(2)}, u32[]{:S(2)}) collective-permute-start(bf16[1056,256]{1,0:T(8,128)(2,1)S(1)} %get-tuple-element.38), channel_id=1, source_target_pairs={{0,128},{64,192},{128,0},{192,64},{1,129},{65,193},{129,1},{193,65... | collective-permute-start | bytes 1622024 | tf_op jit(solution)/shard_map/ppermute | solution.py:219
  102.9 2.7 %collective-permute-start.9 = (bf16[1056,256]{1,0:T(8,128)(2,1)S(1)}, bf16[1056,256]{1,0:T(8,128)(2,1)S(1)}, u32[]{:S(2)}, u32[]{:S(2)}) collective-permute-start(bf16[1056,256]{1,0:T(8,128)(2,1)S(1)} %get-tuple-element.39), channel_id=1, source_target_pairs={{0,192},{64,0},{128,64},{192,128},{1,193},{65,1},{129,65},{193,129... | collective-permute-start | bytes 1622024 | tf_op jit(solution)/shard_map/ppermute | solution.py:219
  105.7 7.4 %collective-permute-done.7.p1 = bf16[1056,256]{1,0:T(8,128)(2,1)S(1)} collective-permute-done((bf16[1056,256]{1,0:T(8,128)(2,1)S(1)}, bf16[1056,256]{1,0:T(8,128)(2,1)S(1)}, u32[]{:S(2)}, u32[]{:S(2)}) %collective-permute-start.7) | collective-permute-done | bytes 540704 | tf_op jit(solution)/shard_map/ppermute | solution.py:219
  113.1 4.1 %collective-permute-done.8.p2 = bf16[1056,256]{1,0:T(8,128)(2,1)S(1)} collective-permute-done((bf16[1056,256]{1,0:T(8,128)(2,1)S(1)}, bf16[1056,256]{1,0:T(8,128)(2,1)S(1)}, u32[]{:S(2)}, u32[]{:S(2)}) %collective-permute-start.8) | collective-permute-done | bytes 540704 | tf_op jit(solution)/shard_map/ppermute | solution.py:219
  117.2 10.5 %collective-permute-done.9.p3 = bf16[1056,256]{1,0:T(8,128)(2,1)S(1)} collective-permute-done((bf16[1056,256]{1,0:T(8,128)(2,1)S(1)}, bf16[1056,256]{1,0:T(8,128)(2,1)S(1)}, u32[]{:S(2)}, u32[]{:S(2)}) %collective-permute-start.9) | collective-permute-done | bytes 540704 | tf_op jit(solution)/shard_map/ppermute | solution.py:219
  127.6 1.1 shard_map.107
  128.8 0.0 all-to-all-done.1
  128.8 0.0 copy-done
  128.8 0.0 copy-done.1
  128.8 0.0 copy-done.3
  128.8 1.1 shard_map.105
  (3 shorter events, 0.1 us)
Async XLA Ops:
  0.6 21.0 %copy-start.4 = (bf16[1,256,512]{2,1,0:T(8,128)(2,1)S(1)}, bf16[1,256,512]{2,1,0:T(8,128)(2,1)}, u32[]{:S(2)}) copy-start(bf16[1,256,512]{2,1,0:T(8,128)(2,1)} %param.10) | copy-start | bytes 786436
  0.6 21.0 %copy-start.5 = (bf16[1,512,256]{2,1,0:T(8,128)(2,1)S(1)}, bf16[1,512,256]{2,1,0:T(8,128)(2,1)}, u32[]{:S(2)}) copy-start(bf16[1,512,256]{2,1,0:T(8,128)(2,1)} %param.9) | copy-start | bytes 786436
  0.7 55.1 %copy-start.2 = (bf16[1,512]{1,0:T(2,128)(2,1)S(1)}, bf16[1,512]{1,0:T(2,128)(2,1)}, u32[]{:S(2)}) copy-start(bf16[1,512]{1,0:T(2,128)(2,1)} %centroid_ref.3) | copy-start | bytes 3076
  2.8 50.9 %all-to-all-start = ((bf16[64,8,512]{2,1,0:T(8,128)(2,1)}), bf16[64,8,512]{2,1,0:T(8,128)(2,1)S(1)}, u32[]{:S(2)}, u32[]{:S(2)}) async-start(bf16[64,8,512]{2,1,0:T(8,128)(2,1)} %bitcast), calls=%async_computation | async-start | bytes 1048576 | tf_op jit(solution)/shard_map/all_to_all | solution.py:240
  21.7 34.0 %collective-permute-start.2 = (bf16[1024,256]{1,0:T(8,128)(2,1)S(1)}, bf16[1024,256]{1,0:T(8,128)(2,1)S(1)}, u32[]{:S(2)}, u32[]{:S(2)}) collective-permute-start(bf16[1024,256]{1,0:T(8,128)(2,1)S(1)} %pad_maximum_fusion.s0), channel_id=1, source_target_pairs={{0,64},{64,128},{128,192},{192,0},{1,65},{65,129},{129,193},{193,1... | collective-permute-start | bytes 1572872 | tf_op jit(solution)/shard_map/ppermute | solution.py:219
  24.1 31.6 %collective-permute-start.1 = (bf16[1024,256]{1,0:T(8,128)(2,1)S(1)}, bf16[1024,256]{1,0:T(8,128)(2,1)S(1)}, u32[]{:S(2)}, u32[]{:S(2)}) collective-permute-start(bf16[1024,256]{1,0:T(8,128)(2,1)S(1)} %pad_maximum_fusion.s0), channel_id=1, source_target_pairs={{0,128},{64,192},{128,0},{192,64},{1,129},{65,193},{129,1},{193,65... | collective-permute-start | bytes 1572872 | tf_op jit(solution)/shard_map/ppermute | solution.py:219
  28.4 27.3 %collective-permute-start = (bf16[1024,256]{1,0:T(8,128)(2,1)S(1)}, bf16[1024,256]{1,0:T(8,128)(2,1)S(1)}, u32[]{:S(2)}, u32[]{:S(2)}) collective-permute-start(bf16[1024,256]{1,0:T(8,128)(2,1)S(1)} %pad_maximum_fusion.s0), channel_id=1, source_target_pairs={{0,192},{64,0},{128,64},{192,128},{1,193},{65,1},{129,65},{193,129... | collective-permute-start | bytes 1572872 | tf_op jit(solution)/shard_map/ppermute | solution.py:219
  53.8 4.9 %collective-permute-start.3 = (bf16[512,512]{1,0:T(8,128)(2,1)S(1)}, bf16[512,512]{1,0:T(8,128)(2,1)S(1)}, u32[]{:S(2)}, u32[]{:S(2)}) collective-permute-start(bf16[512,512]{1,0:T(8,128)(2,1)S(1)} %bitcast.6), channel_id=1, source_target_pairs={{0,32},{32,0},{1,33},{33,1},{2,34},{34,2},{3,35},{35,3},{4,36},{36... | collective-permute-start | bytes 1572872 | tf_op jit(solution)/shard_map/ppermute | solution.py:219
  61.6 16.6 %collective-permute-start.4 = (bf16[512,512]{1,0:T(8,128)(2,1)S(1)}, bf16[512,512]{1,0:T(8,128)(2,1)S(1)}, u32[]{:S(2)}, u32[]{:S(2)}) collective-permute-start(bf16[512,512]{1,0:T(8,128)(2,1)S(1)} %get-tuple-element.26), channel_id=1, source_target_pairs={{0,32},{32,0},{1,33},{33,1},{2,34},{34,2},{3,35},{35,3},{4,36},{36... | collective-permute-start | bytes 1572872 | tf_op jit(solution)/shard_map/ppermute | solution.py:219
  64.0 14.2 %collective-permute-start.5 = (f32[1,512]{1,0:T(1,128)S(1)}, f32[1,512]{1,0:T(1,128)S(1)}, u32[]{:S(2)}, u32[]{:S(2)}) collective-permute-start(f32[1,512]{1,0:T(1,128)S(1)} %get-tuple-element.27.here_ref), channel_id=1, source_target_pairs={{0,256},{256,0},{1,257},{257,1},{2,258},{258,2},{3,259},{259,3},{4... | collective-permute-start | bytes 6152 | tf_op jit(solution)/shard_map/ppermute | solution.py:219
  79.1 49.7 %all-to-all-start.1 = ((bf16[64,8,512]{2,1,0:T(8,128)(2,1)}), bf16[64,8,512]{2,1,0:T(8,128)(2,1)S(1)}, u32[]{:S(2)}, u32[]{:S(2)}) async-start(bf16[64,8,512]{2,1,0:T(8,128)(2,1)} %bitcast.4), calls=%async_computation.1 | async-start | bytes 1048576 | tf_op jit(solution)/shard_map/all_to_all | solution.py:259
  89.6 3.1 %collective-permute-start.6 = (f32[1,512]{1,0:T(1,128)S(1)}, f32[1,512]{1,0:T(1,128)S(1)}, u32[]{:S(2)}, u32[]{:S(2)}) collective-permute-start(f32[1,512]{1,0:T(1,128)S(1)} %get-tuple-element.33.here_ref), channel_id=1, source_target_pairs={{0,32},{32,0},{1,33},{33,1},{2,34},{34,2},{3,35},{35,3},{4,36},{36... | collective-permute-start | bytes 6152 | tf_op jit(solution)/shard_map/ppermute | solution.py:219
  95.9 32.9 %copy-start = (bf16[128,512]{1,0:T(8,128)(2,1)S(1)}, bf16[128,512]{1,0:T(8,128)(2,1)}, u32[]{:S(2)}) copy-start(bf16[128,512]{1,0:T(8,128)(2,1)} %tok_ref.3) | copy-start | bytes 393220
  95.9 32.9 %copy-start.1 = (bf16[128,512]{1,0:T(8,128)(2,1)S(1)}, bf16[128,512]{1,0:T(8,128)(2,1)}, u32[]{:S(2)}) copy-start(bf16[128,512]{1,0:T(8,128)(2,1)} %grad_ref.3) | copy-start | bytes 393220
  95.9 32.9 %copy-start.3 = (s32[1,128]{1,0:T(1,128)S(1)}, s32[1,128]{1,0:T(1,128)}, u32[]{:S(2)}) copy-start(s32[1,128]{1,0:T(1,128)} %order_ref.3) | copy-start | bytes 1540
  95.9 17.1 %collective-permute-start.7 = (bf16[1056,256]{1,0:T(8,128)(2,1)S(1)}, bf16[1056,256]{1,0:T(8,128)(2,1)S(1)}, u32[]{:S(2)}, u32[]{:S(2)}) collective-permute-start(bf16[1056,256]{1,0:T(8,128)(2,1)S(1)} %get-tuple-element.37), channel_id=1, source_target_pairs={{0,64},{64,128},{128,192},{192,0},{1,65},{65,129},{129,193},{193,1... | collective-permute-start | bytes 1622024 | tf_op jit(solution)/shard_map/ppermute | solution.py:219
  98.6 18.6 %collective-permute-start.8 = (bf16[1056,256]{1,0:T(8,128)(2,1)S(1)}, bf16[1056,256]{1,0:T(8,128)(2,1)S(1)}, u32[]{:S(2)}, u32[]{:S(2)}) collective-permute-start(bf16[1056,256]{1,0:T(8,128)(2,1)S(1)} %get-tuple-element.38), channel_id=1, source_target_pairs={{0,128},{64,192},{128,0},{192,64},{1,129},{65,193},{129,1},{193,65... | collective-permute-start | bytes 1622024 | tf_op jit(solution)/shard_map/ppermute | solution.py:219
  102.9 24.7 %collective-permute-start.9 = (bf16[1056,256]{1,0:T(8,128)(2,1)S(1)}, bf16[1056,256]{1,0:T(8,128)(2,1)S(1)}, u32[]{:S(2)}, u32[]{:S(2)}) collective-permute-start(bf16[1056,256]{1,0:T(8,128)(2,1)S(1)} %get-tuple-element.39), channel_id=1, source_target_pairs={{0,192},{64,0},{128,64},{192,128},{1,193},{65,1},{129,65},{193,129... | collective-permute-start | bytes 1622024 | tf_op jit(solution)/shard_map/ppermute | solution.py:219

commit v5 on v2

--- a/solution.py
+++ b/solution.py
@@ -42,7 +42,7 @@
 
 def pack_kernel(
     order_ref, tok_ref, grad_ref, first_ref, second_ref,
-    out_ref, shard_ref, order_vmem, tok_vmem, grad_vmem, sems,
+    out_ref, shard_ref, order_vmem, tok_vmem, grad_vmem, shard_vmem, sems,
 ):
     copies = [
         pltpu.make_async_copy(source, target, sems.at[i])
@@ -51,14 +51,18 @@
                 (order_ref, order_vmem),
                 (tok_ref, tok_vmem),
                 (grad_ref, grad_vmem),
-                (first_ref.at[0], shard_ref.at[:D, :]),
-                (second_ref.at[0, :, :HALF], shard_ref.at[D : D + UNITS, :]),
-                (second_ref.at[0, :, HALF:], shard_ref.at[D + UNITS :, :]),
+                (first_ref.at[0], shard_vmem.at[:D, :]),
+                (second_ref.at[0, :, :HALF], shard_vmem.at[D : D + UNITS, :]),
+                (second_ref.at[0, :, HALF:], shard_vmem.at[D + UNITS :, :]),
             )
         )
     ]
     for copy in copies:
         copy.start()
+    for copy in copies[3:]:
+        copy.wait()
+    shard_out = pltpu.make_async_copy(shard_vmem, shard_ref, sems.at[6])
+    shard_out.start()
     token_pick, grad_pick = mixed_picks(TOK, True)
     copies[0].wait()
     order = jnp.broadcast_to(order_vmem[...].astype(F32), (8, TOK)).astype(BF)
@@ -74,15 +78,16 @@
     mixed = (mixed + dot(pick_grad, grad_vmem[...], 0, 0)).astype(BF)
     for half in range(ZH):
         out_ref[half * 2 * TOK : (half + 1) * 2 * TOK, :] = mixed
-    for copy in copies[3:]:
-        copy.wait()
+    shard_out.wait()
 
 
 def expert_kernel(
     rows_ref, centroid_ref, shards_ref,
     mixed_ref, centroid_grad_ref, routed_ref, d_expert_ref, hidden_ref, d_hidden_ref,
-    shards_vmem, sems,
+    shards_vmem, centroid_vmem, sems,
 ):
+    centroid_copy = pltpu.make_async_copy(centroid_ref, centroid_vmem, sems.at[SHARDS])
+    centroid_copy.start()
     copies = [
         pltpu.make_async_copy(
             shards_ref.at[k * PACKED : (k + 1) * PACKED, :], shards_vmem.at[k], sems.at[k]
@@ -95,7 +100,8 @@
     received = rows_ref[...]
     routed = dot(token_pick, received)
     d_routed = dot(grad_pick, received)
-    centroid = centroid_ref[...].astype(F32)
+    centroid_copy.wait()
+    centroid = centroid_vmem[...].astype(F32)
     gating = jax.nn.sigmoid(jnp.sum(routed * centroid, axis=1, keepdims=True))
     routed_half = routed.astype(BF)
     d_expert = (gating * d_routed).astype(BF)
@@ -152,7 +158,10 @@
         copy.wait()
 
 
-def spread_kernel(packed_ref, first_ref, second_ref):
+def spread_kernel(grads_ref, first_ref, second_ref, packed_ref, sem):
+    copy = pltpu.make_async_copy(grads_ref, packed_ref, sem)
+    copy.start()
+    copy.wait()
     first_ref[0] = packed_ref[:D, :].astype(F32)
     second_ref[0, :, :HALF] = packed_ref[D : D + UNITS, :].astype(F32)
     second_ref[0, :, HALF:] = packed_ref[D + UNITS :, :].astype(F32)
@@ -194,6 +203,10 @@
     )(*operands)
 
 
+def shift(value, axis, size, by):
+    return lax.ppermute(value, axis, [(i, (i + by) % size) for i in range(size)])
+
+
 def on_device(tokens, slot_order, centroid, weight_in, weight_out, out_grad):
     vmem, hbm = pl.BlockSpec(memory_space=pltpu.VMEM), pl.BlockSpec(memory_space=pltpu.HBM)
     packed, shard = call(
@@ -206,7 +219,8 @@
             pltpu.VMEM((1, TOK), jnp.int32),
             pltpu.VMEM((TOK, D), BF),
             pltpu.VMEM((TOK, D), BF),
-            pltpu.SemaphoreType.DMA((6,)),
+            pltpu.VMEM((PACKED, UNITS), BF),
+            pltpu.SemaphoreType.DMA((7,)),
         ],
     )
     shards = lax.all_gather(shard, ("x", "core"), axis=0, tiled=True)
@@ -219,11 +233,13 @@
             ((MIXED, D), BF), ((1, D), F32), ((ROWS, D), BF), ((ROWS, D), BF),
             ((ROWS, SHARDS * UNITS), BF), ((ROWS, SHARDS * UNITS), BF),
         ],
-        rows, centroid, in_hbm(shards),
-        in_specs=[vmem, vmem, hbm],
+        rows, in_hbm(centroid), in_hbm(shards),
+        in_specs=[vmem, hbm, hbm],
         out_specs=[vmem] * 6,
         scratch_shapes=[
-            pltpu.VMEM((SHARDS, PACKED, UNITS), BF), pltpu.SemaphoreType.DMA((SHARDS,)),
+            pltpu.VMEM((SHARDS, PACKED, UNITS), BF),
+            pltpu.VMEM((1, D), BF),
+            pltpu.SemaphoreType.DMA((SHARDS + 1,)),
         ],
     )
     home = lax.all_to_all(
@@ -241,10 +257,16 @@
     )
     grads = lax.psum_scatter(packed_grads, ("x", "core"), scatter_dimension=0, tiled=True)
     first_grad, second_grad = call(
-        spread_kernel, [((1, D, UNITS), F32), ((1, UNITS, D), F32)], grads
-    )
-    centroid_terms = lax.all_gather(centroid_term, ("zh", "x", "core"), axis=0, tiled=True)
-    grad_centroid = jnp.sum(centroid_terms, axis=0, keepdims=True)
+        spread_kernel,
+        [((1, D, UNITS), F32), ((1, UNITS, D), F32)],
+        in_hbm(grads),
+        in_specs=[hbm],
+        out_specs=[vmem, vmem],
+        scratch_shapes=[pltpu.VMEM((PACKED, UNITS), BF), pltpu.SemaphoreType.DMA(())],
+    )
+    centroid_term += shift(centroid_term, "zh", ZH, 1)
+    centroid_term += shift(centroid_term, "core", CORE, 1)
+    grad_centroid = centroid_term + sum(shift(centroid_term, "x", X, k) for k in range(1, X))
     layer_out, grad_tokens = call(
         unpack_kernel, [((TOK, D), BF), ((TOK, D), BF)], slot_order, home, tokens, out_grad
     )

time: 159 us -> 140 us (0.88)
  blocking collectives: 104 us -> 50.7 us
  starting transfers between devices: 7.57 us -> 33.8 us
  waiting for transfers between devices: 0.04 us -> 23.9 us
  Pallas kernels: 28.1 us -> 14.1 us
  local copies, waits for them, and re-layouts: 1.74 us -> 0.02 us
    all_gather x1 -> x0, blocking collectives: 53 us -> none  [on_device(): lax.all_gather(centroid_term, ('zh', 'x', 'core'), axis=0, tiled=True)]
    ppermute x0 -> x5, starting transfers between devices: none -> 24.9 us  [shift(): lax.ppermute(value, axis, [(i, (i + by) % size) for i in range(size)])]
    ppermute x0 -> x5, waiting for transfers between devices: none -> 23.9 us  [shift(): lax.ppermute(value, axis, [(i, (i + by) % size) for i in range(size)])]
    pallas_call x5, Pallas kernels: 28.1 us -> 14.1 us  [call(): pl.pallas_call(kernel, out_shape=[out if hasattr(out, 'memory_space') els...]
    unnamed x10 -> x6, local copies, waits for them, and re-layouts: 1.74 us -> 0.02 us
  transfers between devices with their start and end apart: 3 -> 8, of which waited for: 0 -> 3; matrix products, arithmetic and copies ran while one was open for 0% -> 0% of each run, Pallas kernels for 1% -> 1%
where the time goes in v5:
time: 140 us; the launch traced here: 137 us
  blocking collectives  50.7 us (36%)
  starting transfers between devices  33.8 us (24%)
  waiting for transfers between devices  23.9 us (17%)
  between operations  14.2 us (10%)
  Pallas kernels  14.1 us (10%)
    all_to_all x1, blocking collectives, on_device(): lax.all_to_all(packed.reshape(ZH * EXPERTS, 2 * BLK, D), ('zh', 'y', 'zl'...  50.7 us
    ppermute x5, starting transfers between devices, shift(): lax.ppermute(value, axis, [(i, (i + by) % size) for i in range(size)])  24.9 us
    ppermute x5, waiting for transfers between devices, shift(): lax.ppermute(value, axis, [(i, (i + by) % size) for i in range(size)])  23.9 us
    pallas_call x5, Pallas kernels, call(): pl.pallas_call(kernel, out_shape=[out if hasattr(out, 'memory_space') els...  14.1 us
    all_to_all x1, starting transfers between devices, on_device(): lax.all_to_all(mixed.reshape(ZH * EXPERTS, 2 * BLK, D), ('zh', 'y', 'zl')...  8.83 us
  transfers between devices with their start and end apart: 8, of which 3 were waited for; matrix products, arithmetic and copies ran while one was open for 0% of the time, Pallas kernels for 1%

profile of v5, /device:TPU:6, one launch (start us, length us, event | category | flops | bytes accessed | tf_op | source)
XLA Modules:
  0.0 137.3 jit_solution(8174727819305969543)
XLA Ops:
  7.2 0.0 all-gather.2.cloned.1.call-start
  7.2 2.0 %shard_map.101 = (bf16[512,512]{1,0:T(8,128)(2,1)S(1)}, bf16[1024,256]{1,0:T(8,128)(2,1)}) custom-call(s32[1,128]{1,0:T(1,128)} %order_ref.3, bf16[128,512]{1,0:T(8,128)(2,1)} %tok_ref.3, bf16[128,512]{1,0:T(8,128)(2,1)} %grad_ref.3, bf16[1,512,256]{2,1,0:T(8,128)(2,1)} %first_ref.1, bf16[1,256,512]{2,1,0:T(8,128)(2,1)} %second_ref.1), custom_call_target="tpu_custom_call" | custom-call | tf_op jit(solution)/shard_map/pallas_call | solution.py:196
  9.2 0.0 all-gather.2.cloned.1.call-update
  9.3 0.0 reduce-scatter.2.cloned.1.call-start
  9.3 50.7 %all_to_all.10 = bf16[64,8,512]{2,1,0:T(8,128)(2,1)S(1)} all-to-all(bf16[64,8,512]{2,1,0:T(8,128)(2,1)S(1)} %bitcast.6), channel_id=1, replica_groups=mesh['zh'=2,'x'=4,'core'=2,'y'=4,'zl'=8] {'zh','y','zl'}, dimensions={0} | all-to-all | bytes 1048576 | tf_op jit(solution)/shard_map/all_to_all | solution.py:227
  60.0 0.0 all-gather.2.cloned.1.call-done.shards_ref
  60.0 6.5 %shard_map.102 = (bf16[512,512]{1,0:T(8,128)(2,1)}, f32[1,512]{1,0:T(1,128)S(1)}, bf16[256,512]{1,0:T(8,128)(2,1)S(1)}, bf16[256,512]{1,0:T(8,128)(2,1)S(1)}, bf...) custom-call(bf16[512,512]{1,0:T(8,128)(2,1)S(1)} %bitcast.4, bf16[1,512]{1,0:T(2,128)(2,1)} %centroid_ref.1, ...), custom_call_target="tpu_custom_call" | custom-call | tf_op jit(solution)/shard_map/pallas_call | solution.py:196
  66.6 2.4 %shard_map.104 = bf16[8192,256]{1,0:T(8,128)(2,1)} custom-call(bf16[256,512]{1,0:T(8,128)(2,1)S(1)} %get-tuple-element.23.routed_ref, bf16[256,512]{1,0:T(8,128)(2,1)S(1)} %get-tuple-element.24.d_expert_ref, bf16[256,2048]{1,0:T(8,128)(2,1)S(1)} %get-tuple-element.25.hidden_ref, bf16[256,2048]{1,0:T(8,128)(2,1)S(1)} %get-tuple-element.26.d_hidden_ref), custom_call_target="tpu_custom_call" | custom-call | tf_op jit(solution)/shard_map/pallas_call | solution.py:196
  69.0 0.0 copy-start
  69.0 0.0 copy-start.1
  69.0 0.0 copy-start.2
  69.0 0.0 reduce-scatter.2.cloned.1.call-update
  69.0 8.8 %all-to-all-start.1 = ((bf16[64,8,512]{2,1,0:T(8,128)(2,1)}), bf16[64,8,512]{2,1,0:T(8,128)(2,1)S(1)}, u32[]{:S(2)}, u32[]{:S(2)}) async-start(bf16[64,8,512]{2,1,0:T(8,128)(2,1)} %bitcast.2), calls=%async_computation.1 | async-start | bytes 1048576 | tf_op jit(solution)/shard_map/all_to_all | solution.py:245
  77.9 12.3 %collective-permute-start = (f32[1,512]{1,0:T(1,128)S(1)}, f32[1,512]{1,0:T(1,128)S(1)}, u32[]{:S(2)}, u32[]{:S(2)}) collective-permute-start(f32[1,512]{1,0:T(1,128)S(1)} %get-tuple-element.22), channel_id=1, source_target_pairs={{0,256},{256,0},{1,257},{257,1},{2,258},{258,2},{3,259},{259,3},{4... | collective-permute-start | bytes 6152 | tf_op jit(solution)/shard_map/ppermute | solution.py:207
  90.2 20.3 %collective-permute-done = f32[1,512]{1,0:T(1,128)S(1)} collective-permute-done((f32[1,512]{1,0:T(1,128)S(1)}, f32[1,512]{1,0:T(1,128)S(1)}, u32[]{:S(2)}, u32[]{:S(2)}) %collective-permute-start) | collective-permute-done | bytes 2080 | tf_op jit(solution)/shard_map/ppermute | solution.py:207
  110.5 1.9 %collective-permute-start.1 = (f32[1,512]{1,0:T(1,128)S(1)}, f32[1,512]{1,0:T(1,128)S(1)}, u32[]{:S(2)}, u32[]{:S(2)}) collective-permute-start(f32[1,512]{1,0:T(1,128)S(1)} %add.17), channel_id=1, source_target_pairs={{0,32},{32,0},{1,33},{33,1},{2,34},{34,2},{3,35},{35,3},{4,36},{36... | collective-permute-start | bytes 6152 | tf_op jit(solution)/shard_map/ppermute | solution.py:207
  112.4 1.1 collective-permute-done.1
  113.6 3.3 %collective-permute-start.4 = (f32[1,512]{1,0:T(1,128)S(1)}, f32[1,512]{1,0:T(1,128)S(1)}, u32[]{:S(2)}, u32[]{:S(2)}) collective-permute-start(f32[1,512]{1,0:T(1,128)S(1)} %add.18), channel_id=1, source_target_pairs={{0,192},{64,0},{128,64},{192,128},{1,193},{65,1},{129,65},{193,129... | collective-permute-start | bytes 6152 | tf_op jit(solution)/shard_map/ppermute | solution.py:207
  116.9 4.3 %collective-permute-start.3 = (f32[1,512]{1,0:T(1,128)S(1)}, f32[1,512]{1,0:T(1,128)S(1)}, u32[]{:S(2)}, u32[]{:S(2)}) collective-permute-start(f32[1,512]{1,0:T(1,128)S(1)} %add.18), channel_id=1, source_target_pairs={{0,128},{64,192},{128,0},{192,64},{1,129},{65,193},{129,1},{193,65... | collective-permute-start | bytes 6152 | tf_op jit(solution)/shard_map/ppermute | solution.py:207
  121.2 3.0 %collective-permute-start.2 = (f32[1,512]{1,0:T(1,128)S(1)}, f32[1,512]{1,0:T(1,128)S(1)}, u32[]{:S(2)}, u32[]{:S(2)}) collective-permute-start(f32[1,512]{1,0:T(1,128)S(1)} %add.18), channel_id=1, source_target_pairs={{0,64},{64,128},{128,192},{192,0},{1,65},{65,129},{129,193},{193,1... | collective-permute-start | bytes 6152 | tf_op jit(solution)/shard_map/ppermute | solution.py:207
  124.3 0.0 collective-permute-done.4
  124.3 0.0 collective-permute-done.3
  124.3 2.4 %collective-permute-done.2 = f32[1,512]{1,0:T(1,128)S(1)} collective-permute-done((f32[1,512]{1,0:T(1,128)S(1)}, f32[1,512]{1,0:T(1,128)S(1)}, u32[]{:S(2)}, u32[]{:S(2)}) %collective-permute-start.2) | collective-permute-done | bytes 2080 | tf_op jit(solution)/shard_map/ppermute | solution.py:207
  126.7 0.6 add_add_fusion
  127.3 0.0 all-to-all-done.1
  127.3 0.0 copy-done
  127.3 0.0 copy-done.1
  127.3 0.0 copy-done.2
  127.3 1.1 shard_map.103
  128.4 0.0 reduce-scatter.2.cloned.1.call-done.grads_ref
  128.4 2.0 %shard_map.105 = (f32[1,512,256]{2,1,0:T(8,128)}, f32[1,256,512]{2,1,0:T(8,128)}) custom-call(bf16[1024,256]{1,0:T(8,128)(2,1)} %reduce-scatter.2.cloned.1.call-done.grads_ref), custom_call_target="tpu_custom_call" | custom-call | tf_op jit(solution)/shard_map/pallas_call | solution.py:196
  (2 shorter events, 0.0 us)
Async XLA Ops:
  7.2 52.9 %all-gather.2.cloned.1.call-start = ((), (), s32[]{:S(2)}) async-start(), calls=%async_computation.3 | async-start | bytes 4718592 | tf_op jit(solution)/shard_map/all_gather | solution.py:226
  9.3 119.1 %reduce-scatter.2.cloned.1.call-start = ((), (), s32[]{:S(2)}) async-start(), calls=%async_computation.4 | async-start | bytes 4718592 | tf_op jit(solution)/shard_map/reduce_scatter | solution.py:258
  69.0 58.3 %copy-start = (bf16[128,512]{1,0:T(8,128)(2,1)S(1)}, bf16[128,512]{1,0:T(8,128)(2,1)}, u32[]{:S(2)}) copy-start(bf16[128,512]{1,0:T(8,128)(2,1)} %tok_ref.3) | copy-start | bytes 393220
  69.0 58.3 %copy-start.1 = (bf16[128,512]{1,0:T(8,128)(2,1)S(1)}, bf16[128,512]{1,0:T(8,128)(2,1)}, u32[]{:S(2)}) copy-start(bf16[128,512]{1,0:T(8,128)(2,1)} %grad_ref.3) | copy-start | bytes 393220
  69.0 58.3 %copy-start.2 = (s32[1,128]{1,0:T(1,128)S(1)}, s32[1,128]{1,0:T(1,128)}, u32[]{:S(2)}) copy-start(s32[1,128]{1,0:T(1,128)} %order_ref.3) | copy-start | bytes 1540
  69.0 58.3 %all-to-all-start.1 = ((bf16[64,8,512]{2,1,0:T(8,128)(2,1)}), bf16[64,8,512]{2,1,0:T(8,128)(2,1)S(1)}, u32[]{:S(2)}, u32[]{:S(2)}) async-start(bf16[64,8,512]{2,1,0:T(8,128)(2,1)} %bitcast.2), calls=%async_computation.1 | async-start | bytes 1048576 | tf_op jit(solution)/shard_map/all_to_all | solution.py:245
  77.9 32.6 %collective-permute-start = (f32[1,512]{1,0:T(1,128)S(1)}, f32[1,512]{1,0:T(1,128)S(1)}, u32[]{:S(2)}, u32[]{:S(2)}) collective-permute-start(f32[1,512]{1,0:T(1,128)S(1)} %get-tuple-element.22), channel_id=1, source_target_pairs={{0,256},{256,0},{1,257},{257,1},{2,258},{258,2},{3,259},{259,3},{4... | collective-permute-start | bytes 6152 | tf_op jit(solution)/shard_map/ppermute | solution.py:207
  110.5 3.0 %collective-permute-start.1 = (f32[1,512]{1,0:T(1,128)S(1)}, f32[1,512]{1,0:T(1,128)S(1)}, u32[]{:S(2)}, u32[]{:S(2)}) collective-permute-start(f32[1,512]{1,0:T(1,128)S(1)} %add.17), channel_id=1, source_target_pairs={{0,32},{32,0},{1,33},{33,1},{2,34},{34,2},{3,35},{35,3},{4,36},{36... | collective-permute-start | bytes 6152 | tf_op jit(solution)/shard_map/ppermute | solution.py:207
  113.6 10.7 %collective-permute-start.4 = (f32[1,512]{1,0:T(1,128)S(1)}, f32[1,512]{1,0:T(1,128)S(1)}, u32[]{:S(2)}, u32[]{:S(2)}) collective-permute-start(f32[1,512]{1,0:T(1,128)S(1)} %add.18), channel_id=1, source_target_pairs={{0,192},{64,0},{128,64},{192,128},{1,193},{65,1},{129,65},{193,129... | collective-permute-start | bytes 6152 | tf_op jit(solution)/shard_map/ppermute | solution.py:207
  116.9 7.4 %collective-permute-start.3 = (f32[1,512]{1,0:T(1,128)S(1)}, f32[1,512]{1,0:T(1,128)S(1)}, u32[]{:S(2)}, u32[]{:S(2)}) collective-permute-start(f32[1,512]{1,0:T(1,128)S(1)} %add.18), channel_id=1, source_target_pairs={{0,128},{64,192},{128,0},{192,64},{1,129},{65,193},{129,1},{193,65... | collective-permute-start | bytes 6152 | tf_op jit(solution)/shard_map/ppermute | solution.py:207
  121.2 5.5 %collective-permute-start.2 = (f32[1,512]{1,0:T(1,128)S(1)}, f32[1,512]{1,0:T(1,128)S(1)}, u32[]{:S(2)}, u32[]{:S(2)}) collective-permute-start(f32[1,512]{1,0:T(1,128)S(1)} %add.18), channel_id=1, source_target_pairs={{0,64},{64,128},{128,192},{192,0},{1,65},{65,129},{129,193},{193,1... | collective-permute-start | bytes 6152 | tf_op jit(solution)/shard_map/ppermute | solution.py:207
Sparse Core Ops, SparseCore 0:
  10.7 42.3 all-gather.1
  69.2 37.4 reduce-scatter.1

commit v6 on v3

--- a/solution.py
+++ b/solution.py
@@ -109,24 +109,26 @@
     layer_part = (gating * out_part).astype(BF)
     grad_part = (inner_part + d_logit * centroid).astype(BF)
     token_place, grad_place = mixed_picks(ROWS, False)
-    mixed_ref[:MIXED, :] = (dot(token_place, layer_part) + dot(grad_place, grad_part)).astype(BF)
-    high = centroid_grad.astype(BF).astype(F32)
+    mixed_ref[...] = (dot(token_place, layer_part) + dot(grad_place, grad_part)).astype(BF)
+
+
+def join_kernel(own_ref, other_ref, out_ref):
+    out_ref[...] = (own_ref[...].astype(F32) + other_ref[...].astype(F32)).astype(BF)
+
+
+def weight_grad_kernel(
+    centroid_ref, routed_a, d_expert_a, hidden_a, d_hidden_a,
+    routed_b, d_expert_b, hidden_b, d_hidden_b, after_ref, own_in_ref, own_out_ref, p1, p2, p3,
+    own_in, own_out, sems,
+):
+    high = centroid_ref[...].astype(BF).astype(F32)
     row = iota((NOTE, D), 0)
-    note = jnp.where(row == 0, high, jnp.where(row == 1, centroid_grad - high, 0.0))
-    mixed_ref[MIXED:, :] = note.astype(BF)
-
-
-def join_kernel(own_ref, other_ref, own_centroid_ref, out_ref, centroid_grad_ref):
-    out_ref[...] = (own_ref[:MIXED, :].astype(F32) + other_ref[:MIXED, :].astype(F32)).astype(BF)
-    note = other_ref[MIXED:, :].astype(F32)
-    centroid_grad_ref[...] = own_centroid_ref[...] + note[0:1] + note[1:2]
-
-
-def weight_grad_kernel(
-    routed_a, d_expert_a, hidden_a, d_hidden_a, routed_b, d_expert_b, hidden_b, d_hidden_b,
-    after_ref, own_in, own_out, *sent,
-):
-    for k in range(X):
+    note = jnp.where(row == 0, high, jnp.where(row == 1, centroid_ref[...] - high, 0.0)).astype(BF)
+    copies = [
+        pltpu.make_async_copy(own_in, own_in_ref, sems.at[0]),
+        pltpu.make_async_copy(own_out, own_out_ref, sems.at[1]),
+    ]
+    for k, packed in enumerate((None, p1, p2, p3)):
         units = slice(k * UNITS, (k + 1) * UNITS)
         first = dot(routed_a[...], d_hidden_a[:, units], 0, 0) + dot(
             routed_b[...], d_hidden_b[:, units], 0, 0
@@ -134,21 +136,43 @@
         second = dot(hidden_a[:, units], d_expert_a[...], 0, 0) + dot(
             hidden_b[:, units], d_expert_b[...], 0, 0
         )
-        if k == 0:
+        if packed is None:
             own_in[...] = first
             own_out[...] = second
+            for copy in copies:
+                copy.start()
         else:
-            packed = sent[k - 1]
             packed[:D, :] = first.astype(BF)
             packed[D : D + UNITS, :] = second[:, :HALF].astype(BF)
-            packed[D + UNITS :, :] = second[:, HALF:].astype(BF)
-
-
-def total_kernel(own_in, own_out, p1, p2, p3, first_ref, second_ref):
+            packed[D + UNITS : PACKED, :] = second[:, HALF:].astype(BF)
+            packed[PACKED : PACKED + NOTE, :] = note[:, :HALF]
+            packed[PACKED + NOTE :, :] = note[:, HALF:]
+    for copy in copies:
+        copy.wait()
+
+
+def note_kernel(own_centroid, p1, p2, p3, out_ref):
+    for at, columns in ((PACKED, slice(0, HALF)), (PACKED + NOTE, slice(HALF, D))):
+        rows = slice(at, at + NOTE)
+        notes = p1[rows, :].astype(F32) + p2[rows, :].astype(F32) + p3[rows, :].astype(F32)
+        out_ref[:, columns] = own_centroid[:, columns] + notes[0:1] + notes[1:2]
+
+
+def total_kernel(
+    own_in_ref, own_out_ref, p1, p2, p3, first_ref, second_ref, own_in, own_out, sems
+):
     def total(rows):
         return p1[rows, :].astype(F32) + p2[rows, :].astype(F32) + p3[rows, :].astype(F32)
 
+    copies = [
+        pltpu.make_async_copy(own_in_ref, own_in, sems.at[0]),
+        pltpu.make_async_copy(own_out_ref, own_out, sems.at[1]),
+    ]
+    for copy in copies:
+        copy.start()
+    copies[0].wait()
     first_ref[0] = own_in[...] + total(slice(0, D))
+    copies[1].wait()
     second_ref[0, :, :HALF] = own_out[:, :HALF] + total(slice(D, D + UNITS))
     second_ref[0, :, HALF:] = own_out[:, HALF:] + total(slice(D + UNITS, PACKED))
 
@@ -177,7 +201,9 @@
 def call(kernel, outs, *operands, **options):
     return pl.pallas_call(
         kernel,
-        out_shape=[jax.ShapeDtypeStruct(*out) for out in outs],
+        out_shape=[
+            out if hasattr(out, "memory_space") else jax.ShapeDtypeStruct(*out) for out in outs
+        ],
         compiler_params=pltpu.CompilerParams(vmem_limit_bytes=VMEM_LIMIT),
         **options,
     )(*operands)
@@ -210,31 +236,41 @@
     ).reshape(MIXED, D)
     other_rows = shift(own_rows, "core", CORE, 1)
     part_shapes = [
-        ((MIXED + NOTE, D), BF), ((1, D), F32), ((ROWS, D), BF), ((ROWS, D), BF),
+        ((MIXED, D), BF), ((1, D), F32), ((ROWS, D), BF), ((ROWS, D), BF),
         ((ROWS, X * UNITS), BF), ((ROWS, X * UNITS), BF),
     ]
     nothing = jnp.zeros((1, D), F32)
-    own = call(expert_kernel, part_shapes, own_rows, centroid, nothing, *shards)
-    other = call(expert_kernel, part_shapes, other_rows, centroid, own[1], *shards)
+    other = call(expert_kernel, part_shapes, other_rows, centroid, nothing, *shards)
+    own = call(expert_kernel, part_shapes, own_rows, centroid, other[1], *shards)
     from_other = shift(other[0], "core", CORE, 1)
-    returned, centroid_grad = call(
-        join_kernel, [((MIXED, D), BF), ((1, D), F32)], own[0], from_other, other[1]
-    )
+    own_scratch = [
+        pltpu.VMEM((D, UNITS), F32), pltpu.VMEM((UNITS, D), F32), pltpu.SemaphoreType.DMA((2,)),
+    ]
+    grads = call(
+        weight_grad_kernel,
+        [pltpu.HBM((D, UNITS), F32), pltpu.HBM((UNITS, D), F32)]
+        + [((PACKED + 2 * NOTE, UNITS), BF)] * (X - 1),
+        *own[1:], *other[2:], from_other,
+        in_specs=[vmem] * 9 + [pl.BlockSpec(memory_space=pl.ANY)],
+        out_specs=[hbm, hbm] + [vmem] * (X - 1),
+        scratch_shapes=own_scratch,
+    )
+    arrived = [shift(grads[1 + k], "x", X, k) for k in range(1, X)]
+    (returned,) = call(join_kernel, [((MIXED, D), BF)], own[0], from_other)
     home = lax.all_to_all(
         returned.reshape(ZH * EXPERTS, 2 * BLK, D), ("zh", "y", "zl"), 0, 0, tiled=True
     ).reshape(MIXED, D)
-    grads = call(
-        weight_grad_kernel,
-        [((D, UNITS), F32), ((UNITS, D), F32)] + [((PACKED, UNITS), BF)] * (X - 1),
-        *own[2:], *other[2:], returned,
-        in_specs=[vmem] * 8 + [pl.BlockSpec(memory_space=pl.ANY)],
-    )
-    arrived = [shift(grads[1 + k], "x", X, k) for k in range(1, X)]
+    (centroid_grad,) = call(note_kernel, [((1, D), F32)], own[1], *arrived)
+    centroid_grad += shift(centroid_grad, "core", CORE, 1)
+    grad_centroid = centroid_grad + shift(centroid_grad, "zh", ZH, 1)
     first_grad, second_grad = call(
-        total_kernel, [((1, D, UNITS), F32), ((1, UNITS, D), F32)], *grads[:2], *arrived
-    )
-    centroid_grad += shift(centroid_grad, "zh", ZH, 1)
-    grad_centroid = centroid_grad + sum(shift(centroid_grad, "x", X, k) for k in range(1, X))
+        total_kernel,
+        [((1, D, UNITS), F32), ((1, UNITS, D), F32)],
+        in_hbm(grads[0]), in_hbm(grads[1]), *arrived,
+        in_specs=[hbm, hbm] + [vmem] * (X - 1),
+        scratch_shapes=own_scratch,
+        cost_estimate=pl.CostEstimate(flops=20 * 10**9, transcendentals=0, bytes_accessed=4 * 2**20),
+    )
     layer_out, grad_tokens = call(
         unpack_kernel, [((TOK, D), BF), ((TOK, D), BF)], slot_order, home, tokens, out_grad
     )

time: 132 us -> 126 us (0.955)
  the two profiles are of different devices: /device:TPU:8 before, /device:TPU:6 now
where the time goes in v6:
time: 126 us; the launch traced here: 124 us
  starting transfers between devices  63.3 us (50%)
  waiting for transfers between devices  42.5 us (34%)
  Pallas kernels  14.7 us (12%)
  local copies, waits for them, and re-layouts  1.61 us (1%)
    ppermute x10, starting transfers between devices, shift(): lax.ppermute(value, axis, [(i, (i + by) % size) for i in range(size)])  33.7 us
    all_to_all x1, waiting for transfers between devices, on_device(): lax.all_to_all(packed.reshape(ZH * EXPERTS, 2 * BLK, D), ('zh', 'y', 'zl'...  21.4 us
    ppermute x10, waiting for transfers between devices, shift(): lax.ppermute(value, axis, [(i, (i + by) % size) for i in range(size)])  21.1 us
    all_to_all x1, starting transfers between devices, on_device(): lax.all_to_all(packed.reshape(ZH * EXPERTS, 2 * BLK, D), ('zh', 'y', 'zl'...  18.9 us
    pallas_call x8, Pallas kernels, call(): pl.pallas_call(kernel, out_shape=[out if hasattr(out, 'memory_space') els...  14.7 us
    all_to_all x1, starting transfers between devices, on_device(): lax.all_to_all(returned.reshape(ZH * EXPERTS, 2 * BLK, D), ('zh', 'y', 'z...  10.7 us
  transfers between devices with their start and end apart: 12, of which 6 were waited for; matrix products, arithmetic and copies ran while one was open for 1% of the time, Pallas kernels for 5%

profile of v6, /device:TPU:6, one launch (start us, length us, event | category | flops | bytes accessed | tf_op | source)
XLA Modules:
  0.0 123.6 jit_solution(15495183050109653012)
XLA Ops:
  0.6 2.1 %shard_map.101 = bf16[512,512]{1,0:T(8,128)(2,1)} custom-call(s32[1,128]{1,0:T(1,128)} %order_ref.3, bf16[128,512]{1,0:T(8,128)(2,1)} %tok_ref.3, bf16[128,512]{1,0:T(8,128)(2,1)} %grad_ref.3), custom_call_target="tpu_custom_call" | custom-call | tf_op jit(solution)/shard_map/pallas_call | solution.py:202
  2.8 0.0 copy-start.4
  2.8 18.9 %all-to-all-start = ((bf16[64,8,512]{2,1,0:T(8,128)(2,1)}), bf16[64,8,512]{2,1,0:T(8,128)(2,1)S(1)}, u32[]{:S(2)}, u32[]{:S(2)}) async-start(bf16[64,8,512]{2,1,0:T(8,128)(2,1)} %bitcast), calls=%async_computation | async-start | bytes 1048576 | tf_op jit(solution)/shard_map/all_to_all | solution.py:234
  21.7 0.0 copy-done.4
  21.7 0.0 copy-start.5
  21.7 0.9 copy-done.5
  22.7 0.0 copy-start.2
  22.7 2.7 %collective-permute-start.1 = (bf16[1024,256]{1,0:T(8,128)(2,1)S(1)}, bf16[1024,256]{1,0:T(8,128)(2,1)S(1)}, u32[]{:S(2)}, u32[]{:S(2)}) collective-permute-start(bf16[1024,256]{1,0:T(8,128)(2,1)S(1)} %pad_maximum_fusion.s0), channel_id=1, source_target_pairs={{0,192},{64,0},{128,64},{192,128},{1,193},{65,1},{129,65},{193,129... | collective-permute-start | bytes 1572872 | tf_op jit(solution)/shard_map/ppermute | solution.py:213
  25.4 3.0 %collective-permute-start.2 = (bf16[1024,256]{1,0:T(8,128)(2,1)S(1)}, bf16[1024,256]{1,0:T(8,128)(2,1)S(1)}, u32[]{:S(2)}, u32[]{:S(2)}) collective-permute-start(bf16[1024,256]{1,0:T(8,128)(2,1)S(1)} %pad_maximum_fusion.s0), channel_id=1, source_target_pairs={{0,128},{64,192},{128,0},{192,64},{1,129},{65,193},{129,1},{193,65... | collective-permute-start | bytes 1572872 | tf_op jit(solution)/shard_map/ppermute | solution.py:213
  28.4 4.0 %collective-permute-start.3 = (bf16[1024,256]{1,0:T(8,128)(2,1)S(1)}, bf16[1024,256]{1,0:T(8,128)(2,1)S(1)}, u32[]{:S(2)}, u32[]{:S(2)}) collective-permute-start(bf16[1024,256]{1,0:T(8,128)(2,1)S(1)} %pad_maximum_fusion.s0), channel_id=1, source_target_pairs={{0,64},{64,128},{128,192},{192,0},{1,65},{65,129},{129,193},{193,1... | collective-permute-start | bytes 1572872 | tf_op jit(solution)/shard_map/ppermute | solution.py:213
  32.5 21.4 %all-to-all-done = bf16[64,8,512]{2,1,0:T(8,128)(2,1)S(1)} async-done(((bf16[64,8,512]{2,1,0:T(8,128)(2,1)}), bf16[64,8,512]{2,1,0:T(8,128)(2,1)S(1)}, u32[]{:S(2)}, u32[]{:S(2)}) %all-to-all-start) | async-done | bytes 524320 | tf_op jit(solution)/shard_map/all_to_all | solution.py:234
  53.9 1.9 %collective-permute-start = (bf16[512,512]{1,0:T(8,128)(2,1)S(1)}, bf16[512,512]{1,0:T(8,128)(2,1)S(1)}, u32[]{:S(2)}, u32[]{:S(2)}) collective-permute-start(bf16[512,512]{1,0:T(8,128)(2,1)S(1)} %bitcast.6), channel_id=1, source_target_pairs={{0,32},{32,0},{1,33},{33,1},{2,34},{34,2},{3,35},{35,3},{4,36},{36... | collective-permute-start | bytes 1572872 | tf_op jit(solution)/shard_map/ppermute | solution.py:213
  55.8 0.0 collective-permute-done.1.s1
  55.8 0.0 collective-permute-done.2.s2
  55.8 0.0 collective-permute-done.3.s3
  55.8 1.8 %collective-permute-done.rows_ref = bf16[512,512]{1,0:T(8,128)(2,1)S(1)} collective-permute-done((bf16[512,512]{1,0:T(8,128)(2,1)S(1)}, bf16[512,512]{1,0:T(8,128)(2,1)S(1)}, u32[]{:S(2)}, u32[]{:S(2)}) %collective-permute-start) | collective-permute-done | bytes 524320 | tf_op jit(solution)/shard_map/ppermute | solution.py:213
  57.7 0.0 copy-done.2
  57.7 2.7 %shard_map.102 = (bf16[512,512]{1,0:T(8,128)(2,1)S(1)}, f32[1,512]{1,0:T(1,128)S(1)}, bf16[256,512]{1,0:T(8,128)(2,1)S(1)}, bf16[256,512]{1,0:T(8,128)(2,1)S(1)}...) custom-call(bf16[512,512]{1,0:T(8,128)(2,1)S(1)} %collective-permute-done.rows_ref, ...), custom_call_target="tpu_custom_call" | custom-call | tf_op jit(solution)/shard_map/pallas_call | solution.py:202
  60.3 2.0 %collective-permute-start.4 = (bf16[512,512]{1,0:T(8,128)(2,1)S(1)}, bf16[512,512]{1,0:T(8,128)(2,1)S(1)}, u32[]{:S(2)}, u32[]{:S(2)}) collective-permute-start(bf16[512,512]{1,0:T(8,128)(2,1)S(1)} %get-tuple-element.28), channel_id=1, source_target_pairs={{0,32},{32,0},{1,33},{33,1},{2,34},{34,2},{3,35},{35,3},{4,36},{36... | collective-permute-start | bytes 1572872 | tf_op jit(solution)/shard_map/ppermute | solution.py:213
  62.4 2.7 %shard_map.103 = (bf16[512,512]{1,0:T(8,128)(2,1)S(1)}, f32[1,512]{1,0:T(1,128)S(1)}, bf16[256,512]{1,0:T(8,128)(2,1)S(1)}, bf16[256,512]{1,0:T(8,128)(2,1)S(1)}...) custom-call(bf16[512,512]{1,0:T(8,128)(2,1)S(1)} %bitcast.7, bf16[1,512]{1,0:T(2,128)(2,1)S(1)} %copy-done.2, ...), custom_call_target="tpu_custom_call" | custom-call | tf_op jit(solution)/shard_map/pallas_call | solution.py:202
  65.1 0.0 collective-permute-done.4.other_ref.after_ref
  65.1 3.0 %shard_map.106 = (f32[512,256]{1,0:T(8,128)}, f32[256,512]{1,0:T(8,128)}, bf16[1056,256]{1,0:T(8,128)(2,1)}, bf16[1056,256]{1,0:T(8,128)(2,1)}, bf16[1056,256]{1,0:T(8,128)(2,1)S(1)}) custom-call(f32[1,512]{1,0:T(1,128)S(1)} %get-tuple-element.31.centroid_ref.own_centroid, bf16[256,512]{1,0:T(8,128)(2,1)S(1)} %get-tuple-element.32.routed_a, ...), custom_call_target="tpu_custom_call" | custom-call | tf_op jit(solution)/shard_map/pallas_call | solution.py:202
  68.1 2.4 %collective-permute-start.5 = (bf16[1056,256]{1,0:T(8,128)(2,1)}, bf16[1056,256]{1,0:T(8,128)(2,1)S(1)}, u32[]{:S(2)}, u32[]{:S(2)}) collective-permute-start(bf16[1056,256]{1,0:T(8,128)(2,1)} %get-tuple-element.40), channel_id=1, source_target_pairs={{0,64},{64,128},{128,192},{192,0},{1,65},{65,129},{129,193},{193,1... | collective-permute-start | bytes 1622024 | tf_op jit(solution)/shard_map/ppermute | solution.py:213
  70.5 4.3 %collective-permute-start.6 = (bf16[1056,256]{1,0:T(8,128)(2,1)}, bf16[1056,256]{1,0:T(8,128)(2,1)S(1)}, u32[]{:S(2)}, u32[]{:S(2)}) collective-permute-start(bf16[1056,256]{1,0:T(8,128)(2,1)} %get-tuple-element.41), channel_id=1, source_target_pairs={{0,128},{64,192},{128,0},{192,64},{1,129},{65,193},{129,1},{193,65... | collective-permute-start | bytes 1622024 | tf_op jit(solution)/shard_map/ppermute | solution.py:213
  74.8 1.9 %collective-permute-start.7 = (bf16[1056,256]{1,0:T(8,128)(2,1)S(1)}, bf16[1056,256]{1,0:T(8,128)(2,1)S(1)}, u32[]{:S(2)}, u32[]{:S(2)}) collective-permute-start(bf16[1056,256]{1,0:T(8,128)(2,1)S(1)} %get-tuple-element.42), channel_id=1, source_target_pairs={{0,192},{64,0},{128,64},{192,128},{1,193},{65,1},{129,65},{193,129... | collective-permute-start | bytes 1622024 | tf_op jit(solution)/shard_map/ppermute | solution.py:213
  76.7 0.9 shard_map.104
  77.7 10.7 %all-to-all-start.1 = ((bf16[64,8,512]{2,1,0:T(8,128)(2,1)}), bf16[64,8,512]{2,1,0:T(8,128)(2,1)S(1)}, u32[]{:S(2)}, u32[]{:S(2)}) async-start(bf16[64,8,512]{2,1,0:T(8,128)(2,1)} %bitcast.4), calls=%async_computation.1 | async-start | bytes 1048576 | tf_op jit(solution)/shard_map/all_to_all | solution.py:260
  88.3 0.0 collective-permute-done.5.p1
  88.3 0.9 collective-permute-done.6.p2
  89.3 10.7 %collective-permute-done.7.p3 = bf16[1056,256]{1,0:T(8,128)(2,1)S(1)} collective-permute-done((bf16[1056,256]{1,0:T(8,128)(2,1)S(1)}, bf16[1056,256]{1,0:T(8,128)(2,1)S(1)}, u32[]{:S(2)}, u32[]{:S(2)}) %collective-permute-start.7) | collective-permute-done | bytes 540704 | tf_op jit(solution)/shard_map/ppermute | solution.py:213
  99.9 1.9 %collective-permute-start.8 = (f32[1,512]{1,0:T(1,128)S(1)}, f32[1,512]{1,0:T(1,128)S(1)}, u32[]{:S(2)}, u32[]{:S(2)}) collective-permute-start(f32[1,512]{1,0:T(1,128)S(1)} %shard_map.107), channel_id=1, source_target_pairs={{0,32},{32,0},{1,33},{33,1},{2,34},{34,2},{3,35},{35,3},{4,36},{36... | collective-permute-start | bytes 6152 | tf_op jit(solution)/shard_map/ppermute | solution.py:213
  101.9 1.1 collective-permute-done.8
  103.0 9.5 %collective-permute-start.9 = (f32[1,512]{1,0:T(1,128)S(1)}, f32[1,512]{1,0:T(1,128)S(1)}, u32[]{:S(2)}, u32[]{:S(2)}) collective-permute-start(f32[1,512]{1,0:T(1,128)S(1)} %add.6), channel_id=1, source_target_pairs={{0,256},{256,0},{1,257},{257,1},{2,258},{258,2},{3,259},{259,3},{4... | collective-permute-start | bytes 6152 | tf_op jit(solution)/shard_map/ppermute | solution.py:213
  112.5 0.0 copy-start
  112.5 0.0 copy-start.1
  112.5 2.2 %shard_map.108 = (f32[1,512,256]{2,1,0:T(8,128)}, f32[1,256,512]{2,1,0:T(8,128)}) custom-call(f32[512,256]{1,0:T(8,128)} %get-tuple-element.43.own_in_ref, f32[256,512]{1,0:T(8,128)} %get-tuple-element.44.own_out_ref, bf16[1056,256]{1,0:T(8,128)(2,1)S(1)} %collective-permute-done.5.p1, bf16[1056,256]{1,0:T(8,128)(2,1)S(1)} %collective-permute-done.6.p2, ...), custom_call_target="tpu_custom_call" | custom-call | flops 20000000000 | bytes 4194304 | tf_op jit(solution)/shard_map/pallas_call | solution.py:202
  114.7 6.6 %collective-permute-done.9 = f32[1,512]{1,0:T(1,128)S(1)} collective-permute-done((f32[1,512]{1,0:T(1,128)S(1)}, f32[1,512]{1,0:T(1,128)S(1)}, u32[]{:S(2)}, u32[]{:S(2)}) %collective-permute-start.9) | collective-permute-done | bytes 2080 | tf_op jit(solution)/shard_map/ppermute | solution.py:213
  121.3 0.6 add.7
  121.9 0.0 copy-start.3
  121.9 0.0 all-to-all-done.1
  121.9 0.0 copy-done
  121.9 0.0 copy-done.1
  121.9 0.6 copy-done.3
  122.5 1.1 shard_map.105
  (5 shorter events, 0.1 us)
Async XLA Ops:
  2.8 18.9 %copy-start.4 = (bf16[1,256,512]{2,1,0:T(8,128)(2,1)S(1)}, bf16[1,256,512]{2,1,0:T(8,128)(2,1)}, u32[]{:S(2)}) copy-start(bf16[1,256,512]{2,1,0:T(8,128)(2,1)} %param.10) | copy-start | bytes 786436
  2.8 51.1 %all-to-all-start = ((bf16[64,8,512]{2,1,0:T(8,128)(2,1)}), bf16[64,8,512]{2,1,0:T(8,128)(2,1)S(1)}, u32[]{:S(2)}, u32[]{:S(2)}) async-start(bf16[64,8,512]{2,1,0:T(8,128)(2,1)} %bitcast), calls=%async_computation | async-start | bytes 1048576 | tf_op jit(solution)/shard_map/all_to_all | solution.py:234
  21.7 1.0 copy-start.5
  22.7 35.0 %copy-start.2 = (bf16[1,512]{1,0:T(2,128)(2,1)S(1)}, bf16[1,512]{1,0:T(2,128)(2,1)}, u32[]{:S(2)}) copy-start(bf16[1,512]{1,0:T(2,128)(2,1)} %centroid_ref.3) | copy-start | bytes 3076
  22.7 33.1 %collective-permute-start.1 = (bf16[1024,256]{1,0:T(8,128)(2,1)S(1)}, bf16[1024,256]{1,0:T(8,128)(2,1)S(1)}, u32[]{:S(2)}, u32[]{:S(2)}) collective-permute-start(bf16[1024,256]{1,0:T(8,128)(2,1)S(1)} %pad_maximum_fusion.s0), channel_id=1, source_target_pairs={{0,192},{64,0},{128,64},{192,128},{1,193},{65,1},{129,65},{193,129... | collective-permute-start | bytes 1572872 | tf_op jit(solution)/shard_map/ppermute | solution.py:213
  25.4 30.4 %collective-permute-start.2 = (bf16[1024,256]{1,0:T(8,128)(2,1)S(1)}, bf16[1024,256]{1,0:T(8,128)(2,1)S(1)}, u32[]{:S(2)}, u32[]{:S(2)}) collective-permute-start(bf16[1024,256]{1,0:T(8,128)(2,1)S(1)} %pad_maximum_fusion.s0), channel_id=1, source_target_pairs={{0,128},{64,192},{128,0},{192,64},{1,129},{65,193},{129,1},{193,65... | collective-permute-start | bytes 1572872 | tf_op jit(solution)/shard_map/ppermute | solution.py:213
  28.4 27.4 %collective-permute-start.3 = (bf16[1024,256]{1,0:T(8,128)(2,1)S(1)}, bf16[1024,256]{1,0:T(8,128)(2,1)S(1)}, u32[]{:S(2)}, u32[]{:S(2)}) collective-permute-start(bf16[1024,256]{1,0:T(8,128)(2,1)S(1)} %pad_maximum_fusion.s0), channel_id=1, source_target_pairs={{0,64},{64,128},{128,192},{192,0},{1,65},{65,129},{129,193},{193,1... | collective-permute-start | bytes 1572872 | tf_op jit(solution)/shard_map/ppermute | solution.py:213
  53.9 3.8 %collective-permute-start = (bf16[512,512]{1,0:T(8,128)(2,1)S(1)}, bf16[512,512]{1,0:T(8,128)(2,1)S(1)}, u32[]{:S(2)}, u32[]{:S(2)}) collective-permute-start(bf16[512,512]{1,0:T(8,128)(2,1)S(1)} %bitcast.6), channel_id=1, source_target_pairs={{0,32},{32,0},{1,33},{33,1},{2,34},{34,2},{3,35},{35,3},{4,36},{36... | collective-permute-start | bytes 1572872 | tf_op jit(solution)/shard_map/ppermute | solution.py:213
  60.3 4.7 %collective-permute-start.4 = (bf16[512,512]{1,0:T(8,128)(2,1)S(1)}, bf16[512,512]{1,0:T(8,128)(2,1)S(1)}, u32[]{:S(2)}, u32[]{:S(2)}) collective-permute-start(bf16[512,512]{1,0:T(8,128)(2,1)S(1)} %get-tuple-element.28), channel_id=1, source_target_pairs={{0,32},{32,0},{1,33},{33,1},{2,34},{34,2},{3,35},{35,3},{4,36},{36... | collective-permute-start | bytes 1572872 | tf_op jit(solution)/shard_map/ppermute | solution.py:213
  68.1 20.3 %collective-permute-start.5 = (bf16[1056,256]{1,0:T(8,128)(2,1)}, bf16[1056,256]{1,0:T(8,128)(2,1)S(1)}, u32[]{:S(2)}, u32[]{:S(2)}) collective-permute-start(bf16[1056,256]{1,0:T(8,128)(2,1)} %get-tuple-element.40), channel_id=1, source_target_pairs={{0,64},{64,128},{128,192},{192,0},{1,65},{65,129},{129,193},{193,1... | collective-permute-start | bytes 1622024 | tf_op jit(solution)/shard_map/ppermute | solution.py:213
  70.5 18.8 %collective-permute-start.6 = (bf16[1056,256]{1,0:T(8,128)(2,1)}, bf16[1056,256]{1,0:T(8,128)(2,1)S(1)}, u32[]{:S(2)}, u32[]{:S(2)}) collective-permute-start(bf16[1056,256]{1,0:T(8,128)(2,1)} %get-tuple-element.41), channel_id=1, source_target_pairs={{0,128},{64,192},{128,0},{192,64},{1,129},{65,193},{129,1},{193,65... | collective-permute-start | bytes 1622024 | tf_op jit(solution)/shard_map/ppermute | solution.py:213
  74.8 25.1 %collective-permute-start.7 = (bf16[1056,256]{1,0:T(8,128)(2,1)S(1)}, bf16[1056,256]{1,0:T(8,128)(2,1)S(1)}, u32[]{:S(2)}, u32[]{:S(2)}) collective-permute-start(bf16[1056,256]{1,0:T(8,128)(2,1)S(1)} %get-tuple-element.42), channel_id=1, source_target_pairs={{0,192},{64,0},{128,64},{192,128},{1,193},{65,1},{129,65},{193,129... | collective-permute-start | bytes 1622024 | tf_op jit(solution)/shard_map/ppermute | solution.py:213
  77.7 44.2 %all-to-all-start.1 = ((bf16[64,8,512]{2,1,0:T(8,128)(2,1)}), bf16[64,8,512]{2,1,0:T(8,128)(2,1)S(1)}, u32[]{:S(2)}, u32[]{:S(2)}) async-start(bf16[64,8,512]{2,1,0:T(8,128)(2,1)} %bitcast.4), calls=%async_computation.1 | async-start | bytes 1048576 | tf_op jit(solution)/shard_map/all_to_all | solution.py:260
  99.9 3.1 %collective-permute-start.8 = (f32[1,512]{1,0:T(1,128)S(1)}, f32[1,512]{1,0:T(1,128)S(1)}, u32[]{:S(2)}, u32[]{:S(2)}) collective-permute-start(f32[1,512]{1,0:T(1,128)S(1)} %shard_map.107), channel_id=1, source_target_pairs={{0,32},{32,0},{1,33},{33,1},{2,34},{34,2},{3,35},{35,3},{4,36},{36... | collective-permute-start | bytes 6152 | tf_op jit(solution)/shard_map/ppermute | solution.py:213
  103.0 18.3 %collective-permute-start.9 = (f32[1,512]{1,0:T(1,128)S(1)}, f32[1,512]{1,0:T(1,128)S(1)}, u32[]{:S(2)}, u32[]{:S(2)}) collective-permute-start(f32[1,512]{1,0:T(1,128)S(1)} %add.6), channel_id=1, source_target_pairs={{0,256},{256,0},{1,257},{257,1},{2,258},{258,2},{3,259},{259,3},{4... | collective-permute-start | bytes 6152 | tf_op jit(solution)/shard_map/ppermute | solution.py:213
  112.5 9.4 %copy-start = (bf16[128,512]{1,0:T(8,128)(2,1)S(1)}, bf16[128,512]{1,0:T(8,128)(2,1)}, u32[]{:S(2)}) copy-start(bf16[128,512]{1,0:T(8,128)(2,1)} %tok_ref.3) | copy-start | bytes 393220
  112.5 9.4 %copy-start.1 = (bf16[128,512]{1,0:T(8,128)(2,1)S(1)}, bf16[128,512]{1,0:T(8,128)(2,1)}, u32[]{:S(2)}) copy-start(bf16[128,512]{1,0:T(8,128)(2,1)} %grad_ref.3) | copy-start | bytes 393220
  121.9 0.7 copy-start.3

commit v7 on v6

--- a/solution.py
+++ b/solution.py
@@ -32,11 +32,14 @@
     return lax.broadcasted_iota(jnp.int32, shape, axis)
 
 
-def mixed_picks(rows, on_rows_first):
+def mixed_picks(rows, on_rows_first, slots=False):
     shape = (rows, 2 * rows) if on_rows_first else (2 * rows, rows)
     plain = iota(shape, 0 if on_rows_first else 1)
     mixed = iota(shape, 1 if on_rows_first else 0)
-    place = (plain // BLK) * (2 * BLK) + plain % BLK
+    group = plain // BLK
+    if slots:
+        group = (group % ZL) * Y + group // ZL
+    place = group * (2 * BLK) + plain % BLK
     return (mixed == place).astype(BF), (mixed == place + BLK).astype(BF)
 
 
@@ -51,7 +54,7 @@
     ]
     for copy in copies:
         copy.start()
-    token_pick, grad_pick = mixed_picks(TOK, True)
+    token_pick, grad_pick = mixed_picks(TOK, True, slots=True)
     source = iota((TOK, 2 * TOK), 0).astype(F32)
     kind = (iota((TOK, 2 * TOK), 1) // BLK) % 2
     copies[0].wait()
@@ -118,17 +121,13 @@
 
 def weight_grad_kernel(
     centroid_ref, routed_a, d_expert_a, hidden_a, d_hidden_a,
-    routed_b, d_expert_b, hidden_b, d_hidden_b, after_ref, own_in_ref, own_out_ref, p1, p2, p3,
-    own_in, own_out, sems,
+    routed_b, d_expert_b, hidden_b, d_hidden_b, after_ref, own_ref, p1, p2, p3, own, sem,
 ):
     high = centroid_ref[...].astype(BF).astype(F32)
     row = iota((NOTE, D), 0)
     note = jnp.where(row == 0, high, jnp.where(row == 1, centroid_ref[...] - high, 0.0)).astype(BF)
-    copies = [
-        pltpu.make_async_copy(own_in, own_in_ref, sems.at[0]),
-        pltpu.make_async_copy(own_out, own_out_ref, sems.at[1]),
-    ]
-    for k, packed in enumerate((None, p1, p2, p3)):
+    copy = pltpu.make_async_copy(own, own_ref, sem)
+    for k, packed in enumerate((own, p1, p2, p3)):
         units = slice(k * UNITS, (k + 1) * UNITS)
         first = dot(routed_a[...], d_hidden_a[:, units], 0, 0) + dot(
             routed_b[...], d_hidden_b[:, units], 0, 0
@@ -136,19 +135,15 @@
         second = dot(hidden_a[:, units], d_expert_a[...], 0, 0) + dot(
             hidden_b[:, units], d_expert_b[...], 0, 0
         )
-        if packed is None:
-            own_in[...] = first
-            own_out[...] = second
-            for copy in copies:
-                copy.start()
+        packed[:D, :] = first.astype(BF)
+        packed[D : D + UNITS, :] = second[:, :HALF].astype(BF)
+        packed[D + UNITS : PACKED, :] = second[:, HALF:].astype(BF)
+        if k == 0:
+            copy.start()
         else:
-            packed[:D, :] = first.astype(BF)
-            packed[D : D + UNITS, :] = second[:, :HALF].astype(BF)
-            packed[D + UNITS : PACKED, :] = second[:, HALF:].astype(BF)
             packed[PACKED : PACKED + NOTE, :] = note[:, :HALF]
             packed[PACKED + NOTE :, :] = note[:, HALF:]
-    for copy in copies:
-        copy.wait()
+    copy.wait()
 
 
 def note_kernel(own_centroid, p1, p2, p3, out_ref):
@@ -158,34 +153,43 @@
         out_ref[:, columns] = own_centroid[:, columns] + notes[0:1] + notes[1:2]
 
 
-def total_kernel(
-    own_in_ref, own_out_ref, p1, p2, p3, first_ref, second_ref, own_in, own_out, sems
+def total_kernel(own_ref, p1, p2, p3, first_ref, second_ref, own, sem):
+    copy = pltpu.make_async_copy(own_ref, own, sem)
+    copy.start()
+    copy.wait()
+
+    def total(rows):
+        return (own[rows, :].astype(F32) + p1[rows, :].astype(F32)) + (
+            p2[rows, :].astype(F32) + p3[rows, :].astype(F32)
+        )
+
+    first_ref[0] = total(slice(0, D))
+    second_ref[0, :, :HALF] = total(slice(D, D + UNITS))
+    second_ref[0, :, HALF:] = total(slice(D + UNITS, PACKED))
+
+
+def unpack_kernel(
+    order_ref, home_ref, tok_ref, grad_ref, layer_ref, grad_out_ref, order_vmem, tok, grad_vmem, sems
 ):
-    def total(rows):
-        return p1[rows, :].astype(F32) + p2[rows, :].astype(F32) + p3[rows, :].astype(F32)
-
     copies = [
-        pltpu.make_async_copy(own_in_ref, own_in, sems.at[0]),
-        pltpu.make_async_copy(own_out_ref, own_out, sems.at[1]),
+        pltpu.make_async_copy(source, target, sems.at[i])
+        for i, (source, target) in enumerate(
+            ((order_ref, order_vmem), (tok_ref, tok), (grad_ref, grad_vmem))
+        )
     ]
     for copy in copies:
         copy.start()
     copies[0].wait()
-    first_ref[0] = own_in[...] + total(slice(0, D))
-    copies[1].wait()
-    second_ref[0, :, :HALF] = own_out[:, :HALF] + total(slice(D, D + UNITS))
-    second_ref[0, :, HALF:] = own_out[:, HALF:] + total(slice(D + UNITS, PACKED))
-
-
-def unpack_kernel(order_ref, home_ref, tok_ref, grad_ref, layer_ref, grad_out_ref):
-    order = jnp.broadcast_to(order_ref[...].astype(F32), (8, TOK)).astype(BF)
+    order = jnp.broadcast_to(order_vmem[...].astype(F32), (8, TOK)).astype(BF)
     token = iota((TOK, 2 * TOK), 0).astype(F32)
-    token_pick, grad_pick = mixed_picks(TOK, True)
+    token_pick, grad_pick = mixed_picks(TOK, True, slots=True)
     kind = (iota((TOK, 2 * TOK), 1) // BLK) % 2
     pick_token = ((token == dot(order, token_pick)[0:1]) & (kind == 0)).astype(BF)
     pick_grad = ((token == dot(order, grad_pick)[0:1]) & (kind == 1)).astype(BF)
-    layer = tok_ref[...].astype(F32)
-    grad = grad_ref[...].astype(F32)
+    copies[1].wait()
+    copies[2].wait()
+    layer = tok[...].astype(F32)
+    grad = grad_vmem[...].astype(F32)
     for half in range(ZH):
         rows = home_ref[half * 2 * TOK : (half + 1) * 2 * TOK, :]
         layer += dot(pick_token, rows)
@@ -218,21 +222,22 @@
     second = weight_out[0]
     shard = jnp.concatenate([weight_in[0], second[:, :HALF], second[:, HALF:]], axis=0)
     shards = [shard] + [shift(shard, "x", X, -k) for k in range(1, X)]
+    token_scratch = [
+        pltpu.VMEM((1, TOK), jnp.int32),
+        pltpu.VMEM((TOK, D), BF),
+        pltpu.VMEM((TOK, D), BF),
+        pltpu.SemaphoreType.DMA((3,)),
+    ]
     (packed,) = call(
         pack_kernel,
         [((MIXED, D), BF)],
         *(in_hbm(each) for each in (slot_order, tokens, out_grad)),
         in_specs=[hbm] * 3,
         out_specs=[vmem],
-        scratch_shapes=[
-            pltpu.VMEM((1, TOK), jnp.int32),
-            pltpu.VMEM((TOK, D), BF),
-            pltpu.VMEM((TOK, D), BF),
-            pltpu.SemaphoreType.DMA((3,)),
-        ],
+        scratch_shapes=token_scratch,
     )
     own_rows = lax.all_to_all(
-        packed.reshape(ZH * EXPERTS, 2 * BLK, D), ("zh", "y", "zl"), 0, 0, tiled=True
+        packed.reshape(ZH * EXPERTS, 2 * BLK, D), ("zh", "zl", "y"), 0, 0, tiled=True
     ).reshape(MIXED, D)
     other_rows = shift(own_rows, "core", CORE, 1)
     part_shapes = [
@@ -243,22 +248,19 @@
     other = call(expert_kernel, part_shapes, other_rows, centroid, nothing, *shards)
     own = call(expert_kernel, part_shapes, own_rows, centroid, other[1], *shards)
     from_other = shift(other[0], "core", CORE, 1)
-    own_scratch = [
-        pltpu.VMEM((D, UNITS), F32), pltpu.VMEM((UNITS, D), F32), pltpu.SemaphoreType.DMA((2,)),
-    ]
+    own_scratch = [pltpu.VMEM((PACKED, UNITS), BF), pltpu.SemaphoreType.DMA(())]
     grads = call(
         weight_grad_kernel,
-        [pltpu.HBM((D, UNITS), F32), pltpu.HBM((UNITS, D), F32)]
-        + [((PACKED + 2 * NOTE, UNITS), BF)] * (X - 1),
+        [pltpu.HBM((PACKED, UNITS), BF)] + [((PACKED + 2 * NOTE, UNITS), BF)] * (X - 1),
         *own[1:], *other[2:], from_other,
         in_specs=[vmem] * 9 + [pl.BlockSpec(memory_space=pl.ANY)],
-        out_specs=[hbm, hbm] + [vmem] * (X - 1),
+        out_specs=[hbm] + [vmem] * (X - 1),
         scratch_shapes=own_scratch,
     )
-    arrived = [shift(grads[1 + k], "x", X, k) for k in range(1, X)]
+    arrived = [shift(grads[k], "x", X, k) for k in range(1, X)]
     (returned,) = call(join_kernel, [((MIXED, D), BF)], own[0], from_other)
     home = lax.all_to_all(
-        returned.reshape(ZH * EXPERTS, 2 * BLK, D), ("zh", "y", "zl"), 0, 0, tiled=True
+        returned.reshape(ZH * EXPERTS, 2 * BLK, D), ("zh", "zl", "y"), 0, 0, tiled=True
     ).reshape(MIXED, D)
     (centroid_grad,) = call(note_kernel, [((1, D), F32)], own[1], *arrived)
     centroid_grad += shift(centroid_grad, "core", CORE, 1)
@@ -266,13 +268,17 @@
     first_grad, second_grad = call(
         total_kernel,
         [((1, D, UNITS), F32), ((1, UNITS, D), F32)],
-        in_hbm(grads[0]), in_hbm(grads[1]), *arrived,
-        in_specs=[hbm, hbm] + [vmem] * (X - 1),
+        in_hbm(grads[0]), *arrived,
+        in_specs=[hbm] + [vmem] * (X - 1),
         scratch_shapes=own_scratch,
         cost_estimate=pl.CostEstimate(flops=20 * 10**9, transcendentals=0, bytes_accessed=4 * 2**20),
     )
     layer_out, grad_tokens = call(
-        unpack_kernel, [((TOK, D), BF), ((TOK, D), BF)], slot_order, home, tokens, out_grad
+        unpack_kernel,
+        [((TOK, D), BF), ((TOK, D), BF)],
+        in_hbm(slot_order), home, in_hbm(tokens), in_hbm(out_grad),
+        in_specs=[hbm, vmem, hbm, hbm],
+        scratch_shapes=token_scratch,
     )
     return (layer_out, grad_tokens, grad_centroid, first_grad, second_grad)
 

time: 126 us -> 126 us (level)
  starting transfers between devices: 63.3 us -> 58.8 us
  waiting for transfers between devices: 42.5 us -> 47 us
    ppermute x10, starting transfers between devices: 33.7 us -> 29.8 us  [shift(): lax.ppermute(value, axis, [(i, (i + by) % size) for i in range(size)])]
    ppermute x10, waiting for transfers between devices: 21.1 us -> 23.9 us  [shift(): lax.ppermute(value, axis, [(i, (i + by) % size) for i in range(size)])]
    all_to_all x2, waiting for transfers between devices: 21.4 us -> 23.2 us  [the longest x1 23.1 us: on_device(): lax.all_to_all(packed.reshape(ZH * EXPERTS, 2 * BLK, D), ('zh', 'zl', 'y'...]
where the time goes in v7:
time: 126 us; the launch traced here: 124 us
  starting transfers between devices  58.8 us (47%)
  waiting for transfers between devices  47 us (37%)
  Pallas kernels  15.2 us (12%)
    ppermute x10, starting transfers between devices, shift(): lax.ppermute(value, axis, [(i, (i + by) % size) for i in range(size)])  29.8 us
    ppermute x10, waiting for transfers between devices, shift(): lax.ppermute(value, axis, [(i, (i + by) % size) for i in range(size)])  23.9 us
    all_to_all x1, waiting for transfers between devices, on_device(): lax.all_to_all(packed.reshape(ZH * EXPERTS, 2 * BLK, D), ('zh', 'zl', 'y'...  23.1 us
    all_to_all x1, starting transfers between devices, on_device(): lax.all_to_all(packed.reshape(ZH * EXPERTS, 2 * BLK, D), ('zh', 'zl', 'y'...  18.9 us
    pallas_call x8, Pallas kernels, call(): pl.pallas_call(kernel, out_shape=[out if hasattr(out, 'memory_space') els...  15.2 us
    all_to_all x1, starting transfers between devices, on_device(): lax.all_to_all(returned.reshape(ZH * EXPERTS, 2 * BLK, D), ('zh', 'zl', '...  10.1 us
  transfers between devices with their start and end apart: 12, of which 6 were waited for; matrix products, arithmetic and copies ran while one was open for 1% of the time, Pallas kernels for 5%

profile of v7, /device:TPU:6, one launch (start us, length us, event | category | flops | bytes accessed | tf_op | source)
XLA Modules:
  0.0 123.5 jit_solution(11989714176884017718)
XLA Ops:
  0.6 2.1 %shard_map.101 = bf16[512,512]{1,0:T(8,128)(2,1)} custom-call(s32[1,128]{1,0:T(1,128)} %order_ref.3, bf16[128,512]{1,0:T(8,128)(2,1)} %tok_ref.3, bf16[128,512]{1,0:T(8,128)(2,1)} %grad_ref.3), custom_call_target="tpu_custom_call" | custom-call | tf_op jit(solution)/shard_map/pallas_call | solution.py:206
  2.8 0.0 copy-start.1
  2.8 18.9 %all-to-all-start = ((bf16[64,8,512]{2,1,0:T(8,128)(2,1)}), bf16[64,8,512]{2,1,0:T(8,128)(2,1)S(1)}, u32[]{:S(2)}, u32[]{:S(2)}) async-start(bf16[64,8,512]{2,1,0:T(8,128)(2,1)} %bitcast), calls=%async_computation | async-start | bytes 1048576 | tf_op jit(solution)/shard_map/all_to_all | solution.py:239
  21.7 0.0 copy-done.1
  21.7 0.0 copy-start.2
  21.7 0.9 copy-done.2
  22.7 0.0 copy-start
  22.7 2.4 %collective-permute-start.3 = (bf16[1024,256]{1,0:T(8,128)(2,1)S(1)}, bf16[1024,256]{1,0:T(8,128)(2,1)S(1)}, u32[]{:S(2)}, u32[]{:S(2)}) collective-permute-start(bf16[1024,256]{1,0:T(8,128)(2,1)S(1)} %pad_maximum_fusion.s0), channel_id=1, source_target_pairs={{0,64},{64,128},{128,192},{192,0},{1,65},{65,129},{129,193},{193,1... | collective-permute-start | bytes 1572872 | tf_op jit(solution)/shard_map/ppermute | solution.py:217
  25.1 4.3 %collective-permute-start.2 = (bf16[1024,256]{1,0:T(8,128)(2,1)S(1)}, bf16[1024,256]{1,0:T(8,128)(2,1)S(1)}, u32[]{:S(2)}, u32[]{:S(2)}) collective-permute-start(bf16[1024,256]{1,0:T(8,128)(2,1)S(1)} %pad_maximum_fusion.s0), channel_id=1, source_target_pairs={{0,128},{64,192},{128,0},{192,64},{1,129},{65,193},{129,1},{193,65... | collective-permute-start | bytes 1572872 | tf_op jit(solution)/shard_map/ppermute | solution.py:217
  29.4 1.9 %collective-permute-start.1 = (bf16[1024,256]{1,0:T(8,128)(2,1)S(1)}, bf16[1024,256]{1,0:T(8,128)(2,1)S(1)}, u32[]{:S(2)}, u32[]{:S(2)}) collective-permute-start(bf16[1024,256]{1,0:T(8,128)(2,1)S(1)} %pad_maximum_fusion.s0), channel_id=1, source_target_pairs={{0,192},{64,0},{128,64},{192,128},{1,193},{65,1},{129,65},{193,129... | collective-permute-start | bytes 1572872 | tf_op jit(solution)/shard_map/ppermute | solution.py:217
  31.3 23.1 %all-to-all-done = bf16[64,8,512]{2,1,0:T(8,128)(2,1)S(1)} async-done(((bf16[64,8,512]{2,1,0:T(8,128)(2,1)}), bf16[64,8,512]{2,1,0:T(8,128)(2,1)S(1)}, u32[]{:S(2)}, u32[]{:S(2)}) %all-to-all-start) | async-done | bytes 524320 | tf_op jit(solution)/shard_map/all_to_all | solution.py:239
  54.5 1.9 %collective-permute-start = (bf16[512,512]{1,0:T(8,128)(2,1)S(1)}, bf16[512,512]{1,0:T(8,128)(2,1)S(1)}, u32[]{:S(2)}, u32[]{:S(2)}) collective-permute-start(bf16[512,512]{1,0:T(8,128)(2,1)S(1)} %bitcast.6), channel_id=1, source_target_pairs={{0,32},{32,0},{1,33},{33,1},{2,34},{34,2},{3,35},{35,3},{4,36},{36... | collective-permute-start | bytes 1572872 | tf_op jit(solution)/shard_map/ppermute | solution.py:217
  56.4 0.0 collective-permute-done.3.s3
  56.4 0.0 collective-permute-done.2.s2
  56.4 0.0 collective-permute-done.1.s1
  56.4 1.8 %collective-permute-done.rows_ref = bf16[512,512]{1,0:T(8,128)(2,1)S(1)} collective-permute-done((bf16[512,512]{1,0:T(8,128)(2,1)S(1)}, bf16[512,512]{1,0:T(8,128)(2,1)S(1)}, u32[]{:S(2)}, u32[]{:S(2)}) %collective-permute-start) | collective-permute-done | bytes 524320 | tf_op jit(solution)/shard_map/ppermute | solution.py:217
  58.3 0.0 copy-done
  58.3 2.7 %shard_map.102 = (bf16[512,512]{1,0:T(8,128)(2,1)S(1)}, f32[1,512]{1,0:T(1,128)S(1)}, bf16[256,512]{1,0:T(8,128)(2,1)S(1)}, bf16[256,512]{1,0:T(8,128)(2,1)S(1)}...) custom-call(bf16[512,512]{1,0:T(8,128)(2,1)S(1)} %collective-permute-done.rows_ref, ...), custom_call_target="tpu_custom_call" | custom-call | tf_op jit(solution)/shard_map/pallas_call | solution.py:206
  61.0 2.0 %collective-permute-start.4 = (bf16[512,512]{1,0:T(8,128)(2,1)S(1)}, bf16[512,512]{1,0:T(8,128)(2,1)S(1)}, u32[]{:S(2)}, u32[]{:S(2)}) collective-permute-start(bf16[512,512]{1,0:T(8,128)(2,1)S(1)} %get-tuple-element.27), channel_id=1, source_target_pairs={{0,32},{32,0},{1,33},{33,1},{2,34},{34,2},{3,35},{35,3},{4,36},{36... | collective-permute-start | bytes 1572872 | tf_op jit(solution)/shard_map/ppermute | solution.py:217
  63.0 2.7 %shard_map.103 = (bf16[512,512]{1,0:T(8,128)(2,1)S(1)}, f32[1,512]{1,0:T(1,128)S(1)}, bf16[256,512]{1,0:T(8,128)(2,1)S(1)}, bf16[256,512]{1,0:T(8,128)(2,1)S(1)}...) custom-call(bf16[512,512]{1,0:T(8,128)(2,1)S(1)} %bitcast.7, bf16[1,512]{1,0:T(2,128)(2,1)S(1)} %copy-done, ...), custom_call_target="tpu_custom_call" | custom-call | tf_op jit(solution)/shard_map/pallas_call | solution.py:206
  65.7 0.0 collective-permute-done.4.other_ref.after_ref
  65.7 2.7 %shard_map.106 = (bf16[1024,256]{1,0:T(8,128)(2,1)}, bf16[1056,256]{1,0:T(8,128)(2,1)}, bf16[1056,256]{1,0:T(8,128)(2,1)}, bf16[1056,256]{1,0:T(8,128)(2,1)S(1)}) custom-call(f32[1,512]{1,0:T(1,128)S(1)} %get-tuple-element.30.centroid_ref.own_centroid, bf16[256,512]{1,0:T(8,128)(2,1)S(1)} %get-tuple-element.31.routed_a, ...), custom_call_target="tpu_custom_call" | custom-call | tf_op jit(solution)/shard_map/pallas_call | solution.py:206
  68.4 2.4 %collective-permute-start.5 = (bf16[1056,256]{1,0:T(8,128)(2,1)}, bf16[1056,256]{1,0:T(8,128)(2,1)S(1)}, u32[]{:S(2)}, u32[]{:S(2)}) collective-permute-start(bf16[1056,256]{1,0:T(8,128)(2,1)} %get-tuple-element.39), channel_id=1, source_target_pairs={{0,64},{64,128},{128,192},{192,0},{1,65},{65,129},{129,193},{193,1... | collective-permute-start | bytes 1622024 | tf_op jit(solution)/shard_map/ppermute | solution.py:217
  70.8 4.3 %collective-permute-start.6 = (bf16[1056,256]{1,0:T(8,128)(2,1)}, bf16[1056,256]{1,0:T(8,128)(2,1)S(1)}, u32[]{:S(2)}, u32[]{:S(2)}) collective-permute-start(bf16[1056,256]{1,0:T(8,128)(2,1)} %get-tuple-element.40), channel_id=1, source_target_pairs={{0,128},{64,192},{128,0},{192,64},{1,129},{65,193},{129,1},{193,65... | collective-permute-start | bytes 1622024 | tf_op jit(solution)/shard_map/ppermute | solution.py:217
  75.2 1.9 %collective-permute-start.7 = (bf16[1056,256]{1,0:T(8,128)(2,1)S(1)}, bf16[1056,256]{1,0:T(8,128)(2,1)S(1)}, u32[]{:S(2)}, u32[]{:S(2)}) collective-permute-start(bf16[1056,256]{1,0:T(8,128)(2,1)S(1)} %get-tuple-element.41), channel_id=1, source_target_pairs={{0,192},{64,0},{128,64},{192,128},{1,193},{65,1},{129,65},{193,129... | collective-permute-start | bytes 1622024 | tf_op jit(solution)/shard_map/ppermute | solution.py:217
  77.1 0.9 shard_map.104
  78.0 10.1 %all-to-all-start.1 = ((bf16[64,8,512]{2,1,0:T(8,128)(2,1)}), bf16[64,8,512]{2,1,0:T(8,128)(2,1)S(1)}, u32[]{:S(2)}, u32[]{:S(2)}) async-start(bf16[64,8,512]{2,1,0:T(8,128)(2,1)} %bitcast.4), calls=%async_computation.1 | async-start | bytes 1048576 | tf_op jit(solution)/shard_map/all_to_all | solution.py:262
  88.1 0.0 collective-permute-done.5.p1
  88.2 1.5 %collective-permute-done.6.p2 = bf16[1056,256]{1,0:T(8,128)(2,1)S(1)} collective-permute-done((bf16[1056,256]{1,0:T(8,128)(2,1)}, bf16[1056,256]{1,0:T(8,128)(2,1)S(1)}, u32[]{:S(2)}, u32[]{:S(2)}) %collective-permute-start.6) | collective-permute-done | bytes 540704 | tf_op jit(solution)/shard_map/ppermute | solution.py:217
  89.6 10.7 %collective-permute-done.7.p3 = bf16[1056,256]{1,0:T(8,128)(2,1)S(1)} collective-permute-done((bf16[1056,256]{1,0:T(8,128)(2,1)S(1)}, bf16[1056,256]{1,0:T(8,128)(2,1)S(1)}, u32[]{:S(2)}, u32[]{:S(2)}) %collective-permute-start.7) | collective-permute-done | bytes 540704 | tf_op jit(solution)/shard_map/ppermute | solution.py:217
  100.3 1.9 %collective-permute-start.8 = (f32[1,512]{1,0:T(1,128)S(1)}, f32[1,512]{1,0:T(1,128)S(1)}, u32[]{:S(2)}, u32[]{:S(2)}) collective-permute-start(f32[1,512]{1,0:T(1,128)S(1)} %shard_map.107), channel_id=1, source_target_pairs={{0,32},{32,0},{1,33},{33,1},{2,34},{34,2},{3,35},{35,3},{4,36},{36... | collective-permute-start | bytes 6152 | tf_op jit(solution)/shard_map/ppermute | solution.py:217
  102.2 1.1 collective-permute-done.8
  103.3 6.7 %collective-permute-start.9 = (f32[1,512]{1,0:T(1,128)S(1)}, f32[1,512]{1,0:T(1,128)S(1)}, u32[]{:S(2)}, u32[]{:S(2)}) collective-permute-start(f32[1,512]{1,0:T(1,128)S(1)} %add.6), channel_id=1, source_target_pairs={{0,256},{256,0},{1,257},{257,1},{2,258},{258,2},{3,259},{259,3},{4... | collective-permute-start | bytes 6152 | tf_op jit(solution)/shard_map/ppermute | solution.py:217
  110.0 2.1 %shard_map.108 = (f32[1,512,256]{2,1,0:T(8,128)}, f32[1,256,512]{2,1,0:T(8,128)}) custom-call(bf16[1024,256]{1,0:T(8,128)(2,1)} %get-tuple-element.42.own_ref, bf16[1056,256]{1,0:T(8,128)(2,1)S(1)} %collective-permute-done.5.p1, bf16[1056,256]{1,0:T(8,128)(2,1)S(1)} %collective-permute-done.6.p2, bf16[1056,256]{1,0:T(8,128)(2,1)S(1)} %collective-permute-done.7.p3), custom_call_target="tpu_custom_call" | custom-call | flops 20000000000 | bytes 4194304 | tf_op jit(solution)/shard_map/pallas_call | solution.py:206
  112.2 8.8 %collective-permute-done.9 = f32[1,512]{1,0:T(1,128)S(1)} collective-permute-done((f32[1,512]{1,0:T(1,128)S(1)}, f32[1,512]{1,0:T(1,128)S(1)}, u32[]{:S(2)}, u32[]{:S(2)}) %collective-permute-start.9) | collective-permute-done | bytes 2080 | tf_op jit(solution)/shard_map/ppermute | solution.py:217
  121.0 0.6 add.7
  121.5 0.0 all-to-all-done.1
  121.5 2.0 %shard_map.105 = (bf16[128,512]{1,0:T(8,128)(2,1)}, bf16[128,512]{1,0:T(8,128)(2,1)}) custom-call(s32[1,128]{1,0:T(1,128)} %order_ref.3, bf16[512,512]{1,0:T(8,128)(2,1)S(1)} %bitcast.8, bf16[128,512]{1,0:T(8,128)(2,1)} %tok_ref.3, bf16[128,512]{1,0:T(8,128)(2,1)} %grad_ref.3), custom_call_target="tpu_custom_call" | custom-call | tf_op jit(solution)/shard_map/pallas_call | solution.py:206
  (5 shorter events, 0.1 us)
Async XLA Ops:
  2.8 18.9 %copy-start.1 = (bf16[1,256,512]{2,1,0:T(8,128)(2,1)S(1)}, bf16[1,256,512]{2,1,0:T(8,128)(2,1)}, u32[]{:S(2)}) copy-start(bf16[1,256,512]{2,1,0:T(8,128)(2,1)} %param.10) | copy-start | bytes 786436
  2.8 51.7 %all-to-all-start = ((bf16[64,8,512]{2,1,0:T(8,128)(2,1)}), bf16[64,8,512]{2,1,0:T(8,128)(2,1)S(1)}, u32[]{:S(2)}, u32[]{:S(2)}) async-start(bf16[64,8,512]{2,1,0:T(8,128)(2,1)} %bitcast), calls=%async_computation | async-start | bytes 1048576 | tf_op jit(solution)/shard_map/all_to_all | solution.py:239
  21.7 1.0 copy-start.2
  22.7 35.6 %copy-start = (bf16[1,512]{1,0:T(2,128)(2,1)S(1)}, bf16[1,512]{1,0:T(2,128)(2,1)}, u32[]{:S(2)}) copy-start(bf16[1,512]{1,0:T(2,128)(2,1)} %centroid_ref.3) | copy-start | bytes 3076
  22.7 33.7 %collective-permute-start.3 = (bf16[1024,256]{1,0:T(8,128)(2,1)S(1)}, bf16[1024,256]{1,0:T(8,128)(2,1)S(1)}, u32[]{:S(2)}, u32[]{:S(2)}) collective-permute-start(bf16[1024,256]{1,0:T(8,128)(2,1)S(1)} %pad_maximum_fusion.s0), channel_id=1, source_target_pairs={{0,64},{64,128},{128,192},{192,0},{1,65},{65,129},{129,193},{193,1... | collective-permute-start | bytes 1572872 | tf_op jit(solution)/shard_map/ppermute | solution.py:217
  25.1 31.3 %collective-permute-start.2 = (bf16[1024,256]{1,0:T(8,128)(2,1)S(1)}, bf16[1024,256]{1,0:T(8,128)(2,1)S(1)}, u32[]{:S(2)}, u32[]{:S(2)}) collective-permute-start(bf16[1024,256]{1,0:T(8,128)(2,1)S(1)} %pad_maximum_fusion.s0), channel_id=1, source_target_pairs={{0,128},{64,192},{128,0},{192,64},{1,129},{65,193},{129,1},{193,65... | collective-permute-start | bytes 1572872 | tf_op jit(solution)/shard_map/ppermute | solution.py:217
  29.4 27.0 %collective-permute-start.1 = (bf16[1024,256]{1,0:T(8,128)(2,1)S(1)}, bf16[1024,256]{1,0:T(8,128)(2,1)S(1)}, u32[]{:S(2)}, u32[]{:S(2)}) collective-permute-start(bf16[1024,256]{1,0:T(8,128)(2,1)S(1)} %pad_maximum_fusion.s0), channel_id=1, source_target_pairs={{0,192},{64,0},{128,64},{192,128},{1,193},{65,1},{129,65},{193,129... | collective-permute-start | bytes 1572872 | tf_op jit(solution)/shard_map/ppermute | solution.py:217
  54.5 3.8 %collective-permute-start = (bf16[512,512]{1,0:T(8,128)(2,1)S(1)}, bf16[512,512]{1,0:T(8,128)(2,1)S(1)}, u32[]{:S(2)}, u32[]{:S(2)}) collective-permute-start(bf16[512,512]{1,0:T(8,128)(2,1)S(1)} %bitcast.6), channel_id=1, source_target_pairs={{0,32},{32,0},{1,33},{33,1},{2,34},{34,2},{3,35},{35,3},{4,36},{36... | collective-permute-start | bytes 1572872 | tf_op jit(solution)/shard_map/ppermute | solution.py:217
  61.0 4.7 %collective-permute-start.4 = (bf16[512,512]{1,0:T(8,128)(2,1)S(1)}, bf16[512,512]{1,0:T(8,128)(2,1)S(1)}, u32[]{:S(2)}, u32[]{:S(2)}) collective-permute-start(bf16[512,512]{1,0:T(8,128)(2,1)S(1)} %get-tuple-element.27), channel_id=1, source_target_pairs={{0,32},{32,0},{1,33},{33,1},{2,34},{34,2},{3,35},{35,3},{4,36},{36... | collective-permute-start | bytes 1572872 | tf_op jit(solution)/shard_map/ppermute | solution.py:217
  68.4 19.7 %collective-permute-start.5 = (bf16[1056,256]{1,0:T(8,128)(2,1)}, bf16[1056,256]{1,0:T(8,128)(2,1)S(1)}, u32[]{:S(2)}, u32[]{:S(2)}) collective-permute-start(bf16[1056,256]{1,0:T(8,128)(2,1)} %get-tuple-element.39), channel_id=1, source_target_pairs={{0,64},{64,128},{128,192},{192,0},{1,65},{65,129},{129,193},{193,1... | collective-permute-start | bytes 1622024 | tf_op jit(solution)/shard_map/ppermute | solution.py:217
  70.8 18.8 %collective-permute-start.6 = (bf16[1056,256]{1,0:T(8,128)(2,1)}, bf16[1056,256]{1,0:T(8,128)(2,1)S(1)}, u32[]{:S(2)}, u32[]{:S(2)}) collective-permute-start(bf16[1056,256]{1,0:T(8,128)(2,1)} %get-tuple-element.40), channel_id=1, source_target_pairs={{0,128},{64,192},{128,0},{192,64},{1,129},{65,193},{129,1},{193,65... | collective-permute-start | bytes 1622024 | tf_op jit(solution)/shard_map/ppermute | solution.py:217
  75.2 25.1 %collective-permute-start.7 = (bf16[1056,256]{1,0:T(8,128)(2,1)S(1)}, bf16[1056,256]{1,0:T(8,128)(2,1)S(1)}, u32[]{:S(2)}, u32[]{:S(2)}) collective-permute-start(bf16[1056,256]{1,0:T(8,128)(2,1)S(1)} %get-tuple-element.41), channel_id=1, source_target_pairs={{0,192},{64,0},{128,64},{192,128},{1,193},{65,1},{129,65},{193,129... | collective-permute-start | bytes 1622024 | tf_op jit(solution)/shard_map/ppermute | solution.py:217
  78.0 43.6 %all-to-all-start.1 = ((bf16[64,8,512]{2,1,0:T(8,128)(2,1)}), bf16[64,8,512]{2,1,0:T(8,128)(2,1)S(1)}, u32[]{:S(2)}, u32[]{:S(2)}) async-start(bf16[64,8,512]{2,1,0:T(8,128)(2,1)} %bitcast.4), calls=%async_computation.1 | async-start | bytes 1048576 | tf_op jit(solution)/shard_map/all_to_all | solution.py:262
  100.3 3.1 %collective-permute-start.8 = (f32[1,512]{1,0:T(1,128)S(1)}, f32[1,512]{1,0:T(1,128)S(1)}, u32[]{:S(2)}, u32[]{:S(2)}) collective-permute-start(f32[1,512]{1,0:T(1,128)S(1)} %shard_map.107), channel_id=1, source_target_pairs={{0,32},{32,0},{1,33},{33,1},{2,34},{34,2},{3,35},{35,3},{4,36},{36... | collective-permute-start | bytes 6152 | tf_op jit(solution)/shard_map/ppermute | solution.py:217
  103.3 17.6 %collective-permute-start.9 = (f32[1,512]{1,0:T(1,128)S(1)}, f32[1,512]{1,0:T(1,128)S(1)}, u32[]{:S(2)}, u32[]{:S(2)}) collective-permute-start(f32[1,512]{1,0:T(1,128)S(1)} %add.6), channel_id=1, source_target_pairs={{0,256},{256,0},{1,257},{257,1},{2,258},{258,2},{3,259},{259,3},{4... | collective-permute-start | bytes 6152 | tf_op jit(solution)/shard_map/ppermute | solution.py:217

commit v8 on v7

--- a/solution.py
+++ b/solution.py
@@ -1,3 +1,4 @@
+import functools
 import math
 
 import jax
@@ -120,14 +121,13 @@
 
 
 def weight_grad_kernel(
-    centroid_ref, routed_a, d_expert_a, hidden_a, d_hidden_a,
-    routed_b, d_expert_b, hidden_b, d_hidden_b, after_ref, own_ref, p1, p2, p3, own, sem,
+    shards, centroid_ref, routed_a, d_expert_a, hidden_a, d_hidden_a,
+    routed_b, d_expert_b, hidden_b, d_hidden_b, after_ref, *packed_refs,
 ):
     high = centroid_ref[...].astype(BF).astype(F32)
     row = iota((NOTE, D), 0)
     note = jnp.where(row == 0, high, jnp.where(row == 1, centroid_ref[...] - high, 0.0)).astype(BF)
-    copy = pltpu.make_async_copy(own, own_ref, sem)
-    for k, packed in enumerate((own, p1, p2, p3)):
+    for k, packed in zip(shards, packed_refs):
         units = slice(k * UNITS, (k + 1) * UNITS)
         first = dot(routed_a[...], d_hidden_a[:, units], 0, 0) + dot(
             routed_b[...], d_hidden_b[:, units], 0, 0
@@ -138,12 +138,8 @@
         packed[:D, :] = first.astype(BF)
         packed[D : D + UNITS, :] = second[:, :HALF].astype(BF)
         packed[D + UNITS : PACKED, :] = second[:, HALF:].astype(BF)
-        if k == 0:
-            copy.start()
-        else:
-            packed[PACKED : PACKED + NOTE, :] = note[:, :HALF]
-            packed[PACKED + NOTE :, :] = note[:, HALF:]
-    copy.wait()
+        packed[PACKED : PACKED + NOTE, :] = note[:, :HALF]
+        packed[PACKED + NOTE :, :] = note[:, HALF:]
 
 
 def note_kernel(own_centroid, p1, p2, p3, out_ref):
@@ -153,11 +149,7 @@
         out_ref[:, columns] = own_centroid[:, columns] + notes[0:1] + notes[1:2]
 
 
-def total_kernel(own_ref, p1, p2, p3, first_ref, second_ref, own, sem):
-    copy = pltpu.make_async_copy(own_ref, own, sem)
-    copy.start()
-    copy.wait()
-
+def total_kernel(own, p1, p2, p3, first_ref, second_ref):
     def total(rows):
         return (own[rows, :].astype(F32) + p1[rows, :].astype(F32)) + (
             p2[rows, :].astype(F32) + p3[rows, :].astype(F32)
@@ -169,27 +161,19 @@
 
 
 def unpack_kernel(
-    order_ref, home_ref, tok_ref, grad_ref, layer_ref, grad_out_ref, order_vmem, tok, grad_vmem, sems
-):
-    copies = [
-        pltpu.make_async_copy(source, target, sems.at[i])
-        for i, (source, target) in enumerate(
-            ((order_ref, order_vmem), (tok_ref, tok), (grad_ref, grad_vmem))
-        )
-    ]
-    for copy in copies:
-        copy.start()
-    copies[0].wait()
+    order_ref, home_ref, tok_ref, grad_ref, layer_ref, grad_out_ref, order_vmem, sem
+):
+    copy = pltpu.make_async_copy(order_ref, order_vmem, sem)
+    copy.start()
+    copy.wait()
     order = jnp.broadcast_to(order_vmem[...].astype(F32), (8, TOK)).astype(BF)
     token = iota((TOK, 2 * TOK), 0).astype(F32)
     token_pick, grad_pick = mixed_picks(TOK, True, slots=True)
     kind = (iota((TOK, 2 * TOK), 1) // BLK) % 2
     pick_token = ((token == dot(order, token_pick)[0:1]) & (kind == 0)).astype(BF)
     pick_grad = ((token == dot(order, grad_pick)[0:1]) & (kind == 1)).astype(BF)
-    copies[1].wait()
-    copies[2].wait()
-    layer = tok[...].astype(F32)
-    grad = grad_vmem[...].astype(F32)
+    layer = tok_ref[...].astype(F32)
+    grad = grad_ref[...].astype(F32)
     for half in range(ZH):
         rows = home_ref[half * 2 * TOK : (half + 1) * 2 * TOK, :]
         layer += dot(pick_token, rows)
@@ -248,17 +232,19 @@
     other = call(expert_kernel, part_shapes, other_rows, centroid, nothing, *shards)
     own = call(expert_kernel, part_shapes, own_rows, centroid, other[1], *shards)
     from_other = shift(other[0], "core", CORE, 1)
-    own_scratch = [pltpu.VMEM((PACKED, UNITS), BF), pltpu.SemaphoreType.DMA(())]
-    grads = call(
-        weight_grad_kernel,
-        [pltpu.HBM((PACKED, UNITS), BF)] + [((PACKED + 2 * NOTE, UNITS), BF)] * (X - 1),
-        *own[1:], *other[2:], from_other,
-        in_specs=[vmem] * 9 + [pl.BlockSpec(memory_space=pl.ANY)],
-        out_specs=[hbm] + [vmem] * (X - 1),
-        scratch_shapes=own_scratch,
-    )
-    arrived = [shift(grads[k], "x", X, k) for k in range(1, X)]
+    any_space = pl.BlockSpec(memory_space=pl.ANY)
+
+    def weight_grads(shards, after):
+        return call(
+            functools.partial(weight_grad_kernel, shards),
+            [((PACKED + 2 * NOTE, UNITS), BF)] * len(shards),
+            *own[1:], *other[2:], after,
+            in_specs=[vmem] * 9 + [any_space],
+        )
+
     (returned,) = call(join_kernel, [((MIXED, D), BF)], own[0], from_other)
+    p2, p1, p3, p0 = weight_grads((2, 1, 3, 0), from_other)
+    arrived = [shift(p1, "x", X, 1), shift(p2, "x", X, 2), shift(p3, "x", X, 3)]
     home = lax.all_to_all(
         returned.reshape(ZH * EXPERTS, 2 * BLK, D), ("zh", "zl", "y"), 0, 0, tiled=True
     ).reshape(MIXED, D)
@@ -268,17 +254,15 @@
     first_grad, second_grad = call(
         total_kernel,
         [((1, D, UNITS), F32), ((1, UNITS, D), F32)],
-        in_hbm(grads[0]), *arrived,
-        in_specs=[hbm] + [vmem] * (X - 1),
-        scratch_shapes=own_scratch,
+        p0, *arrived,
         cost_estimate=pl.CostEstimate(flops=20 * 10**9, transcendentals=0, bytes_accessed=4 * 2**20),
     )
     layer_out, grad_tokens = call(
         unpack_kernel,
         [((TOK, D), BF), ((TOK, D), BF)],
-        in_hbm(slot_order), home, in_hbm(tokens), in_hbm(out_grad),
-        in_specs=[hbm, vmem, hbm, hbm],
-        scratch_shapes=token_scratch,
+        in_hbm(slot_order), home, tokens, out_grad,
+        in_specs=[hbm, vmem, vmem, vmem],
+        scratch_shapes=[pltpu.VMEM((1, TOK), jnp.int32), pltpu.SemaphoreType.DMA(())],
     )
     return (layer_out, grad_tokens, grad_centroid, first_grad, second_grad)
 

time: 126 us -> 126 us (level)
  Pallas kernels: 15.2 us -> 13.8 us
    pallas_call x8, Pallas kernels: 15.2 us -> 13.8 us  [call(): pl.pallas_call(kernel, out_shape=[out if hasattr(out, 'memory_space') els...]
  transfers between devices with their start and end apart: 12 -> 12, of which waited for: 6 -> 6; matrix products, arithmetic and copies ran while one was open for 1% -> 1% of each run, Pallas kernels for 5% -> 4%
where the time goes in v8:
time: 126 us; the launch traced here: 123 us
  starting transfers between devices  58.8 us (47%)
  waiting for transfers between devices  48 us (38%)
  Pallas kernels  13.8 us (11%)
    ppermute x10, starting transfers between devices, shift(): lax.ppermute(value, axis, [(i, (i + by) % size) for i in range(size)])  29.8 us
    ppermute x10, waiting for transfers between devices, shift(): lax.ppermute(value, axis, [(i, (i + by) % size) for i in range(size)])  24.9 us
    all_to_all x1, waiting for transfers between devices, on_device(): lax.all_to_all(packed.reshape(ZH * EXPERTS, 2 * BLK, D), ('zh', 'zl', 'y'...  23.1 us
    all_to_all x1, starting transfers between devices, on_device(): lax.all_to_all(packed.reshape(ZH * EXPERTS, 2 * BLK, D), ('zh', 'zl', 'y'...  18.9 us
    pallas_call x8, Pallas kernels, call(): pl.pallas_call(kernel, out_shape=[out if hasattr(out, 'memory_space') els...  13.8 us
    all_to_all x1, starting transfers between devices, on_device(): lax.all_to_all(returned.reshape(ZH * EXPERTS, 2 * BLK, D), ('zh', 'zl', '...  10.1 us
  transfers between devices with their start and end apart: 12, of which 6 were waited for; matrix products, arithmetic and copies ran while one was open for 1% of the time, Pallas kernels for 4%

profile of v8, /device:TPU:6, one launch (start us, length us, event | category | flops | bytes accessed | tf_op | source)
XLA Modules:
  0.0 123.1 jit_solution(13843456176659903648)
XLA Ops:
  0.6 2.1 %shard_map.101 = bf16[512,512]{1,0:T(8,128)(2,1)} custom-call(s32[1,128]{1,0:T(1,128)} %order_ref.3, bf16[128,512]{1,0:T(8,128)(2,1)} %tok_ref.3, bf16[128,512]{1,0:T(8,128)(2,1)} %grad_ref.3), custom_call_target="tpu_custom_call" | custom-call | tf_op jit(solution)/shard_map/pallas_call | solution.py:190
  2.8 0.0 copy-start.3
  2.8 18.9 %all-to-all-start = ((bf16[64,8,512]{2,1,0:T(8,128)(2,1)}), bf16[64,8,512]{2,1,0:T(8,128)(2,1)S(1)}, u32[]{:S(2)}, u32[]{:S(2)}) async-start(bf16[64,8,512]{2,1,0:T(8,128)(2,1)} %bitcast), calls=%async_computation | async-start | bytes 1048576 | tf_op jit(solution)/shard_map/all_to_all | solution.py:223
  21.7 0.0 copy-done.3
  21.7 0.0 copy-start.4
  21.7 0.9 copy-done.4
  22.7 0.0 copy-start.2
  22.7 2.4 %collective-permute-start.3 = (bf16[1024,256]{1,0:T(8,128)(2,1)S(1)}, bf16[1024,256]{1,0:T(8,128)(2,1)S(1)}, u32[]{:S(2)}, u32[]{:S(2)}) collective-permute-start(bf16[1024,256]{1,0:T(8,128)(2,1)S(1)} %pad_maximum_fusion.s0), channel_id=1, source_target_pairs={{0,64},{64,128},{128,192},{192,0},{1,65},{65,129},{129,193},{193,1... | collective-permute-start | bytes 1572872 | tf_op jit(solution)/shard_map/ppermute | solution.py:201
  25.1 4.3 %collective-permute-start.2 = (bf16[1024,256]{1,0:T(8,128)(2,1)S(1)}, bf16[1024,256]{1,0:T(8,128)(2,1)S(1)}, u32[]{:S(2)}, u32[]{:S(2)}) collective-permute-start(bf16[1024,256]{1,0:T(8,128)(2,1)S(1)} %pad_maximum_fusion.s0), channel_id=1, source_target_pairs={{0,128},{64,192},{128,0},{192,64},{1,129},{65,193},{129,1},{193,65... | collective-permute-start | bytes 1572872 | tf_op jit(solution)/shard_map/ppermute | solution.py:201
  29.4 1.9 %collective-permute-start.1 = (bf16[1024,256]{1,0:T(8,128)(2,1)S(1)}, bf16[1024,256]{1,0:T(8,128)(2,1)S(1)}, u32[]{:S(2)}, u32[]{:S(2)}) collective-permute-start(bf16[1024,256]{1,0:T(8,128)(2,1)S(1)} %pad_maximum_fusion.s0), channel_id=1, source_target_pairs={{0,192},{64,0},{128,64},{192,128},{1,193},{65,1},{129,65},{193,129... | collective-permute-start | bytes 1572872 | tf_op jit(solution)/shard_map/ppermute | solution.py:201
  31.3 23.1 %all-to-all-done = bf16[64,8,512]{2,1,0:T(8,128)(2,1)S(1)} async-done(((bf16[64,8,512]{2,1,0:T(8,128)(2,1)}), bf16[64,8,512]{2,1,0:T(8,128)(2,1)S(1)}, u32[]{:S(2)}, u32[]{:S(2)}) %all-to-all-start) | async-done | bytes 524320 | tf_op jit(solution)/shard_map/all_to_all | solution.py:223
  54.5 1.9 %collective-permute-start = (bf16[512,512]{1,0:T(8,128)(2,1)S(1)}, bf16[512,512]{1,0:T(8,128)(2,1)S(1)}, u32[]{:S(2)}, u32[]{:S(2)}) collective-permute-start(bf16[512,512]{1,0:T(8,128)(2,1)S(1)} %bitcast.6), channel_id=1, source_target_pairs={{0,32},{32,0},{1,33},{33,1},{2,34},{34,2},{3,35},{35,3},{4,36},{36... | collective-permute-start | bytes 1572872 | tf_op jit(solution)/shard_map/ppermute | solution.py:201
  56.4 0.0 collective-permute-done.3.s3
  56.4 0.0 collective-permute-done.2.s2
  56.4 0.0 collective-permute-done.1.s1
  56.4 1.8 %collective-permute-done.rows_ref = bf16[512,512]{1,0:T(8,128)(2,1)S(1)} collective-permute-done((bf16[512,512]{1,0:T(8,128)(2,1)S(1)}, bf16[512,512]{1,0:T(8,128)(2,1)S(1)}, u32[]{:S(2)}, u32[]{:S(2)}) %collective-permute-start) | collective-permute-done | bytes 524320 | tf_op jit(solution)/shard_map/ppermute | solution.py:201
  58.3 0.0 copy-done.2
  58.3 2.7 %shard_map.102 = (bf16[512,512]{1,0:T(8,128)(2,1)S(1)}, f32[1,512]{1,0:T(1,128)S(1)}, bf16[256,512]{1,0:T(8,128)(2,1)S(1)}, bf16[256,512]{1,0:T(8,128)(2,1)S(1)}...) custom-call(bf16[512,512]{1,0:T(8,128)(2,1)S(1)} %collective-permute-done.rows_ref, ...), custom_call_target="tpu_custom_call" | custom-call | tf_op jit(solution)/shard_map/pallas_call | solution.py:190
  61.0 2.0 %collective-permute-start.4 = (bf16[512,512]{1,0:T(8,128)(2,1)S(1)}, bf16[512,512]{1,0:T(8,128)(2,1)S(1)}, u32[]{:S(2)}, u32[]{:S(2)}) collective-permute-start(bf16[512,512]{1,0:T(8,128)(2,1)S(1)} %get-tuple-element.27), channel_id=1, source_target_pairs={{0,32},{32,0},{1,33},{33,1},{2,34},{34,2},{3,35},{35,3},{4,36},{36... | collective-permute-start | bytes 1572872 | tf_op jit(solution)/shard_map/ppermute | solution.py:201
  63.0 2.7 %shard_map.103 = (bf16[512,512]{1,0:T(8,128)(2,1)S(1)}, f32[1,512]{1,0:T(1,128)S(1)}, bf16[256,512]{1,0:T(8,128)(2,1)S(1)}, bf16[256,512]{1,0:T(8,128)(2,1)S(1)}...) custom-call(bf16[512,512]{1,0:T(8,128)(2,1)S(1)} %bitcast.7, bf16[1,512]{1,0:T(2,128)(2,1)S(1)} %copy-done.2, ...), custom_call_target="tpu_custom_call" | custom-call | tf_op jit(solution)/shard_map/pallas_call | solution.py:190
  65.7 0.0 collective-permute-done.4.other_ref.after_ref
  65.7 2.5 %shard_map.106 = (bf16[1056,256]{1,0:T(8,128)(2,1)}, bf16[1056,256]{1,0:T(8,128)(2,1)}, bf16[1056,256]{1,0:T(8,128)(2,1)}, bf16[1056,256]{1,0:T(8,128)(2,1)S(1)}) custom-call(f32[1,512]{1,0:T(1,128)S(1)} %get-tuple-element.30.centroid_ref.own_centroid, bf16[256,512]{1,0:T(8,128)(2,1)S(1)} %get-tuple-element.31.routed_a, ...), custom_call_target="tpu_custom_call" | custom-call | tf_op jit(solution)/shard_map/pallas_call | solution.py:190
  68.2 2.4 %collective-permute-start.5 = (bf16[1056,256]{1,0:T(8,128)(2,1)}, bf16[1056,256]{1,0:T(8,128)(2,1)S(1)}, u32[]{:S(2)}, u32[]{:S(2)}) collective-permute-start(bf16[1056,256]{1,0:T(8,128)(2,1)} %get-tuple-element.39), channel_id=1, source_target_pairs={{0,64},{64,128},{128,192},{192,0},{1,65},{65,129},{129,193},{193,1... | collective-permute-start | bytes 1622024 | tf_op jit(solution)/shard_map/ppermute | solution.py:201
  70.6 4.3 %collective-permute-start.6 = (bf16[1056,256]{1,0:T(8,128)(2,1)}, bf16[1056,256]{1,0:T(8,128)(2,1)S(1)}, u32[]{:S(2)}, u32[]{:S(2)}) collective-permute-start(bf16[1056,256]{1,0:T(8,128)(2,1)} %get-tuple-element.40), channel_id=1, source_target_pairs={{0,128},{64,192},{128,0},{192,64},{1,129},{65,193},{129,1},{193,65... | collective-permute-start | bytes 1622024 | tf_op jit(solution)/shard_map/ppermute | solution.py:201
  74.9 1.9 %collective-permute-start.7 = (bf16[1056,256]{1,0:T(8,128)(2,1)}, bf16[1056,256]{1,0:T(8,128)(2,1)S(1)}, u32[]{:S(2)}, u32[]{:S(2)}) collective-permute-start(bf16[1056,256]{1,0:T(8,128)(2,1)} %get-tuple-element.41), channel_id=1, source_target_pairs={{0,192},{64,0},{128,64},{192,128},{1,193},{65,1},{129,65},{193,129... | collective-permute-start | bytes 1622024 | tf_op jit(solution)/shard_map/ppermute | solution.py:201
  76.9 0.9 shard_map.104
  77.8 10.1 %all-to-all-start.1 = ((bf16[64,8,512]{2,1,0:T(8,128)(2,1)}), bf16[64,8,512]{2,1,0:T(8,128)(2,1)S(1)}, u32[]{:S(2)}, u32[]{:S(2)}) async-start(bf16[64,8,512]{2,1,0:T(8,128)(2,1)} %bitcast.4), calls=%async_computation.1 | async-start | bytes 1048576 | tf_op jit(solution)/shard_map/all_to_all | solution.py:248
  87.9 0.0 collective-permute-done.5.p1
  87.9 1.5 %collective-permute-done.6.p2 = bf16[1056,256]{1,0:T(8,128)(2,1)S(1)} collective-permute-done((bf16[1056,256]{1,0:T(8,128)(2,1)}, bf16[1056,256]{1,0:T(8,128)(2,1)S(1)}, u32[]{:S(2)}, u32[]{:S(2)}) %collective-permute-start.6) | collective-permute-done | bytes 540704 | tf_op jit(solution)/shard_map/ppermute | solution.py:201
  89.4 10.7 %collective-permute-done.7.p3 = bf16[1056,256]{1,0:T(8,128)(2,1)S(1)} collective-permute-done((bf16[1056,256]{1,0:T(8,128)(2,1)}, bf16[1056,256]{1,0:T(8,128)(2,1)S(1)}, u32[]{:S(2)}, u32[]{:S(2)}) %collective-permute-start.7) | collective-permute-done | bytes 540704 | tf_op jit(solution)/shard_map/ppermute | solution.py:201
  100.1 1.9 %collective-permute-start.8 = (f32[1,512]{1,0:T(1,128)S(1)}, f32[1,512]{1,0:T(1,128)S(1)}, u32[]{:S(2)}, u32[]{:S(2)}) collective-permute-start(f32[1,512]{1,0:T(1,128)S(1)} %shard_map.107), channel_id=1, source_target_pairs={{0,32},{32,0},{1,33},{33,1},{2,34},{34,2},{3,35},{35,3},{4,36},{36... | collective-permute-start | bytes 6152 | tf_op jit(solution)/shard_map/ppermute | solution.py:201
  102.0 1.1 collective-permute-done.8
  103.1 6.7 %collective-permute-start.9 = (f32[1,512]{1,0:T(1,128)S(1)}, f32[1,512]{1,0:T(1,128)S(1)}, u32[]{:S(2)}, u32[]{:S(2)}) collective-permute-start(f32[1,512]{1,0:T(1,128)S(1)} %add.6), channel_id=1, source_target_pairs={{0,256},{256,0},{1,257},{257,1},{2,258},{258,2},{3,259},{259,3},{4... | collective-permute-start | bytes 6152 | tf_op jit(solution)/shard_map/ppermute | solution.py:201
  109.8 0.0 copy-start
  109.8 0.0 copy-start.1
  109.8 1.1 shard_map.108
  111.0 9.8 %collective-permute-done.9 = f32[1,512]{1,0:T(1,128)S(1)} collective-permute-done((f32[1,512]{1,0:T(1,128)S(1)}, f32[1,512]{1,0:T(1,128)S(1)}, u32[]{:S(2)}, u32[]{:S(2)}) %collective-permute-start.9) | collective-permute-done | bytes 2080 | tf_op jit(solution)/shard_map/ppermute | solution.py:201
  120.7 0.6 add.7
  121.3 0.0 all-to-all-done.1
  121.3 0.0 copy-done
  121.3 0.0 copy-done.1
  121.3 1.8 %shard_map.105 = (bf16[128,512]{1,0:T(8,128)(2,1)}, bf16[128,512]{1,0:T(8,128)(2,1)}) custom-call(s32[1,128]{1,0:T(1,128)} %order_ref.3, bf16[512,512]{1,0:T(8,128)(2,1)S(1)} %bitcast.8, bf16[128,512]{1,0:T(8,128)(2,1)S(1)} %copy-done, bf16[128,512]{1,0:T(8,128)(2,1)S(1)} %copy-done.1), custom_call_target="tpu_custom_call" | custom-call | tf_op jit(solution)/shard_map/pallas_call | solution.py:190
  (5 shorter events, 0.1 us)
Async XLA Ops:
  2.8 18.9 %copy-start.3 = (bf16[1,256,512]{2,1,0:T(8,128)(2,1)S(1)}, bf16[1,256,512]{2,1,0:T(8,128)(2,1)}, u32[]{:S(2)}) copy-start(bf16[1,256,512]{2,1,0:T(8,128)(2,1)} %param.10) | copy-start | bytes 786436
  2.8 51.7 %all-to-all-start = ((bf16[64,8,512]{2,1,0:T(8,128)(2,1)}), bf16[64,8,512]{2,1,0:T(8,128)(2,1)S(1)}, u32[]{:S(2)}, u32[]{:S(2)}) async-start(bf16[64,8,512]{2,1,0:T(8,128)(2,1)} %bitcast), calls=%async_computation | async-start | bytes 1048576 | tf_op jit(solution)/shard_map/all_to_all | solution.py:223
  21.7 1.0 copy-start.4
  22.7 35.6 %copy-start.2 = (bf16[1,512]{1,0:T(2,128)(2,1)S(1)}, bf16[1,512]{1,0:T(2,128)(2,1)}, u32[]{:S(2)}) copy-start(bf16[1,512]{1,0:T(2,128)(2,1)} %centroid_ref.3) | copy-start | bytes 3076
  22.7 33.7 %collective-permute-start.3 = (bf16[1024,256]{1,0:T(8,128)(2,1)S(1)}, bf16[1024,256]{1,0:T(8,128)(2,1)S(1)}, u32[]{:S(2)}, u32[]{:S(2)}) collective-permute-start(bf16[1024,256]{1,0:T(8,128)(2,1)S(1)} %pad_maximum_fusion.s0), channel_id=1, source_target_pairs={{0,64},{64,128},{128,192},{192,0},{1,65},{65,129},{129,193},{193,1... | collective-permute-start | bytes 1572872 | tf_op jit(solution)/shard_map/ppermute | solution.py:201
  25.1 31.3 %collective-permute-start.2 = (bf16[1024,256]{1,0:T(8,128)(2,1)S(1)}, bf16[1024,256]{1,0:T(8,128)(2,1)S(1)}, u32[]{:S(2)}, u32[]{:S(2)}) collective-permute-start(bf16[1024,256]{1,0:T(8,128)(2,1)S(1)} %pad_maximum_fusion.s0), channel_id=1, source_target_pairs={{0,128},{64,192},{128,0},{192,64},{1,129},{65,193},{129,1},{193,65... | collective-permute-start | bytes 1572872 | tf_op jit(solution)/shard_map/ppermute | solution.py:201
  29.4 27.0 %collective-permute-start.1 = (bf16[1024,256]{1,0:T(8,128)(2,1)S(1)}, bf16[1024,256]{1,0:T(8,128)(2,1)S(1)}, u32[]{:S(2)}, u32[]{:S(2)}) collective-permute-start(bf16[1024,256]{1,0:T(8,128)(2,1)S(1)} %pad_maximum_fusion.s0), channel_id=1, source_target_pairs={{0,192},{64,0},{128,64},{192,128},{1,193},{65,1},{129,65},{193,129... | collective-permute-start | bytes 1572872 | tf_op jit(solution)/shard_map/ppermute | solution.py:201
  54.5 3.8 %collective-permute-start = (bf16[512,512]{1,0:T(8,128)(2,1)S(1)}, bf16[512,512]{1,0:T(8,128)(2,1)S(1)}, u32[]{:S(2)}, u32[]{:S(2)}) collective-permute-start(bf16[512,512]{1,0:T(8,128)(2,1)S(1)} %bitcast.6), channel_id=1, source_target_pairs={{0,32},{32,0},{1,33},{33,1},{2,34},{34,2},{3,35},{35,3},{4,36},{36... | collective-permute-start | bytes 1572872 | tf_op jit(solution)/shard_map/ppermute | solution.py:201
  61.0 4.7 %collective-permute-start.4 = (bf16[512,512]{1,0:T(8,128)(2,1)S(1)}, bf16[512,512]{1,0:T(8,128)(2,1)S(1)}, u32[]{:S(2)}, u32[]{:S(2)}) collective-permute-start(bf16[512,512]{1,0:T(8,128)(2,1)S(1)} %get-tuple-element.27), channel_id=1, source_target_pairs={{0,32},{32,0},{1,33},{33,1},{2,34},{34,2},{3,35},{35,3},{4,36},{36... | collective-permute-start | bytes 1572872 | tf_op jit(solution)/shard_map/ppermute | solution.py:201
  68.2 19.7 %collective-permute-start.5 = (bf16[1056,256]{1,0:T(8,128)(2,1)}, bf16[1056,256]{1,0:T(8,128)(2,1)S(1)}, u32[]{:S(2)}, u32[]{:S(2)}) collective-permute-start(bf16[1056,256]{1,0:T(8,128)(2,1)} %get-tuple-element.39), channel_id=1, source_target_pairs={{0,64},{64,128},{128,192},{192,0},{1,65},{65,129},{129,193},{193,1... | collective-permute-start | bytes 1622024 | tf_op jit(solution)/shard_map/ppermute | solution.py:201
  70.6 18.8 %collective-permute-start.6 = (bf16[1056,256]{1,0:T(8,128)(2,1)}, bf16[1056,256]{1,0:T(8,128)(2,1)S(1)}, u32[]{:S(2)}, u32[]{:S(2)}) collective-permute-start(bf16[1056,256]{1,0:T(8,128)(2,1)} %get-tuple-element.40), channel_id=1, source_target_pairs={{0,128},{64,192},{128,0},{192,64},{1,129},{65,193},{129,1},{193,65... | collective-permute-start | bytes 1622024 | tf_op jit(solution)/shard_map/ppermute | solution.py:201
  74.9 25.1 %collective-permute-start.7 = (bf16[1056,256]{1,0:T(8,128)(2,1)}, bf16[1056,256]{1,0:T(8,128)(2,1)S(1)}, u32[]{:S(2)}, u32[]{:S(2)}) collective-permute-start(bf16[1056,256]{1,0:T(8,128)(2,1)} %get-tuple-element.41), channel_id=1, source_target_pairs={{0,192},{64,0},{128,64},{192,128},{1,193},{65,1},{129,65},{193,129... | collective-permute-start | bytes 1622024 | tf_op jit(solution)/shard_map/ppermute | solution.py:201
  77.8 43.6 %all-to-all-start.1 = ((bf16[64,8,512]{2,1,0:T(8,128)(2,1)}), bf16[64,8,512]{2,1,0:T(8,128)(2,1)S(1)}, u32[]{:S(2)}, u32[]{:S(2)}) async-start(bf16[64,8,512]{2,1,0:T(8,128)(2,1)} %bitcast.4), calls=%async_computation.1 | async-start | bytes 1048576 | tf_op jit(solution)/shard_map/all_to_all | solution.py:248
  100.1 3.1 %collective-permute-start.8 = (f32[1,512]{1,0:T(1,128)S(1)}, f32[1,512]{1,0:T(1,128)S(1)}, u32[]{:S(2)}, u32[]{:S(2)}) collective-permute-start(f32[1,512]{1,0:T(1,128)S(1)} %shard_map.107), channel_id=1, source_target_pairs={{0,32},{32,0},{1,33},{33,1},{2,34},{34,2},{3,35},{35,3},{4,36},{36... | collective-permute-start | bytes 6152 | tf_op jit(solution)/shard_map/ppermute | solution.py:201
  103.1 17.6 %collective-permute-start.9 = (f32[1,512]{1,0:T(1,128)S(1)}, f32[1,512]{1,0:T(1,128)S(1)}, u32[]{:S(2)}, u32[]{:S(2)}) collective-permute-start(f32[1,512]{1,0:T(1,128)S(1)} %add.6), channel_id=1, source_target_pairs={{0,256},{256,0},{1,257},{257,1},{2,258},{258,2},{3,259},{259,3},{4... | collective-permute-start | bytes 6152 | tf_op jit(solution)/shard_map/ppermute | solution.py:201
  109.8 11.5 %copy-start = (bf16[128,512]{1,0:T(8,128)(2,1)S(1)}, bf16[128,512]{1,0:T(8,128)(2,1)}, u32[]{:S(2)}) copy-start(bf16[128,512]{1,0:T(8,128)(2,1)} %tok_ref.3) | copy-start | bytes 393220
  109.8 11.5 %copy-start.1 = (bf16[128,512]{1,0:T(8,128)(2,1)S(1)}, bf16[128,512]{1,0:T(8,128)(2,1)}, u32[]{:S(2)}) copy-start(bf16[128,512]{1,0:T(8,128)(2,1)} %grad_ref.3) | copy-start | bytes 393220

commit v9 on v8

--- a/solution.py
+++ b/solution.py
@@ -149,7 +149,12 @@
         out_ref[:, columns] = own_centroid[:, columns] + notes[0:1] + notes[1:2]
 
 
-def total_kernel(own, p1, p2, p3, first_ref, second_ref):
+def total_kernel(
+    own, p1, p2, p3, order_ref, first_ref, second_ref, pick_token_ref, pick_grad_ref, order_vmem, sem
+):
+    copy = pltpu.make_async_copy(order_ref, order_vmem, sem)
+    copy.start()
+
     def total(rows):
         return (own[rows, :].astype(F32) + p1[rows, :].astype(F32)) + (
             p2[rows, :].astype(F32) + p3[rows, :].astype(F32)
@@ -158,28 +163,28 @@
     first_ref[0] = total(slice(0, D))
     second_ref[0, :, :HALF] = total(slice(D, D + UNITS))
     second_ref[0, :, HALF:] = total(slice(D + UNITS, PACKED))
-
-
-def unpack_kernel(
-    order_ref, home_ref, tok_ref, grad_ref, layer_ref, grad_out_ref, order_vmem, sem
-):
-    copy = pltpu.make_async_copy(order_ref, order_vmem, sem)
-    copy.start()
     copy.wait()
     order = jnp.broadcast_to(order_vmem[...].astype(F32), (8, TOK)).astype(BF)
     token = iota((TOK, 2 * TOK), 0).astype(F32)
     token_pick, grad_pick = mixed_picks(TOK, True, slots=True)
     kind = (iota((TOK, 2 * TOK), 1) // BLK) % 2
-    pick_token = ((token == dot(order, token_pick)[0:1]) & (kind == 0)).astype(BF)
-    pick_grad = ((token == dot(order, grad_pick)[0:1]) & (kind == 1)).astype(BF)
+    pick_token_ref[...] = ((token == dot(order, token_pick)[0:1]) & (kind == 0)).astype(BF)
+    pick_grad_ref[...] = ((token == dot(order, grad_pick)[0:1]) & (kind == 1)).astype(BF)
+
+
+def unpack_kernel(
+    pick_token, pick_grad, home_ref, tok_ref, grad_ref, here_ref, there_ref,
+    layer_ref, grad_out_ref, centroid_grad_ref,
+):
     layer = tok_ref[...].astype(F32)
     grad = grad_ref[...].astype(F32)
     for half in range(ZH):
         rows = home_ref[half * 2 * TOK : (half + 1) * 2 * TOK, :]
-        layer += dot(pick_token, rows)
-        grad += dot(pick_grad, rows)
+        layer += dot(pick_token[...], rows)
+        grad += dot(pick_grad[...], rows)
     layer_ref[...] = layer.astype(BF)
     grad_out_ref[...] = grad.astype(BF)
+    centroid_grad_ref[...] = here_ref[...] + there_ref[...]
 
 
 def in_hbm(value):
@@ -237,7 +242,7 @@
     def weight_grads(shards, after):
         return call(
             functools.partial(weight_grad_kernel, shards),
-            [((PACKED + 2 * NOTE, UNITS), BF)] * len(shards),
+            [pltpu.VMEM((PACKED + 2 * NOTE, UNITS), BF)] * len(shards),
             *own[1:], *other[2:], after,
             in_specs=[vmem] * 9 + [any_space],
         )
@@ -250,19 +255,20 @@
     ).reshape(MIXED, D)
     (centroid_grad,) = call(note_kernel, [((1, D), F32)], own[1], *arrived)
     centroid_grad += shift(centroid_grad, "core", CORE, 1)
-    grad_centroid = centroid_grad + shift(centroid_grad, "zh", ZH, 1)
-    first_grad, second_grad = call(
+    first_grad, second_grad, *picks = call(
         total_kernel,
-        [((1, D, UNITS), F32), ((1, UNITS, D), F32)],
-        p0, *arrived,
+        [
+            ((1, D, UNITS), F32), ((1, UNITS, D), F32), ((TOK, 2 * TOK), BF), ((TOK, 2 * TOK), BF),
+        ],
+        p0, *arrived, in_hbm(slot_order),
+        in_specs=[vmem] * X + [hbm],
+        scratch_shapes=[pltpu.VMEM((1, TOK), jnp.int32), pltpu.SemaphoreType.DMA(())],
         cost_estimate=pl.CostEstimate(flops=20 * 10**9, transcendentals=0, bytes_accessed=4 * 2**20),
     )
-    layer_out, grad_tokens = call(
+    layer_out, grad_tokens, grad_centroid = call(
         unpack_kernel,
-        [((TOK, D), BF), ((TOK, D), BF)],
-        in_hbm(slot_order), home, tokens, out_grad,
-        in_specs=[hbm, vmem, vmem, vmem],
-        scratch_shapes=[pltpu.VMEM((1, TOK), jnp.int32), pltpu.SemaphoreType.DMA(())],
+        [((TOK, D), BF), ((TOK, D), BF), ((1, D), F32)],
+        *picks, home, tokens, out_grad, centroid_grad, shift(centroid_grad, "zh", ZH, 1),
     )
     return (layer_out, grad_tokens, grad_centroid, first_grad, second_grad)
 

time: 126 us -> 124 us (0.984)
  transfers between devices with their start and end apart: 12 -> 12, of which waited for: 6 -> 6; matrix products, arithmetic and copies ran while one was open for 1% -> 0% of each run, Pallas kernels for 4% -> 4%
where the time goes in v9:
time: 124 us; the launch traced here: 122 us
  starting transfers between devices  58.8 us (47%)
  waiting for transfers between devices  47.5 us (38%)
  Pallas kernels  13.6 us (11%)
    ppermute x10, starting transfers between devices, shift(): lax.ppermute(value, axis, [(i, (i + by) % size) for i in range(size)])  29.8 us
    ppermute x10, waiting for transfers between devices, shift(): lax.ppermute(value, axis, [(i, (i + by) % size) for i in range(size)])  24.3 us
    all_to_all x1, waiting for transfers between devices, on_device(): lax.all_to_all(packed.reshape(ZH * EXPERTS, 2 * BLK, D), ('zh', 'zl', 'y'...  23.1 us
    all_to_all x1, starting transfers between devices, on_device(): lax.all_to_all(packed.reshape(ZH * EXPERTS, 2 * BLK, D), ('zh', 'zl', 'y'...  18.9 us
    pallas_call x8, Pallas kernels, call(): pl.pallas_call(kernel, out_shape=[out if hasattr(out, 'memory_space') els...  13.6 us
    all_to_all x1, starting transfers between devices, on_device(): lax.all_to_all(returned.reshape(ZH * EXPERTS, 2 * BLK, D), ('zh', 'zl', '...  10.1 us
  transfers between devices with their start and end apart: 12, of which 6 were waited for; matrix products, arithmetic and copies ran while one was open for 0% of the time, Pallas kernels for 4%

profile of v9, /device:TPU:6, one launch (start us, length us, event | category | flops | bytes accessed | tf_op | source)
XLA Modules:
  0.0 121.7 jit_solution(12007185325418719425)
XLA Ops:
  0.6 2.1 %shard_map.101 = bf16[512,512]{1,0:T(8,128)(2,1)} custom-call(s32[1,128]{1,0:T(1,128)} %order_ref.3, bf16[128,512]{1,0:T(8,128)(2,1)} %tok_ref.3, bf16[128,512]{1,0:T(8,128)(2,1)} %grad_ref.3), custom_call_target="tpu_custom_call" | custom-call | tf_op jit(solution)/shard_map/pallas_call | solution.py:195
  2.8 0.0 copy-start.3
  2.8 18.9 %all-to-all-start = ((bf16[64,8,512]{2,1,0:T(8,128)(2,1)}), bf16[64,8,512]{2,1,0:T(8,128)(2,1)S(1)}, u32[]{:S(2)}, u32[]{:S(2)}) async-start(bf16[64,8,512]{2,1,0:T(8,128)(2,1)} %bitcast), calls=%async_computation | async-start | bytes 1048576 | tf_op jit(solution)/shard_map/all_to_all | solution.py:228
  21.7 0.0 copy-done.3
  21.7 0.0 copy-start.4
  21.7 0.9 copy-done.4
  22.7 0.0 copy-start.2
  22.7 2.4 %collective-permute-start.3 = (bf16[1024,256]{1,0:T(8,128)(2,1)S(1)}, bf16[1024,256]{1,0:T(8,128)(2,1)S(1)}, u32[]{:S(2)}, u32[]{:S(2)}) collective-permute-start(bf16[1024,256]{1,0:T(8,128)(2,1)S(1)} %pad_maximum_fusion.s0), channel_id=1, source_target_pairs={{0,64},{64,128},{128,192},{192,0},{1,65},{65,129},{129,193},{193,1... | collective-permute-start | bytes 1572872 | tf_op jit(solution)/shard_map/ppermute | solution.py:206
  25.1 4.3 %collective-permute-start.2 = (bf16[1024,256]{1,0:T(8,128)(2,1)S(1)}, bf16[1024,256]{1,0:T(8,128)(2,1)S(1)}, u32[]{:S(2)}, u32[]{:S(2)}) collective-permute-start(bf16[1024,256]{1,0:T(8,128)(2,1)S(1)} %pad_maximum_fusion.s0), channel_id=1, source_target_pairs={{0,128},{64,192},{128,0},{192,64},{1,129},{65,193},{129,1},{193,65... | collective-permute-start | bytes 1572872 | tf_op jit(solution)/shard_map/ppermute | solution.py:206
  29.4 1.9 %collective-permute-start.1 = (bf16[1024,256]{1,0:T(8,128)(2,1)S(1)}, bf16[1024,256]{1,0:T(8,128)(2,1)S(1)}, u32[]{:S(2)}, u32[]{:S(2)}) collective-permute-start(bf16[1024,256]{1,0:T(8,128)(2,1)S(1)} %pad_maximum_fusion.s0), channel_id=1, source_target_pairs={{0,192},{64,0},{128,64},{192,128},{1,193},{65,1},{129,65},{193,129... | collective-permute-start | bytes 1572872 | tf_op jit(solution)/shard_map/ppermute | solution.py:206
  31.3 23.1 %all-to-all-done = bf16[64,8,512]{2,1,0:T(8,128)(2,1)S(1)} async-done(((bf16[64,8,512]{2,1,0:T(8,128)(2,1)}), bf16[64,8,512]{2,1,0:T(8,128)(2,1)S(1)}, u32[]{:S(2)}, u32[]{:S(2)}) %all-to-all-start) | async-done | bytes 524320 | tf_op jit(solution)/shard_map/all_to_all | solution.py:228
  54.5 1.9 %collective-permute-start = (bf16[512,512]{1,0:T(8,128)(2,1)S(1)}, bf16[512,512]{1,0:T(8,128)(2,1)S(1)}, u32[]{:S(2)}, u32[]{:S(2)}) collective-permute-start(bf16[512,512]{1,0:T(8,128)(2,1)S(1)} %bitcast.6), channel_id=1, source_target_pairs={{0,32},{32,0},{1,33},{33,1},{2,34},{34,2},{3,35},{35,3},{4,36},{36... | collective-permute-start | bytes 1572872 | tf_op jit(solution)/shard_map/ppermute | solution.py:206
  56.4 0.0 collective-permute-done.3.s3
  56.4 0.0 collective-permute-done.2.s2
  56.4 0.0 collective-permute-done.1.s1
  56.4 1.8 %collective-permute-done.rows_ref = bf16[512,512]{1,0:T(8,128)(2,1)S(1)} collective-permute-done((bf16[512,512]{1,0:T(8,128)(2,1)S(1)}, bf16[512,512]{1,0:T(8,128)(2,1)S(1)}, u32[]{:S(2)}, u32[]{:S(2)}) %collective-permute-start) | collective-permute-done | bytes 524320 | tf_op jit(solution)/shard_map/ppermute | solution.py:206
  58.3 0.0 copy-done.2
  58.3 2.7 %shard_map.102 = (bf16[512,512]{1,0:T(8,128)(2,1)S(1)}, f32[1,512]{1,0:T(1,128)S(1)}, bf16[256,512]{1,0:T(8,128)(2,1)S(1)}, bf16[256,512]{1,0:T(8,128)(2,1)S(1)}...) custom-call(bf16[512,512]{1,0:T(8,128)(2,1)S(1)} %collective-permute-done.rows_ref, ...), custom_call_target="tpu_custom_call" | custom-call | tf_op jit(solution)/shard_map/pallas_call | solution.py:195
  61.0 2.0 %collective-permute-start.4 = (bf16[512,512]{1,0:T(8,128)(2,1)S(1)}, bf16[512,512]{1,0:T(8,128)(2,1)S(1)}, u32[]{:S(2)}, u32[]{:S(2)}) collective-permute-start(bf16[512,512]{1,0:T(8,128)(2,1)S(1)} %get-tuple-element.38), channel_id=1, source_target_pairs={{0,32},{32,0},{1,33},{33,1},{2,34},{34,2},{3,35},{35,3},{4,36},{36... | collective-permute-start | bytes 1572872 | tf_op jit(solution)/shard_map/ppermute | solution.py:206
  63.0 2.7 %shard_map.103 = (bf16[512,512]{1,0:T(8,128)(2,1)S(1)}, f32[1,512]{1,0:T(1,128)S(1)}, bf16[256,512]{1,0:T(8,128)(2,1)S(1)}, bf16[256,512]{1,0:T(8,128)(2,1)S(1)}...) custom-call(bf16[512,512]{1,0:T(8,128)(2,1)S(1)} %bitcast.7, bf16[1,512]{1,0:T(2,128)(2,1)S(1)} %copy-done.2, ...), custom_call_target="tpu_custom_call" | custom-call | tf_op jit(solution)/shard_map/pallas_call | solution.py:195
  65.7 0.0 collective-permute-done.4.after_ref.other_ref
  65.7 2.5 %shard_map.104 = (bf16[1056,256]{1,0:T(8,128)(2,1)}, bf16[1056,256]{1,0:T(8,128)(2,1)}, bf16[1056,256]{1,0:T(8,128)(2,1)}, bf16[1056,256]{1,0:T(8,128)(2,1)S(1)}) custom-call(f32[1,512]{1,0:T(1,128)S(1)} %get-tuple-element.29.centroid_ref.own_centroid, bf16[256,512]{1,0:T(8,128)(2,1)S(1)} %get-tuple-element.30.routed_a, ...), custom_call_target="tpu_custom_call" | custom-call | tf_op jit(solution)/shard_map/pallas_call | solution.py:195
  68.2 2.4 %collective-permute-start.5 = (bf16[1056,256]{1,0:T(8,128)(2,1)}, bf16[1056,256]{1,0:T(8,128)(2,1)S(1)}, u32[]{:S(2)}, u32[]{:S(2)}) collective-permute-start(bf16[1056,256]{1,0:T(8,128)(2,1)} %get-tuple-element.40), channel_id=1, source_target_pairs={{0,64},{64,128},{128,192},{192,0},{1,65},{65,129},{129,193},{193,1... | collective-permute-start | bytes 1622024 | tf_op jit(solution)/shard_map/ppermute | solution.py:206
  70.6 4.3 %collective-permute-start.6 = (bf16[1056,256]{1,0:T(8,128)(2,1)}, bf16[1056,256]{1,0:T(8,128)(2,1)S(1)}, u32[]{:S(2)}, u32[]{:S(2)}) collective-permute-start(bf16[1056,256]{1,0:T(8,128)(2,1)} %get-tuple-element.41), channel_id=1, source_target_pairs={{0,128},{64,192},{128,0},{192,64},{1,129},{65,193},{129,1},{193,65... | collective-permute-start | bytes 1622024 | tf_op jit(solution)/shard_map/ppermute | solution.py:206
  74.9 1.9 %collective-permute-start.7 = (bf16[1056,256]{1,0:T(8,128)(2,1)}, bf16[1056,256]{1,0:T(8,128)(2,1)S(1)}, u32[]{:S(2)}, u32[]{:S(2)}) collective-permute-start(bf16[1056,256]{1,0:T(8,128)(2,1)} %get-tuple-element.42), channel_id=1, source_target_pairs={{0,192},{64,0},{128,64},{192,128},{1,193},{65,1},{129,65},{193,129... | collective-permute-start | bytes 1622024 | tf_op jit(solution)/shard_map/ppermute | solution.py:206
  76.9 0.9 shard_map.106
  77.8 10.1 %all-to-all-start.1 = ((bf16[64,8,512]{2,1,0:T(8,128)(2,1)}), bf16[64,8,512]{2,1,0:T(8,128)(2,1)S(1)}, u32[]{:S(2)}, u32[]{:S(2)}) async-start(bf16[64,8,512]{2,1,0:T(8,128)(2,1)} %bitcast.4), calls=%async_computation.1 | async-start | bytes 1048576 | tf_op jit(solution)/shard_map/all_to_all | solution.py:253
  87.9 0.0 collective-permute-done.5.p1
  87.9 1.4 %collective-permute-done.6.p2 = bf16[1056,256]{1,0:T(8,128)(2,1)S(1)} collective-permute-done((bf16[1056,256]{1,0:T(8,128)(2,1)}, bf16[1056,256]{1,0:T(8,128)(2,1)S(1)}, u32[]{:S(2)}, u32[]{:S(2)}) %collective-permute-start.6) | collective-permute-done | bytes 540704 | tf_op jit(solution)/shard_map/ppermute | solution.py:206
  89.4 10.7 %collective-permute-done.7.p3 = bf16[1056,256]{1,0:T(8,128)(2,1)S(1)} collective-permute-done((bf16[1056,256]{1,0:T(8,128)(2,1)}, bf16[1056,256]{1,0:T(8,128)(2,1)S(1)}, u32[]{:S(2)}, u32[]{:S(2)}) %collective-permute-start.7) | collective-permute-done | bytes 540704 | tf_op jit(solution)/shard_map/ppermute | solution.py:206
  100.1 1.9 %collective-permute-start.8 = (f32[1,512]{1,0:T(1,128)S(1)}, f32[1,512]{1,0:T(1,128)S(1)}, u32[]{:S(2)}, u32[]{:S(2)}) collective-permute-start(f32[1,512]{1,0:T(1,128)S(1)} %shard_map.107), channel_id=1, source_target_pairs={{0,32},{32,0},{1,33},{33,1},{2,34},{34,2},{3,35},{35,3},{4,36},{36... | collective-permute-start | bytes 6152 | tf_op jit(solution)/shard_map/ppermute | solution.py:206
  102.0 1.1 collective-permute-done.8
  103.1 6.7 %collective-permute-start.9 = (f32[1,512]{1,0:T(1,128)S(1)}, f32[1,512]{1,0:T(1,128)S(1)}, u32[]{:S(2)}, u32[]{:S(2)}) collective-permute-start(f32[1,512]{1,0:T(1,128)S(1)} %add.3.here_ref), channel_id=1, source_target_pairs={{0,256},{256,0},{1,257},{257,1},{2,258},{258,2},{3,259},{259,3},{4... | collective-permute-start | bytes 6152 | tf_op jit(solution)/shard_map/ppermute | solution.py:206
  109.8 0.0 copy-start
  109.8 0.0 copy-start.1
  109.8 1.7 %shard_map.105 = (f32[1,512,256]{2,1,0:T(8,128)}, f32[1,256,512]{2,1,0:T(8,128)}, bf16[128,256]{1,0:T(8,128)(2,1)S(1)}, bf16[128,256]{1,0:T(8,128)(2,1)S(1)}) custom-call(bf16[1056,256]{1,0:T(8,128)(2,1)S(1)} %get-tuple-element.39.own, bf16[1056,256]{1,0:T(8,128)(2,1)S(1)} %collective-permute-done.5.p1, bf16[1056,256]{1,0:T(8,128)(2,1)S(1)} %collective-permute-done.6.p2, ...), custom_call_target="tpu_custom_call" | custom-call | flops 20000000000 | bytes 4194304 | tf_op jit(solution)/shard_map/pallas_call | solution.py:195
  111.5 9.2 %collective-permute-done.9.there_ref = f32[1,512]{1,0:T(1,128)S(1)} collective-permute-done((f32[1,512]{1,0:T(1,128)S(1)}, f32[1,512]{1,0:T(1,128)S(1)}, u32[]{:S(2)}, u32[]{:S(2)}) %collective-permute-start.9) | collective-permute-done | bytes 2080 | tf_op jit(solution)/shard_map/ppermute | solution.py:206
  120.7 0.0 all-to-all-done.1
  120.7 0.0 copy-done
  120.7 0.0 copy-done.1
  120.7 1.0 shard_map.108
  (5 shorter events, 0.1 us)
Async XLA Ops:
  2.8 18.9 %copy-start.3 = (bf16[1,256,512]{2,1,0:T(8,128)(2,1)S(1)}, bf16[1,256,512]{2,1,0:T(8,128)(2,1)}, u32[]{:S(2)}) copy-start(bf16[1,256,512]{2,1,0:T(8,128)(2,1)} %param.10) | copy-start | bytes 786436
  2.8 51.7 %all-to-all-start = ((bf16[64,8,512]{2,1,0:T(8,128)(2,1)}), bf16[64,8,512]{2,1,0:T(8,128)(2,1)S(1)}, u32[]{:S(2)}, u32[]{:S(2)}) async-start(bf16[64,8,512]{2,1,0:T(8,128)(2,1)} %bitcast), calls=%async_computation | async-start | bytes 1048576 | tf_op jit(solution)/shard_map/all_to_all | solution.py:228
  21.7 1.0 copy-start.4
  22.7 35.6 %copy-start.2 = (bf16[1,512]{1,0:T(2,128)(2,1)S(1)}, bf16[1,512]{1,0:T(2,128)(2,1)}, u32[]{:S(2)}) copy-start(bf16[1,512]{1,0:T(2,128)(2,1)} %centroid_ref.3) | copy-start | bytes 3076
  22.7 33.7 %collective-permute-start.3 = (bf16[1024,256]{1,0:T(8,128)(2,1)S(1)}, bf16[1024,256]{1,0:T(8,128)(2,1)S(1)}, u32[]{:S(2)}, u32[]{:S(2)}) collective-permute-start(bf16[1024,256]{1,0:T(8,128)(2,1)S(1)} %pad_maximum_fusion.s0), channel_id=1, source_target_pairs={{0,64},{64,128},{128,192},{192,0},{1,65},{65,129},{129,193},{193,1... | collective-permute-start | bytes 1572872 | tf_op jit(solution)/shard_map/ppermute | solution.py:206
  25.1 31.3 %collective-permute-start.2 = (bf16[1024,256]{1,0:T(8,128)(2,1)S(1)}, bf16[1024,256]{1,0:T(8,128)(2,1)S(1)}, u32[]{:S(2)}, u32[]{:S(2)}) collective-permute-start(bf16[1024,256]{1,0:T(8,128)(2,1)S(1)} %pad_maximum_fusion.s0), channel_id=1, source_target_pairs={{0,128},{64,192},{128,0},{192,64},{1,129},{65,193},{129,1},{193,65... | collective-permute-start | bytes 1572872 | tf_op jit(solution)/shard_map/ppermute | solution.py:206
  29.4 27.0 %collective-permute-start.1 = (bf16[1024,256]{1,0:T(8,128)(2,1)S(1)}, bf16[1024,256]{1,0:T(8,128)(2,1)S(1)}, u32[]{:S(2)}, u32[]{:S(2)}) collective-permute-start(bf16[1024,256]{1,0:T(8,128)(2,1)S(1)} %pad_maximum_fusion.s0), channel_id=1, source_target_pairs={{0,192},{64,0},{128,64},{192,128},{1,193},{65,1},{129,65},{193,129... | collective-permute-start | bytes 1572872 | tf_op jit(solution)/shard_map/ppermute | solution.py:206
  54.5 3.8 %collective-permute-start = (bf16[512,512]{1,0:T(8,128)(2,1)S(1)}, bf16[512,512]{1,0:T(8,128)(2,1)S(1)}, u32[]{:S(2)}, u32[]{:S(2)}) collective-permute-start(bf16[512,512]{1,0:T(8,128)(2,1)S(1)} %bitcast.6), channel_id=1, source_target_pairs={{0,32},{32,0},{1,33},{33,1},{2,34},{34,2},{3,35},{35,3},{4,36},{36... | collective-permute-start | bytes 1572872 | tf_op jit(solution)/shard_map/ppermute | solution.py:206
  61.0 4.7 %collective-permute-start.4 = (bf16[512,512]{1,0:T(8,128)(2,1)S(1)}, bf16[512,512]{1,0:T(8,128)(2,1)S(1)}, u32[]{:S(2)}, u32[]{:S(2)}) collective-permute-start(bf16[512,512]{1,0:T(8,128)(2,1)S(1)} %get-tuple-element.38), channel_id=1, source_target_pairs={{0,32},{32,0},{1,33},{33,1},{2,34},{34,2},{3,35},{35,3},{4,36},{36... | collective-permute-start | bytes 1572872 | tf_op jit(solution)/shard_map/ppermute | solution.py:206
  68.2 19.7 %collective-permute-start.5 = (bf16[1056,256]{1,0:T(8,128)(2,1)}, bf16[1056,256]{1,0:T(8,128)(2,1)S(1)}, u32[]{:S(2)}, u32[]{:S(2)}) collective-permute-start(bf16[1056,256]{1,0:T(8,128)(2,1)} %get-tuple-element.40), channel_id=1, source_target_pairs={{0,64},{64,128},{128,192},{192,0},{1,65},{65,129},{129,193},{193,1... | collective-permute-start | bytes 1622024 | tf_op jit(solution)/shard_map/ppermute | solution.py:206
  70.6 18.8 %collective-permute-start.6 = (bf16[1056,256]{1,0:T(8,128)(2,1)}, bf16[1056,256]{1,0:T(8,128)(2,1)S(1)}, u32[]{:S(2)}, u32[]{:S(2)}) collective-permute-start(bf16[1056,256]{1,0:T(8,128)(2,1)} %get-tuple-element.41), channel_id=1, source_target_pairs={{0,128},{64,192},{128,0},{192,64},{1,129},{65,193},{129,1},{193,65... | collective-permute-start | bytes 1622024 | tf_op jit(solution)/shard_map/ppermute | solution.py:206
  74.9 25.1 %collective-permute-start.7 = (bf16[1056,256]{1,0:T(8,128)(2,1)}, bf16[1056,256]{1,0:T(8,128)(2,1)S(1)}, u32[]{:S(2)}, u32[]{:S(2)}) collective-permute-start(bf16[1056,256]{1,0:T(8,128)(2,1)} %get-tuple-element.42), channel_id=1, source_target_pairs={{0,192},{64,0},{128,64},{192,128},{1,193},{65,1},{129,65},{193,129... | collective-permute-start | bytes 1622024 | tf_op jit(solution)/shard_map/ppermute | solution.py:206
  77.8 43.0 %all-to-all-start.1 = ((bf16[64,8,512]{2,1,0:T(8,128)(2,1)}), bf16[64,8,512]{2,1,0:T(8,128)(2,1)S(1)}, u32[]{:S(2)}, u32[]{:S(2)}) async-start(bf16[64,8,512]{2,1,0:T(8,128)(2,1)} %bitcast.4), calls=%async_computation.1 | async-start | bytes 1048576 | tf_op jit(solution)/shard_map/all_to_all | solution.py:253
  100.1 3.1 %collective-permute-start.8 = (f32[1,512]{1,0:T(1,128)S(1)}, f32[1,512]{1,0:T(1,128)S(1)}, u32[]{:S(2)}, u32[]{:S(2)}) collective-permute-start(f32[1,512]{1,0:T(1,128)S(1)} %shard_map.107), channel_id=1, source_target_pairs={{0,32},{32,0},{1,33},{33,1},{2,34},{34,2},{3,35},{35,3},{4,36},{36... | collective-permute-start | bytes 6152 | tf_op jit(solution)/shard_map/ppermute | solution.py:206
  103.1 17.6 %collective-permute-start.9 = (f32[1,512]{1,0:T(1,128)S(1)}, f32[1,512]{1,0:T(1,128)S(1)}, u32[]{:S(2)}, u32[]{:S(2)}) collective-permute-start(f32[1,512]{1,0:T(1,128)S(1)} %add.3.here_ref), channel_id=1, source_target_pairs={{0,256},{256,0},{1,257},{257,1},{2,258},{258,2},{3,259},{259,3},{4... | collective-permute-start | bytes 6152 | tf_op jit(solution)/shard_map/ppermute | solution.py:206
  109.8 10.9 %copy-start = (bf16[128,512]{1,0:T(8,128)(2,1)S(1)}, bf16[128,512]{1,0:T(8,128)(2,1)}, u32[]{:S(2)}) copy-start(bf16[128,512]{1,0:T(8,128)(2,1)} %tok_ref.3) | copy-start | bytes 393220
  109.8 10.9 %copy-start.1 = (bf16[128,512]{1,0:T(8,128)(2,1)S(1)}, bf16[128,512]{1,0:T(8,128)(2,1)}, u32[]{:S(2)}) copy-start(bf16[128,512]{1,0:T(8,128)(2,1)} %grad_ref.3) | copy-start | bytes 393220

commit v10 on v9

--- a/solution.py
+++ b/solution.py
@@ -247,7 +247,7 @@
             in_specs=[vmem] * 9 + [any_space],
         )
 
-    (returned,) = call(join_kernel, [((MIXED, D), BF)], own[0], from_other)
+    (returned,) = call(join_kernel, [pltpu.VMEM((MIXED, D), BF)], own[0], from_other)
     p2, p1, p3, p0 = weight_grads((2, 1, 3, 0), from_other)
     arrived = [shift(p1, "x", X, 1), shift(p2, "x", X, 2), shift(p3, "x", X, 3)]
     home = lax.all_to_all(

time: 124 us -> 124 us (level)
  no operation moved by 1% of the time
where the time goes in v10:
time: 124 us; the launch traced here: 122 us
  starting transfers between devices  58.8 us (47%)
  waiting for transfers between devices  47.5 us (38%)
  Pallas kernels  13.6 us (11%)
    ppermute x10, starting transfers between devices, shift(): lax.ppermute(value, axis, [(i, (i + by) % size) for i in range(size)])  29.8 us
    ppermute x10, waiting for transfers between devices, shift(): lax.ppermute(value, axis, [(i, (i + by) % size) for i in range(size)])  24.3 us
    all_to_all x1, waiting for transfers between devices, on_device(): lax.all_to_all(packed.reshape(ZH * EXPERTS, 2 * BLK, D), ('zh', 'zl', 'y'...  23.1 us
    all_to_all x1, starting transfers between devices, on_device(): lax.all_to_all(packed.reshape(ZH * EXPERTS, 2 * BLK, D), ('zh', 'zl', 'y'...  18.9 us
    pallas_call x8, Pallas kernels, call(): pl.pallas_call(kernel, out_shape=[out if hasattr(out, 'memory_space') els...  13.6 us
    all_to_all x1, starting transfers between devices, on_device(): lax.all_to_all(returned.reshape(ZH * EXPERTS, 2 * BLK, D), ('zh', 'zl', '...  10.1 us
  transfers between devices with their start and end apart: 12, of which 6 were waited for; matrix products, arithmetic and copies ran while one was open for 0% of the time, Pallas kernels for 4%

profile of v10, /device:TPU:6, one launch (start us, length us, event | category | flops | bytes accessed | tf_op | source)
XLA Modules:
  0.0 121.7 jit_solution(12007185325418719425)
XLA Ops:
  0.6 2.1 %shard_map.101 = bf16[512,512]{1,0:T(8,128)(2,1)} custom-call(s32[1,128]{1,0:T(1,128)} %order_ref.3, bf16[128,512]{1,0:T(8,128)(2,1)} %tok_ref.3, bf16[128,512]{1,0:T(8,128)(2,1)} %grad_ref.3), custom_call_target="tpu_custom_call" | custom-call | tf_op jit(solution)/shard_map/pallas_call | solution.py:195
  2.8 0.0 copy-start.3
  2.8 18.9 %all-to-all-start = ((bf16[64,8,512]{2,1,0:T(8,128)(2,1)}), bf16[64,8,512]{2,1,0:T(8,128)(2,1)S(1)}, u32[]{:S(2)}, u32[]{:S(2)}) async-start(bf16[64,8,512]{2,1,0:T(8,128)(2,1)} %bitcast), calls=%async_computation | async-start | bytes 1048576 | tf_op jit(solution)/shard_map/all_to_all | solution.py:228
  21.7 0.0 copy-done.3
  21.7 0.0 copy-start.4
  21.7 0.9 copy-done.4
  22.7 0.0 copy-start.2
  22.7 2.4 %collective-permute-start.3 = (bf16[1024,256]{1,0:T(8,128)(2,1)S(1)}, bf16[1024,256]{1,0:T(8,128)(2,1)S(1)}, u32[]{:S(2)}, u32[]{:S(2)}) collective-permute-start(bf16[1024,256]{1,0:T(8,128)(2,1)S(1)} %pad_maximum_fusion.s0), channel_id=1, source_target_pairs={{0,64},{64,128},{128,192},{192,0},{1,65},{65,129},{129,193},{193,1... | collective-permute-start | bytes 1572872 | tf_op jit(solution)/shard_map/ppermute | solution.py:206
  25.1 4.3 %collective-permute-start.2 = (bf16[1024,256]{1,0:T(8,128)(2,1)S(1)}, bf16[1024,256]{1,0:T(8,128)(2,1)S(1)}, u32[]{:S(2)}, u32[]{:S(2)}) collective-permute-start(bf16[1024,256]{1,0:T(8,128)(2,1)S(1)} %pad_maximum_fusion.s0), channel_id=1, source_target_pairs={{0,128},{64,192},{128,0},{192,64},{1,129},{65,193},{129,1},{193,65... | collective-permute-start | bytes 1572872 | tf_op jit(solution)/shard_map/ppermute | solution.py:206
  29.4 1.9 %collective-permute-start.1 = (bf16[1024,256]{1,0:T(8,128)(2,1)S(1)}, bf16[1024,256]{1,0:T(8,128)(2,1)S(1)}, u32[]{:S(2)}, u32[]{:S(2)}) collective-permute-start(bf16[1024,256]{1,0:T(8,128)(2,1)S(1)} %pad_maximum_fusion.s0), channel_id=1, source_target_pairs={{0,192},{64,0},{128,64},{192,128},{1,193},{65,1},{129,65},{193,129... | collective-permute-start | bytes 1572872 | tf_op jit(solution)/shard_map/ppermute | solution.py:206
  31.3 23.1 %all-to-all-done = bf16[64,8,512]{2,1,0:T(8,128)(2,1)S(1)} async-done(((bf16[64,8,512]{2,1,0:T(8,128)(2,1)}), bf16[64,8,512]{2,1,0:T(8,128)(2,1)S(1)}, u32[]{:S(2)}, u32[]{:S(2)}) %all-to-all-start) | async-done | bytes 524320 | tf_op jit(solution)/shard_map/all_to_all | solution.py:228
  54.5 1.9 %collective-permute-start = (bf16[512,512]{1,0:T(8,128)(2,1)S(1)}, bf16[512,512]{1,0:T(8,128)(2,1)S(1)}, u32[]{:S(2)}, u32[]{:S(2)}) collective-permute-start(bf16[512,512]{1,0:T(8,128)(2,1)S(1)} %bitcast.6), channel_id=1, source_target_pairs={{0,32},{32,0},{1,33},{33,1},{2,34},{34,2},{3,35},{35,3},{4,36},{36... | collective-permute-start | bytes 1572872 | tf_op jit(solution)/shard_map/ppermute | solution.py:206
  56.4 0.0 collective-permute-done.3.s3
  56.4 0.0 collective-permute-done.2.s2
  56.4 0.0 collective-permute-done.1.s1
  56.4 1.8 %collective-permute-done.rows_ref = bf16[512,512]{1,0:T(8,128)(2,1)S(1)} collective-permute-done((bf16[512,512]{1,0:T(8,128)(2,1)S(1)}, bf16[512,512]{1,0:T(8,128)(2,1)S(1)}, u32[]{:S(2)}, u32[]{:S(2)}) %collective-permute-start) | collective-permute-done | bytes 524320 | tf_op jit(solution)/shard_map/ppermute | solution.py:206
  58.3 0.0 copy-done.2
  58.3 2.7 %shard_map.102 = (bf16[512,512]{1,0:T(8,128)(2,1)S(1)}, f32[1,512]{1,0:T(1,128)S(1)}, bf16[256,512]{1,0:T(8,128)(2,1)S(1)}, bf16[256,512]{1,0:T(8,128)(2,1)S(1)}...) custom-call(bf16[512,512]{1,0:T(8,128)(2,1)S(1)} %collective-permute-done.rows_ref, ...), custom_call_target="tpu_custom_call" | custom-call | tf_op jit(solution)/shard_map/pallas_call | solution.py:195
  61.0 2.0 %collective-permute-start.4 = (bf16[512,512]{1,0:T(8,128)(2,1)S(1)}, bf16[512,512]{1,0:T(8,128)(2,1)S(1)}, u32[]{:S(2)}, u32[]{:S(2)}) collective-permute-start(bf16[512,512]{1,0:T(8,128)(2,1)S(1)} %get-tuple-element.38), channel_id=1, source_target_pairs={{0,32},{32,0},{1,33},{33,1},{2,34},{34,2},{3,35},{35,3},{4,36},{36... | collective-permute-start | bytes 1572872 | tf_op jit(solution)/shard_map/ppermute | solution.py:206
  63.0 2.7 %shard_map.103 = (bf16[512,512]{1,0:T(8,128)(2,1)S(1)}, f32[1,512]{1,0:T(1,128)S(1)}, bf16[256,512]{1,0:T(8,128)(2,1)S(1)}, bf16[256,512]{1,0:T(8,128)(2,1)S(1)}...) custom-call(bf16[512,512]{1,0:T(8,128)(2,1)S(1)} %bitcast.7, bf16[1,512]{1,0:T(2,128)(2,1)S(1)} %copy-done.2, ...), custom_call_target="tpu_custom_call" | custom-call | tf_op jit(solution)/shard_map/pallas_call | solution.py:195
  65.7 0.0 collective-permute-done.4.after_ref.other_ref
  65.7 2.5 %shard_map.104 = (bf16[1056,256]{1,0:T(8,128)(2,1)}, bf16[1056,256]{1,0:T(8,128)(2,1)}, bf16[1056,256]{1,0:T(8,128)(2,1)}, bf16[1056,256]{1,0:T(8,128)(2,1)S(1)}) custom-call(f32[1,512]{1,0:T(1,128)S(1)} %get-tuple-element.29.centroid_ref.own_centroid, bf16[256,512]{1,0:T(8,128)(2,1)S(1)} %get-tuple-element.30.routed_a, ...), custom_call_target="tpu_custom_call" | custom-call | tf_op jit(solution)/shard_map/pallas_call | solution.py:195
  68.2 2.4 %collective-permute-start.5 = (bf16[1056,256]{1,0:T(8,128)(2,1)}, bf16[1056,256]{1,0:T(8,128)(2,1)S(1)}, u32[]{:S(2)}, u32[]{:S(2)}) collective-permute-start(bf16[1056,256]{1,0:T(8,128)(2,1)} %get-tuple-element.40), channel_id=1, source_target_pairs={{0,64},{64,128},{128,192},{192,0},{1,65},{65,129},{129,193},{193,1... | collective-permute-start | bytes 1622024 | tf_op jit(solution)/shard_map/ppermute | solution.py:206
  70.6 4.3 %collective-permute-start.6 = (bf16[1056,256]{1,0:T(8,128)(2,1)}, bf16[1056,256]{1,0:T(8,128)(2,1)S(1)}, u32[]{:S(2)}, u32[]{:S(2)}) collective-permute-start(bf16[1056,256]{1,0:T(8,128)(2,1)} %get-tuple-element.41), channel_id=1, source_target_pairs={{0,128},{64,192},{128,0},{192,64},{1,129},{65,193},{129,1},{193,65... | collective-permute-start | bytes 1622024 | tf_op jit(solution)/shard_map/ppermute | solution.py:206
  74.9 1.9 %collective-permute-start.7 = (bf16[1056,256]{1,0:T(8,128)(2,1)}, bf16[1056,256]{1,0:T(8,128)(2,1)S(1)}, u32[]{:S(2)}, u32[]{:S(2)}) collective-permute-start(bf16[1056,256]{1,0:T(8,128)(2,1)} %get-tuple-element.42), channel_id=1, source_target_pairs={{0,192},{64,0},{128,64},{192,128},{1,193},{65,1},{129,65},{193,129... | collective-permute-start | bytes 1622024 | tf_op jit(solution)/shard_map/ppermute | solution.py:206
  76.9 0.9 shard_map.106
  77.8 10.1 %all-to-all-start.1 = ((bf16[64,8,512]{2,1,0:T(8,128)(2,1)}), bf16[64,8,512]{2,1,0:T(8,128)(2,1)S(1)}, u32[]{:S(2)}, u32[]{:S(2)}) async-start(bf16[64,8,512]{2,1,0:T(8,128)(2,1)} %bitcast.4), calls=%async_computation.1 | async-start | bytes 1048576 | tf_op jit(solution)/shard_map/all_to_all | solution.py:253
  87.9 0.0 collective-permute-done.5.p1
  87.9 1.4 %collective-permute-done.6.p2 = bf16[1056,256]{1,0:T(8,128)(2,1)S(1)} collective-permute-done((bf16[1056,256]{1,0:T(8,128)(2,1)}, bf16[1056,256]{1,0:T(8,128)(2,1)S(1)}, u32[]{:S(2)}, u32[]{:S(2)}) %collective-permute-start.6) | collective-permute-done | bytes 540704 | tf_op jit(solution)/shard_map/ppermute | solution.py:206
  89.4 10.7 %collective-permute-done.7.p3 = bf16[1056,256]{1,0:T(8,128)(2,1)S(1)} collective-permute-done((bf16[1056,256]{1,0:T(8,128)(2,1)}, bf16[1056,256]{1,0:T(8,128)(2,1)S(1)}, u32[]{:S(2)}, u32[]{:S(2)}) %collective-permute-start.7) | collective-permute-done | bytes 540704 | tf_op jit(solution)/shard_map/ppermute | solution.py:206
  100.1 1.9 %collective-permute-start.8 = (f32[1,512]{1,0:T(1,128)S(1)}, f32[1,512]{1,0:T(1,128)S(1)}, u32[]{:S(2)}, u32[]{:S(2)}) collective-permute-start(f32[1,512]{1,0:T(1,128)S(1)} %shard_map.107), channel_id=1, source_target_pairs={{0,32},{32,0},{1,33},{33,1},{2,34},{34,2},{3,35},{35,3},{4,36},{36... | collective-permute-start | bytes 6152 | tf_op jit(solution)/shard_map/ppermute | solution.py:206
  102.0 1.1 collective-permute-done.8
  103.1 6.7 %collective-permute-start.9 = (f32[1,512]{1,0:T(1,128)S(1)}, f32[1,512]{1,0:T(1,128)S(1)}, u32[]{:S(2)}, u32[]{:S(2)}) collective-permute-start(f32[1,512]{1,0:T(1,128)S(1)} %add.3.here_ref), channel_id=1, source_target_pairs={{0,256},{256,0},{1,257},{257,1},{2,258},{258,2},{3,259},{259,3},{4... | collective-permute-start | bytes 6152 | tf_op jit(solution)/shard_map/ppermute | solution.py:206
  109.8 0.0 copy-start
  109.8 0.0 copy-start.1
  109.8 1.7 %shard_map.105 = (f32[1,512,256]{2,1,0:T(8,128)}, f32[1,256,512]{2,1,0:T(8,128)}, bf16[128,256]{1,0:T(8,128)(2,1)S(1)}, bf16[128,256]{1,0:T(8,128)(2,1)S(1)}) custom-call(bf16[1056,256]{1,0:T(8,128)(2,1)S(1)} %get-tuple-element.39.own, bf16[1056,256]{1,0:T(8,128)(2,1)S(1)} %collective-permute-done.5.p1, bf16[1056,256]{1,0:T(8,128)(2,1)S(1)} %collective-permute-done.6.p2, ...), custom_call_target="tpu_custom_call" | custom-call | flops 20000000000 | bytes 4194304 | tf_op jit(solution)/shard_map/pallas_call | solution.py:195
  111.5 9.2 %collective-permute-done.9.there_ref = f32[1,512]{1,0:T(1,128)S(1)} collective-permute-done((f32[1,512]{1,0:T(1,128)S(1)}, f32[1,512]{1,0:T(1,128)S(1)}, u32[]{:S(2)}, u32[]{:S(2)}) %collective-permute-start.9) | collective-permute-done | bytes 2080 | tf_op jit(solution)/shard_map/ppermute | solution.py:206
  120.7 0.0 all-to-all-done.1
  120.7 0.0 copy-done
  120.7 0.0 copy-done.1
  120.7 1.0 shard_map.108
  (5 shorter events, 0.1 us)
Async XLA Ops:
  2.8 18.9 %copy-start.3 = (bf16[1,256,512]{2,1,0:T(8,128)(2,1)S(1)}, bf16[1,256,512]{2,1,0:T(8,128)(2,1)}, u32[]{:S(2)}) copy-start(bf16[1,256,512]{2,1,0:T(8,128)(2,1)} %param.10) | copy-start | bytes 786436
  2.8 51.7 %all-to-all-start = ((bf16[64,8,512]{2,1,0:T(8,128)(2,1)}), bf16[64,8,512]{2,1,0:T(8,128)(2,1)S(1)}, u32[]{:S(2)}, u32[]{:S(2)}) async-start(bf16[64,8,512]{2,1,0:T(8,128)(2,1)} %bitcast), calls=%async_computation | async-start | bytes 1048576 | tf_op jit(solution)/shard_map/all_to_all | solution.py:228
  21.7 1.0 copy-start.4
  22.7 35.6 %copy-start.2 = (bf16[1,512]{1,0:T(2,128)(2,1)S(1)}, bf16[1,512]{1,0:T(2,128)(2,1)}, u32[]{:S(2)}) copy-start(bf16[1,512]{1,0:T(2,128)(2,1)} %centroid_ref.3) | copy-start | bytes 3076
  22.7 33.7 %collective-permute-start.3 = (bf16[1024,256]{1,0:T(8,128)(2,1)S(1)}, bf16[1024,256]{1,0:T(8,128)(2,1)S(1)}, u32[]{:S(2)}, u32[]{:S(2)}) collective-permute-start(bf16[1024,256]{1,0:T(8,128)(2,1)S(1)} %pad_maximum_fusion.s0), channel_id=1, source_target_pairs={{0,64},{64,128},{128,192},{192,0},{1,65},{65,129},{129,193},{193,1... | collective-permute-start | bytes 1572872 | tf_op jit(solution)/shard_map/ppermute | solution.py:206
  25.1 31.3 %collective-permute-start.2 = (bf16[1024,256]{1,0:T(8,128)(2,1)S(1)}, bf16[1024,256]{1,0:T(8,128)(2,1)S(1)}, u32[]{:S(2)}, u32[]{:S(2)}) collective-permute-start(bf16[1024,256]{1,0:T(8,128)(2,1)S(1)} %pad_maximum_fusion.s0), channel_id=1, source_target_pairs={{0,128},{64,192},{128,0},{192,64},{1,129},{65,193},{129,1},{193,65... | collective-permute-start | bytes 1572872 | tf_op jit(solution)/shard_map/ppermute | solution.py:206
  29.4 27.0 %collective-permute-start.1 = (bf16[1024,256]{1,0:T(8,128)(2,1)S(1)}, bf16[1024,256]{1,0:T(8,128)(2,1)S(1)}, u32[]{:S(2)}, u32[]{:S(2)}) collective-permute-start(bf16[1024,256]{1,0:T(8,128)(2,1)S(1)} %pad_maximum_fusion.s0), channel_id=1, source_target_pairs={{0,192},{64,0},{128,64},{192,128},{1,193},{65,1},{129,65},{193,129... | collective-permute-start | bytes 1572872 | tf_op jit(solution)/shard_map/ppermute | solution.py:206
  54.5 3.8 %collective-permute-start = (bf16[512,512]{1,0:T(8,128)(2,1)S(1)}, bf16[512,512]{1,0:T(8,128)(2,1)S(1)}, u32[]{:S(2)}, u32[]{:S(2)}) collective-permute-start(bf16[512,512]{1,0:T(8,128)(2,1)S(1)} %bitcast.6), channel_id=1, source_target_pairs={{0,32},{32,0},{1,33},{33,1},{2,34},{34,2},{3,35},{35,3},{4,36},{36... | collective-permute-start | bytes 1572872 | tf_op jit(solution)/shard_map/ppermute | solution.py:206
  61.0 4.7 %collective-permute-start.4 = (bf16[512,512]{1,0:T(8,128)(2,1)S(1)}, bf16[512,512]{1,0:T(8,128)(2,1)S(1)}, u32[]{:S(2)}, u32[]{:S(2)}) collective-permute-start(bf16[512,512]{1,0:T(8,128)(2,1)S(1)} %get-tuple-element.38), channel_id=1, source_target_pairs={{0,32},{32,0},{1,33},{33,1},{2,34},{34,2},{3,35},{35,3},{4,36},{36... | collective-permute-start | bytes 1572872 | tf_op jit(solution)/shard_map/ppermute | solution.py:206
  68.2 19.7 %collective-permute-start.5 = (bf16[1056,256]{1,0:T(8,128)(2,1)}, bf16[1056,256]{1,0:T(8,128)(2,1)S(1)}, u32[]{:S(2)}, u32[]{:S(2)}) collective-permute-start(bf16[1056,256]{1,0:T(8,128)(2,1)} %get-tuple-element.40), channel_id=1, source_target_pairs={{0,64},{64,128},{128,192},{192,0},{1,65},{65,129},{129,193},{193,1... | collective-permute-start | bytes 1622024 | tf_op jit(solution)/shard_map/ppermute | solution.py:206
  70.6 18.8 %collective-permute-start.6 = (bf16[1056,256]{1,0:T(8,128)(2,1)}, bf16[1056,256]{1,0:T(8,128)(2,1)S(1)}, u32[]{:S(2)}, u32[]{:S(2)}) collective-permute-start(bf16[1056,256]{1,0:T(8,128)(2,1)} %get-tuple-element.41), channel_id=1, source_target_pairs={{0,128},{64,192},{128,0},{192,64},{1,129},{65,193},{129,1},{193,65... | collective-permute-start | bytes 1622024 | tf_op jit(solution)/shard_map/ppermute | solution.py:206
  74.9 25.1 %collective-permute-start.7 = (bf16[1056,256]{1,0:T(8,128)(2,1)}, bf16[1056,256]{1,0:T(8,128)(2,1)S(1)}, u32[]{:S(2)}, u32[]{:S(2)}) collective-permute-start(bf16[1056,256]{1,0:T(8,128)(2,1)} %get-tuple-element.42), channel_id=1, source_target_pairs={{0,192},{64,0},{128,64},{192,128},{1,193},{65,1},{129,65},{193,129... | collective-permute-start | bytes 1622024 | tf_op jit(solution)/shard_map/ppermute | solution.py:206
  77.8 43.0 %all-to-all-start.1 = ((bf16[64,8,512]{2,1,0:T(8,128)(2,1)}), bf16[64,8,512]{2,1,0:T(8,128)(2,1)S(1)}, u32[]{:S(2)}, u32[]{:S(2)}) async-start(bf16[64,8,512]{2,1,0:T(8,128)(2,1)} %bitcast.4), calls=%async_computation.1 | async-start | bytes 1048576 | tf_op jit(solution)/shard_map/all_to_all | solution.py:253
  100.1 3.1 %collective-permute-start.8 = (f32[1,512]{1,0:T(1,128)S(1)}, f32[1,512]{1,0:T(1,128)S(1)}, u32[]{:S(2)}, u32[]{:S(2)}) collective-permute-start(f32[1,512]{1,0:T(1,128)S(1)} %shard_map.107), channel_id=1, source_target_pairs={{0,32},{32,0},{1,33},{33,1},{2,34},{34,2},{3,35},{35,3},{4,36},{36... | collective-permute-start | bytes 6152 | tf_op jit(solution)/shard_map/ppermute | solution.py:206
  103.1 17.6 %collective-permute-start.9 = (f32[1,512]{1,0:T(1,128)S(1)}, f32[1,512]{1,0:T(1,128)S(1)}, u32[]{:S(2)}, u32[]{:S(2)}) collective-permute-start(f32[1,512]{1,0:T(1,128)S(1)} %add.3.here_ref), channel_id=1, source_target_pairs={{0,256},{256,0},{1,257},{257,1},{2,258},{258,2},{3,259},{259,3},{4... | collective-permute-start | bytes 6152 | tf_op jit(solution)/shard_map/ppermute | solution.py:206
  109.8 10.9 %copy-start = (bf16[128,512]{1,0:T(8,128)(2,1)S(1)}, bf16[128,512]{1,0:T(8,128)(2,1)}, u32[]{:S(2)}) copy-start(bf16[128,512]{1,0:T(8,128)(2,1)} %tok_ref.3) | copy-start | bytes 393220
  109.8 10.9 %copy-start.1 = (bf16[128,512]{1,0:T(8,128)(2,1)S(1)}, bf16[128,512]{1,0:T(8,128)(2,1)}, u32[]{:S(2)}) copy-start(bf16[128,512]{1,0:T(8,128)(2,1)} %grad_ref.3) | copy-start | bytes 393220
